TPU v7x, 512 devices: a whole 4x4x16 slice. The times are simulated.
512 devices in a mesh: dp: 64 (over z_lo, x, core), tp: 8 (over z_hi, y).
Axes of the slice: x: 4, y: 4, z: 16 (z_hi: 2, z_lo: 8; z = z_hi * 8 + z_lo), core: 2. Of those that a mesh axis runs over, the one named last changes fastest.
Arguments:
- attention: bfloat16 [39424, 4096], P('dp', 'tp'), may hold values from -6 to 6
- residual: bfloat16 [39424, 4096], P('dp', 'tp'), may hold values from -6 to 6
- out_weight: bfloat16 [4096, 4096], P('dp', 'tp'), may hold values from -0.09375 to 0.09375
- norm_gain: float32 [4096], P('tp'), may hold values from 0.5 to 1.5
- lengths: int32 [512], P('dp'), may hold values from 8 to 77
- adapter: bfloat16 [4096, 1280], P('tp', 'dp'), may hold values from -0.09375 to 0.09375
- images: float32 [512, 1280], P('dp'), may hold values from -6 to 6
- log_scale: float32 [1], replicated, may hold values from 2 to 3
- logit_bias: float32 [1], replicated, may hold values from -2 to 0
Outputs:
- mean_loss: float32 [1], replicated
- pooled_grad: float32 [512, 4096], P('dp', 'tp')
- image_grad: float32 [512, 1280], P('dp')
All inputs are finite; a program needn't handle non-finite values.
Results may differ from a plain program's by a relative error of at most 0.00075.
The roundings to bfloat16 on the way count: a program that leaves them out, or rounds other values in their place, can miss the bound.
Values may be sent and summed in bfloat16 or wider, within the bound.
No kernel may reach another device: no remote copies, remote signals or barrier semaphores. Data moves between devices by JAX's collectives and lax.ppermute only.
A program may use at most 64 MiB of HBM per device.

v0:
```python
import jax
import jax.numpy as jnp
from jax import lax
from jax.sharding import PartitionSpec as P


def local(
    attention, residual, out_weight, norm_gain, lengths, adapter, images, log_scale, logit_bias
):
    all_heads = lax.all_gather(attention, "tp", axis=1, tiled=True)
    tok_rows = attention.shape[0]
    own_cols = out_weight.shape[1]
    model_width = all_heads.shape[1]
    product = jnp.dot(
        all_heads,
        lax.all_gather(out_weight, "dp", axis=0, tiled=True),
        preferred_element_type=jnp.float32,
    )
    hidden = residual.astype(jnp.float32) + product
    squares = lax.psum(jnp.sum(hidden * hidden, axis=1), "tp")
    normed = hidden * lax.rsqrt(squares / model_width + 1e-05)[:, None] * norm_gain[None, :]
    captions = lengths.shape[0]
    seq_len = tok_rows // captions
    normed = normed.reshape(captions, seq_len, own_cols)
    positions = jnp.arange(seq_len, dtype=jnp.int32)
    live_mask = (positions[None, :] < lengths[:, None]).astype(jnp.float32)
    summed = jnp.sum(normed * live_mask[:, :, None], axis=1)
    pooled = (summed / lengths.astype(jnp.float32)[:, None]).astype(jnp.bfloat16)
    full_adapter = lax.all_gather(adapter, "dp", axis=1, tiled=True)
    raw_text = lax.psum(jnp.dot(pooled, full_adapter, preferred_element_type=jnp.float32), "tp")
    text_norm = jnp.sqrt(jnp.sum(raw_text * raw_text, axis=1, keepdims=True) + 1e-06)
    text_unit = raw_text / text_norm
    image_norm = jnp.sqrt(jnp.sum(images * images, axis=1, keepdims=True) + 1e-06)
    picture = images / image_norm
    every_image = lax.all_gather(picture, "dp", axis=0, tiled=True)
    pair_count = every_image.shape[0]
    logit_scale = jnp.exp(log_scale[0])
    bias_value = logit_bias[0]
    first_row = lax.axis_index("dp") * captions
    row_ids = first_row + jnp.arange(captions, dtype=jnp.int32)
    column_ids = jnp.arange(pair_count, dtype=jnp.int32)
    logits = (
        logit_scale * jnp.dot(text_unit, every_image.T, precision=lax.Precision.HIGHEST)
        + bias_value
    )
    labels = (column_ids[None, :] == row_ids[:, None]).astype(jnp.float32)
    local_total = -jnp.sum(jax.nn.log_sigmoid((2.0 * labels - 1.0) * logits))
    pair_total = lax.psum(local_total, "dp")
    mean_loss = (pair_total / (pair_count * pair_count)).reshape(1)
    pair_slope = jax.nn.sigmoid(logits) - labels
    text_grad = logit_scale * jnp.dot(pair_slope, every_image, precision=lax.Precision.HIGHEST)
    raw_grad = (
        text_grad - text_unit * jnp.sum(text_unit * text_grad, axis=1, keepdims=True)
    ) / text_norm
    pooled_grad = jnp.dot(
        raw_grad, full_adapter.astype(jnp.float32).T, precision=lax.Precision.HIGHEST
    )
    image_terms = logit_scale * jnp.dot(pair_slope.T, text_unit, precision=lax.Precision.HIGHEST)
    picture_grad = lax.psum_scatter(image_terms, "dp", scatter_dimension=0, tiled=True)
    image_grad = (
        picture_grad - picture * jnp.sum(picture * picture_grad, axis=1, keepdims=True)
    ) / image_norm
    return (mean_loss, pooled_grad, image_grad)


def solution(mesh):
    placed = (
        P("dp", "tp"),
        P("dp", "tp"),
        P("dp", "tp"),
        P("tp"),
        P("dp"),
        P("tp", "dp"),
        P("dp", None),
        P(),
        P(),
    )
    return jax.shard_map(
        local,
        mesh=mesh,
        in_specs=placed,
        out_specs=(P(), P("dp", "tp"), P("dp", None)),
        check_vma=False,
    )
```

profile of v0, /device:TPU:1, one launch (start us, length us, event | category | flops | bytes accessed | tf_op | source)
XLA Modules:
  0.0 1026.2 jit_solution(1759489899220627482)
XLA Ops:
  7.2 0.0 all-gather.12.cloned.1.call-start
  7.2 0.7 all-gather.12.cloned.1.call-update
  7.9 0.0 all-gather.8.cloned.1.call-start
  7.9 0.7 all-gather.8.cloned.1.call-update
  8.6 0.0 all-gather.6.cloned.1.call-start
  8.7 0.7 all-gather.6.cloned.1.call-update
  9.4 0.0 all-gather.10.cloned.1.call-start
  9.4 0.9 multiply_reduce_fusion.4
  10.3 1.5 broadcast_divide_fusion
  11.8 0.0 all-gather.10.cloned.1.call-update
  11.8 0.0 reduce-scatter.2.cloned.1.call-start
  11.9 0.7 convert_element_type.22
  13.9 0.7 fusion.10
  14.6 0.0 copy-start.2
  14.6 121.6 %all-gather.12.cloned.1.call-done = bf16[64,20,512]{2,1,0:T(8,128)(2,1)} async-done(((bf16[1,20,512]{2,1,0:T(8,128)(2,1)}), bf16[64,20,512]{2,1,0:T(8,128)(2,1)}) %all-gather.12.cloned.1.call-update) | async-done | bytes 1310736 | tf_op jit(solution)/shard_map/all_gather | solution.py:29
  136.2 2.3 reshape.59
  138.5 0.0 copy-start.1
  138.5 118.2 %all-gather.8.cloned.1.call-done = bf16[4096,512]{1,0:T(8,128)(2,1)} async-done(((bf16[64,512]{1,0:T(8,128)(2,1)}), bf16[4096,512]{1,0:T(8,128)(2,1)}) %all-gather.8.cloned.1.call-update) | async-done | bytes 4194320 | tf_op jit(solution)/shard_map/all_gather | solution.py:16
  256.7 195.5 %all-gather.6.cloned.1.call-done = bf16[616,4096]{1,0:T(8,128)(2,1)} async-done(((bf16[616,512]{1,0:T(8,128)(2,1)}), bf16[616,4096]{1,0:T(8,128)(2,1)}) %all-gather.6.cloned.1.call-update) | async-done | bytes 5046288 | tf_op jit(solution)/shard_map/all_gather | solution.py:10
  452.3 0.0 copy-done.2
  452.3 6.6 multiply_reduce_fusion.1
  458.8 31.1 %psum.21 = f32[616]{0:T(1024)S(1)} all-reduce(f32[616]{0:T(1024)S(1)} %get-tuple-element.3), channel_id=1, replica_groups=mesh['dp'=64,'tp'=8] {'tp'}, use_global_device_ids=true, to_apply=%region_1.0 | all-reduce | flops 616 | bytes 4928 | tf_op jit(solution)/shard_map/psum | solution.py:20
  489.9 0.0 copy-done.1
  489.9 1.2 multiply_multiply_fusion
  491.2 1.5 reshape.56
  492.6 0.2 multiply_reduce_fusion
  492.8 0.4 fusion.8
  493.3 60.0 %psum.22 = f32[8,1280]{1,0:T(8,128)S(1)} all-reduce(f32[8,1280]{1,0:T(8,128)S(1)} %fusion.8), channel_id=1, replica_groups=mesh['dp'=64,'tp'=8] {'tp'}, use_global_device_ids=true, to_apply=%region_3.0 | all-reduce | flops 10240 | bytes 81920 | tf_op jit(solution)/shard_map/psum | solution.py:30
  553.3 0.1 multiply_reduce_fusion.5
  553.4 28.2 %all-gather.10.cloned.1.call-done = f32[512,1280]{1,0:T(8,128)} async-done(((f32[8,1280]{1,0:T(8,128)}), f32[512,1280]{1,0:T(8,128)}) %all-gather.10.cloned.1.call-update) | async-done | bytes 2621456 | tf_op jit(solution)/shard_map/all_gather | solution.py:35
  581.6 4.6 fusion.7
  586.1 3.8 convolution_multiply_fusion
  590.0 0.0 reduce-scatter.2.cloned.1.call-update
  590.0 210.7 %psum.23 = f32[]{:T(128)} all-reduce(f32[]{:T(128)} %get-tuple-element.5), channel_id=1, replica_groups=mesh['dp'=64,'tp'=8] {'dp'}, use_global_device_ids=true, to_apply=%region_7.8 | all-reduce | flops 1 | bytes 8 | tf_op jit(solution)/shard_map/psum | solution.py:48
  801.4 3.1 multiply_reduce_fusion.3
  804.5 0.0 copy-start
  804.5 1.3 fusion.1
  805.8 210.3 %reduce-scatter.2.cloned.1.call-done = f32[8,1280]{1,0:T(8,128)} async-done(((f32[512,1280]{1,0:T(8,128)}), f32[8,1280]{1,0:T(8,128)}) %reduce-scatter.2.cloned.1.call-update) | async-done | bytes 40976 | tf_op jit(solution)/shard_map/reduce_scatter | solution.py:59
  1016.1 0.0 copy-done
  1016.1 1.0 multiply_reduce_fusion.2
  1017.1 1.5 subtract_divide_fusion
  (4 shorter events, 0.0 us)
Async XLA Ops:
  7.2 129.1 %all-gather.12.cloned.1.call-start = ((), (), s32[]{:S(2)}) async-start(), calls=%async_computation.5 | async-start | bytes 1597440 | tf_op jit(solution)/shard_map/all_gather | solution.py:29
  7.9 248.8 %all-gather.8.cloned.1.call-start = ((), (), s32[]{:S(2)}) async-start(), calls=%async_computation.2 | async-start | bytes 4259840 | tf_op jit(solution)/shard_map/all_gather | solution.py:16
  8.6 443.6 %all-gather.6.cloned.1.call-start = ((), (), s32[]{:S(2)}) async-start(), calls=%async_computation.1 | async-start | bytes 5677056 | tf_op jit(solution)/shard_map/all_gather | solution.py:10
  9.4 572.2 %all-gather.10.cloned.1.call-start = ((), (), s32[]{:S(2)}) async-start(), calls=%async_computation.3 | async-start | bytes 2662400 | tf_op jit(solution)/shard_map/all_gather | solution.py:35
  11.8 1004.3 %reduce-scatter.2.cloned.1.call-start = ((), (), s32[]{:S(2)}) async-start(), calls=%async_computation.4 | async-start | bytes 2662400 | tf_op jit(solution)/shard_map/reduce_scatter | solution.py:59
  14.6 437.6 %copy-start.2 = (bf16[616,512]{1,0:T(8,128)(2,1)S(1)}, bf16[616,512]{1,0:T(8,128)(2,1)}, u32[]{:S(2)}) copy-start(bf16[616,512]{1,0:T(8,128)(2,1)} %param.10) | copy-start | bytes 1892356
  138.5 351.4 %copy-start.1 = (f32[512]{0:T(512)S(1)}, f32[512]{0:T(512)}, u32[]{:S(2)}) copy-start(f32[512]{0:T(512)} %param.12) | copy-start | bytes 6148
  804.5 211.6 %copy-start = (f32[8,1280]{1,0:T(8,128)S(1)}, f32[8,1280]{1,0:T(8,128)}, u32[]{:S(2)}) copy-start(f32[8,1280]{1,0:T(8,128)} %param.15) | copy-start | bytes 122884
Sparse Core Ops, SparseCore 0:
  10.1 126.0 all-gather.11
  138.4 118.3 all-gather.7
  259.8 192.4 all-gather.5
  454.8 126.6 all-gather.9
  590.1 425.9 reduce-scatter.1
where the time goes:
time: 1040 us; the launch traced here: 1030 us
  waiting for transfers between devices  676 us (65%)
  blocking collectives  302 us (29%)
  matrix products  19.9 us (2%)
  between operations  17 us (2%)
    psum x1, blocking collectives, local(): pair_total = lax.psum(local_total, 'dp')  211 us
    reduce_scatter x1, waiting for transfers between devices, local(): lax.psum_scatter(image_terms, 'dp', scatter_dimension=0, tiled=True)  210 us
    all_gather x1, waiting for transfers between devices, local(): all_heads = lax.all_gather(attention, 'tp', axis=1, tiled=True)  196 us
    all_gather x1, waiting for transfers between devices, local(): full_adapter = lax.all_gather(adapter, 'dp', axis=1, tiled=True)  122 us
    all_gather x1, waiting for transfers between devices, local(): lax.all_gather(out_weight, 'dp', axis=0, tiled=True)  118 us
    psum x1, blocking collectives, local(): lax.psum(jnp.dot(pooled, full_adapter, preferred_element_type=jnp.float32...  60 us
    psum x1, blocking collectives, local(): squares = lax.psum(jnp.sum(hidden * hidden, axis=1), 'tp')  31.1 us
    all_gather x1, waiting for transfers between devices, local(): every_image = lax.all_gather(picture, 'dp', axis=0, tiled=True)  28.2 us
  transfers between devices with their start and end apart: 5, of which 5 were waited for; matrix products, arithmetic and copies ran while one was open for 2% of the time, Pallas kernels for 0%

commit v1 on v0

v1 whole, which is shorter than its diff:
```python
import jax
import jax.numpy as jnp
from jax import lax
from jax.sharding import Mesh, PartitionSpec as P

F32 = jnp.float32
BF16 = jnp.bfloat16
F16 = jnp.float16
SIZES = {"zl": 8, "x": 4, "c": 2, "zh": 2, "y": 4}
TP = ("zh", "y")


def swap(v, axis):
    return lax.ppermute(v, axis, [(0, 1), (1, 0)])


def shift(v, axis, by):
    n = SIZES[axis]
    return lax.ppermute(v, axis, [(i, (i + by) % n) for i in range(n)])


def around_y(v):
    return [v] + [shift(v, "y", s) for s in (1, 2, 3)]


def add_products(total, blocks, weights, y):
    for back, block in enumerate(blocks):
        w = lax.dynamic_index_in_dim(weights, (y - back) % 4, 0, keepdims=False)
        total = total + jnp.dot(block, w, preferred_element_type=F32)
    return total


def gather(v, axes):
    n = 1
    for a in axes:
        n *= SIZES[a]
    return lax.all_to_all(jnp.broadcast_to(v[None], (n,) + v.shape), axes, 0, 0)


def split(v, n):
    parts = []
    for _ in range(n):
        top = lax.reduce_precision(v, 8, 7)
        parts.append(top.astype(BF16))
        v = v - top
    return parts


def local(
    attention, residual, out_weight, norm_gain, lengths, adapter, images, log_scale, logit_bias
):
    zl, x, c = lax.axis_index("zl"), lax.axis_index("x"), lax.axis_index("c")
    zh, y = lax.axis_index("zh"), lax.axis_index("y")
    tok_rows = attention.shape[0]
    captions = lengths.shape[0]
    seq_len = tok_rows // captions
    half = 304

    image_norm = jnp.sqrt(jnp.sum(images * images, axis=1, keepdims=True) + 1e-06)
    picture = images / image_norm

    far_a = swap(attention[:half], "zh")
    rows = jnp.concatenate([out_weight, adapter.T, jnp.zeros((4, 512), BF16)], axis=0)
    rows = gather(rows, ("zl",))
    near = around_y(attention)
    rows, far_a, near = lax.optimization_barrier((rows, far_a, near))
    far_b = swap(attention[half:], "zh")
    far_a = around_y(far_a)
    rows = gather(rows, ("x",))
    rows, far_a, far_b = lax.optimization_barrier((rows, far_a, far_b))
    other = swap(rows, "c")
    far_b = around_y(far_b)
    pictures = gather(picture, ("zl",))
    first, second = jnp.where(c == 0, rows, other), jnp.where(c == 0, other, rows)
    both = jnp.stack([first, second], axis=2).transpose(1, 0, 2, 3, 4)
    weight = both[:, :, :, :64].reshape(2, 4, 512, 512)
    full_adapter = both[:, :, :, 64:84].reshape(1280, 512)

    near_w = lax.dynamic_index_in_dim(weight, zh, 0, keepdims=False)
    far_w = lax.dynamic_index_in_dim(weight, 1 - zh, 0, keepdims=False)
    hidden = residual.astype(F32)
    hidden = add_products(hidden, near, near_w, y)
    top = add_products(hidden[:half], far_a, far_w, y)
    low = add_products(hidden[half:], far_b, far_w, y)
    hidden = jnp.concatenate([top, low], axis=0)

    squares = jnp.sum(hidden * hidden, axis=1)
    squares, pictures = lax.optimization_barrier((squares, pictures))
    squares = jnp.sum(gather(squares, TP), axis=0)
    every_image = lax.all_gather(pictures, ("x", "c")).reshape(512, 1280)
    normed = hidden * lax.rsqrt(squares / 4096 + 1e-05)[:, None] * norm_gain[None, :]
    normed = normed.reshape(captions, seq_len, 512)
    positions = jnp.arange(seq_len, dtype=jnp.int32)
    live_mask = (positions[None, :] < lengths[:, None]).astype(F32)
    summed = jnp.sum(normed * live_mask[:, :, None], axis=1)
    pooled = (summed / lengths.astype(F32)[:, None]).astype(BF16)
    partial_text = lax.dot_general(
        pooled, full_adapter, (((1,), (1,)), ((), ())), preferred_element_type=F32
    )
    raw_text = jnp.sum(gather(partial_text, TP), axis=0)
    text_norm = jnp.sqrt(jnp.sum(raw_text * raw_text, axis=1, keepdims=True) + 1e-06)
    text_unit = raw_text / text_norm

    texts = gather(gather(text_unit.astype(F16), ("zl",)), ("x",))
    other_texts = swap(texts, "c")
    texts = texts.reshape(256, 1280).astype(F32)
    other_texts = other_texts.reshape(256, 1280).astype(F32)

    logit_scale = jnp.exp(log_scale[0])
    bias_value = logit_bias[0]
    first_row = ((x * 2 + c) * 8 + zl) * captions
    row_ids = first_row + jnp.arange(captions, dtype=jnp.int32)
    column_ids = jnp.arange(512, dtype=jnp.int32)
    labels = (column_ids[None, :] == row_ids[:, None]).astype(F32)
    logits = logit_scale * jnp.dot(text_unit, every_image.T, precision=lax.Precision.HIGHEST) + bias_value
    pair_slope = jax.nn.sigmoid(logits) - labels
    text_grad = logit_scale * jnp.dot(pair_slope, every_image, precision=lax.Precision.HIGHEST)
    raw_grad = (
        text_grad - text_unit * jnp.sum(text_unit * text_grad, axis=1, keepdims=True)
    ) / text_norm
    parts = jnp.concatenate(split(raw_grad, 3), axis=0)
    pooled_grad = jnp.dot(parts, full_adapter, preferred_element_type=F32)
    pooled_grad = jnp.sum(pooled_grad.reshape(3, captions, 512), axis=0)

    t = jnp.arange(256, dtype=jnp.int32)
    pair_of = (t // 64 * 2 + c) * 64 + t % 64
    half_labels = (column_ids[None, :] == pair_of[:, None]).astype(F32)
    half_logits = logit_scale * jnp.dot(texts, every_image.T, precision=lax.Precision.HIGH) + bias_value
    half_total = -jnp.sum(jax.nn.log_sigmoid((2.0 * half_labels - 1.0) * half_logits))
    pair_total = half_total + swap(half_total, "c")
    mean_loss = (pair_total / (512 * 512)).reshape(1)

    own_ids = (x * 8 + zl) * captions + jnp.arange(captions, dtype=jnp.int32)
    own = (t[None, :] == own_ids[:, None]).astype(F32)
    picture_grad = 0.0
    for some, mark in ((texts, own), (other_texts, 0.0)):
        slope = jnp.dot(picture, some.T, precision=lax.Precision.HIGHEST)
        slope = jax.nn.sigmoid(logit_scale * slope + bias_value) - mark
        picture_grad += jnp.dot(slope, some, precision=lax.Precision.HIGHEST)
    picture_grad = logit_scale * picture_grad
    image_grad = (
        picture_grad - picture * jnp.sum(picture * picture_grad, axis=1, keepdims=True)
    ) / image_norm
    return (mean_loss, pooled_grad, image_grad)


def solution(mesh):
    dp, tp = ("zl", "x", "c"), TP
    finer = Mesh(mesh.devices.reshape(8, 4, 2, 2, 4), dp + tp)
    placed = (P(dp, tp), P(dp, tp), P(dp, tp), P(tp), P(dp), P(tp, dp), P(dp, None), P(), P())
    return jax.shard_map(
        local,
        mesh=finer,
        in_specs=placed,
        out_specs=(P(), P(dp, tp), P(dp, None)),
        check_vma=False,
    )
```

time: 1040 us -> 284 us (0.27); the launches traced: 1030 us -> 283 us
  waiting for transfers between devices: 676 us -> 59.9 us
  blocking collectives: 302 us -> 0 us
  starting transfers between devices: 0.19 us -> 158 us
  local copies, waits for them, and re-layouts: 3.76 us -> 17.2 us
    all_gather x4 -> x1, waiting for transfers between devices: 463 us -> 0.02 us  [local(): every_image = lax.all_gather(pictures, ('x', 'c')).reshape(512, 1280)]
    psum x3 -> x0, blocking collectives: 302 us -> none  [the longest x1 211 us: local(): pair_total = lax.psum(local_total, 'dp')]
    reduce_scatter x1 -> x0, waiting for transfers between devices: 210 us -> none  [local(): lax.psum_scatter(image_terms, 'dp', scatter_dimension=0, tiled=True)]
    ppermute x0 -> x14, starting transfers between devices: none -> 97.6 us  [the longest x5 64.4 us: swap(): return lax.ppermute(v, axis, [(0, 1), (1, 0)])]
    all_to_all x0 -> x7, starting transfers between devices: none -> 60.2 us  [gather(): return lax.all_to_all(jnp.broadcast_to(v[None], (n,) + v.shape), axes, 0, 0)]
    all_to_all x0 -> x7, waiting for transfers between devices: none -> 39.1 us  [gather(): return lax.all_to_all(jnp.broadcast_to(v[None], (n,) + v.shape), axes, 0, 0)]
    ppermute x0 -> x14, waiting for transfers between devices: none -> 20.8 us  [the longest x9 11 us: shift(): return lax.ppermute(v, axis, [(i, (i + by) % n) for i in range(n)])]
  transfers between devices with their start and end apart: 5 -> 22, of which waited for: 5 -> 10; matrix products, arithmetic and copies ran while one was open for 2% -> 9% of each run, Pallas kernels for 0% -> 0%
where the time goes in v1:
time: 284 us; the launch traced here: 283 us
  starting transfers between devices  158 us (56%)
  waiting for transfers between devices  59.9 us (21%)
  matrix products  21.7 us (8%)
  between operations  18.5 us (7%)
  local copies, waits for them, and re-layouts  17.2 us (6%)
  other arithmetic  7.43 us (3%)
    ppermute x5, starting transfers between devices, swap(): return lax.ppermute(v, axis, [(0, 1), (1, 0)])  64.4 us
    all_to_all x7, starting transfers between devices, gather(): return lax.all_to_all(jnp.broadcast_to(v[None], (n,) + v.shape), axes, 0, 0)  60.2 us
    all_to_all x7, waiting for transfers between devices, gather(): return lax.all_to_all(jnp.broadcast_to(v[None], (n,) + v.shape), axes, 0, 0)  39.1 us
    ppermute x9, starting transfers between devices, shift(): return lax.ppermute(v, axis, [(i, (i + by) % n) for i in range(n)])  33.2 us
    ppermute x9, waiting for transfers between devices, shift(): return lax.ppermute(v, axis, [(i, (i + by) % n) for i in range(n)])  11 us
    ppermute x5, waiting for transfers between devices, swap(): return lax.ppermute(v, axis, [(0, 1), (1, 0)])  9.82 us
    broadcast_in_dim x7, local copies, waits for them, and re-layouts, gather(): return lax.all_to_all(jnp.broadcast_to(v[None], (n,) + v.shape), axes, 0, 0)  6.42 us
    dot_general x12, matrix products, add_products(): total = total + jnp.dot(block, w, preferred_element_type=F32)  5.7 us
  transfers between devices with their start and end apart: 22, of which 10 were waited for; matrix products, arithmetic and copies ran while one was open for 9% of the time, Pallas kernels for 0%

profile of v1, /device:TPU:1, one launch (start us, length us, event | category | flops | bytes accessed | tf_op | source)
XLA Modules:
  0.0 282.7 jit_solution(1133447862663933889)
XLA Ops:
  7.3 1.0 maximum_maximum_fusion
  8.3 0.9 broadcast_in_dim.17
  9.2 13.1 %all-to-all-start = ((bf16[8,88,512]{2,1,0:T(8,128)(2,1)}), bf16[8,88,512]{2,1,0:T(8,128)(2,1)S(1)}, u32[]{:S(2)}, u32[]{:S(2)}) async-start(bf16[8,88,512]{2,1,0:T(8,128)(2,1)} %broadcast_in_dim.17), calls=%async_computation | async-start | bytes 1441792 | tf_op jit(solution)/shard_map/all_to_all | solution.py:37
  22.2 3.2 %collective-permute-start.1 = (bf16[616,512]{1,0:T(8,128)(2,1)}, bf16[616,512]{1,0:T(8,128)(2,1)S(1)}, u32[]{:S(2)}, u32[]{:S(2)}) collective-permute-start(bf16[616,512]{1,0:T(8,128)(2,1)} %param.9), channel_id=1, source_target_pairs={{0,1},{1,2},{2,3},{3,0},{4,5},{5,6},{6,7},{7,4},{8,9},{9,10},{10,1... | collective-permute-start | bytes 1892360 | tf_op jit(solution)/shard_map/ppermute | solution.py:19
  25.4 4.5 %collective-permute-start.2 = (bf16[616,512]{1,0:T(8,128)(2,1)}, bf16[616,512]{1,0:T(8,128)(2,1)S(1)}, u32[]{:S(2)}, u32[]{:S(2)}) collective-permute-start(bf16[616,512]{1,0:T(8,128)(2,1)} %param.9), channel_id=1, source_target_pairs={{0,2},{1,3},{2,0},{3,1},{4,6},{5,7},{6,4},{7,5},{8,10},{9,11},{10,... | collective-permute-start | bytes 1892360 | tf_op jit(solution)/shard_map/ppermute | solution.py:19
  30.0 3.0 %collective-permute-start.3 = (bf16[616,512]{1,0:T(8,128)(2,1)}, bf16[616,512]{1,0:T(8,128)(2,1)S(1)}, u32[]{:S(2)}, u32[]{:S(2)}) collective-permute-start(bf16[616,512]{1,0:T(8,128)(2,1)} %param.9), channel_id=1, source_target_pairs={{0,3},{1,0},{2,1},{3,2},{4,7},{5,4},{6,5},{7,6},{8,11},{9,8},{10,9... | collective-permute-start | bytes 1892360 | tf_op jit(solution)/shard_map/ppermute | solution.py:19
  33.0 7.9 %collective-permute-start = (bf16[304,512]{1,0:T(8,128)(2,1)S(1)}, bf16[304,512]{1,0:T(8,128)(2,1)S(1)}, u32[]{:S(2)}, u32[]{:S(2)}) collective-permute-start(bf16[304,512]{1,0:T(8,128)(2,1)S(1)} %slice.18), channel_id=1, source_target_pairs={{0,4},{4,0},{1,5},{5,1},{2,6},{6,2},{3,7},{7,3},{8,12},{12,8},{9,1... | collective-permute-start | bytes 933896 | tf_op jit(solution)/shard_map/ppermute | solution.py:14
  41.0 9.8 %collective-permute-done = bf16[304,512]{1,0:T(8,128)(2,1)S(1)} collective-permute-done((bf16[304,512]{1,0:T(8,128)(2,1)S(1)}, bf16[304,512]{1,0:T(8,128)(2,1)S(1)}, u32[]{:S(2)}, u32[]{:S(2)}) %collective-permute-start) | collective-permute-done | bytes 311328 | tf_op jit(solution)/shard_map/ppermute | solution.py:14
  50.8 4.3 %collective-permute-done.2 = bf16[616,512]{1,0:T(8,128)(2,1)S(1)} collective-permute-done((bf16[616,512]{1,0:T(8,128)(2,1)}, bf16[616,512]{1,0:T(8,128)(2,1)S(1)}, u32[]{:S(2)}, u32[]{:S(2)}) %collective-permute-start.2) | collective-permute-done | bytes 630816 | tf_op jit(solution)/shard_map/ppermute | solution.py:19
  55.1 1.8 collective-permute-done.3
  56.9 1.9 broadcast_in_dim.18
  58.7 4.0 %all-to-all-start.1 = ((bf16[4,8,88,512]{3,2,1,0:T(8,128)(2,1)}), bf16[4,8,88,512]{3,2,1,0:T(8,128)(2,1)S(1)}, u32[]{:S(2)}, u32[]{:S(2)}) async-start(bf16[4,8,88,512]{3,2,1,0:T(8,128)(2,1)} %broadcast_in_dim.18), calls=%async_computation.1 | async-start | bytes 5767168 | tf_op jit(solution)/shard_map/all_to_all | solution.py:37
  62.8 16.8 %collective-permute-start.7 = (bf16[312,512]{1,0:T(8,128)(2,1)S(1)}, bf16[312,512]{1,0:T(8,128)(2,1)S(1)}, u32[]{:S(2)}, u32[]{:S(2)}) collective-permute-start(bf16[312,512]{1,0:T(8,128)(2,1)S(1)} %slice.19), channel_id=1, source_target_pairs={{0,4},{4,0},{1,5},{5,1},{2,6},{6,2},{3,7},{7,3},{8,12},{12,8},{9,1... | collective-permute-start | bytes 958472 | tf_op jit(solution)/shard_map/ppermute | solution.py:14
  79.6 3.9 %collective-permute-start.4 = (bf16[304,512]{1,0:T(8,128)(2,1)}, bf16[304,512]{1,0:T(8,128)(2,1)S(1)}, u32[]{:S(2)}, u32[]{:S(2)}) collective-permute-start(bf16[304,512]{1,0:T(8,128)(2,1)} %copy-done.16), channel_id=1, source_target_pairs={{0,1},{1,2},{2,3},{3,0},{4,5},{5,6},{6,7},{7,4},{8,9},{9,10},{10,1... | collective-permute-start | bytes 933896 | tf_op jit(solution)/shard_map/ppermute | solution.py:19
  83.4 5.2 %collective-permute-start.5 = (bf16[304,512]{1,0:T(8,128)(2,1)}, bf16[304,512]{1,0:T(8,128)(2,1)S(1)}, u32[]{:S(2)}, u32[]{:S(2)}) collective-permute-start(bf16[304,512]{1,0:T(8,128)(2,1)} %copy-done.16), channel_id=1, source_target_pairs={{0,2},{1,3},{2,0},{3,1},{4,6},{5,7},{6,4},{7,5},{8,10},{9,11},{10,... | collective-permute-start | bytes 933896 | tf_op jit(solution)/shard_map/ppermute | solution.py:19
  88.6 3.0 %collective-permute-start.6 = (bf16[304,512]{1,0:T(8,128)(2,1)}, bf16[304,512]{1,0:T(8,128)(2,1)}, u32[]{:S(2)}, u32[]{:S(2)}) collective-permute-start(bf16[304,512]{1,0:T(8,128)(2,1)} %copy-done.16), channel_id=1, source_target_pairs={{0,3},{1,0},{2,1},{3,2},{4,7},{5,4},{6,5},{7,6},{8,11},{9,8},{10,9... | collective-permute-start | bytes 933896 | tf_op jit(solution)/shard_map/ppermute | solution.py:19
  91.7 2.8 %collective-permute-done.5 = bf16[304,512]{1,0:T(8,128)(2,1)S(1)} collective-permute-done((bf16[304,512]{1,0:T(8,128)(2,1)}, bf16[304,512]{1,0:T(8,128)(2,1)S(1)}, u32[]{:S(2)}, u32[]{:S(2)}) %collective-permute-start.5) | collective-permute-done | bytes 311328 | tf_op jit(solution)/shard_map/ppermute | solution.py:19
  95.2 1.5 collective-permute-done.6
  96.8 1.9 copy.24
  98.7 31.1 %collective-permute-start.8 = (bf16[4,8,88,512]{3,2,0,1:T(8,128)(2,1)}, bf16[4,8,88,512]{3,2,0,1:T(8,128)(2,1)}, u32[]{:S(2)}, u32[]{:S(2)}) collective-permute-start(bf16[4,8,88,512]{3,2,0,1:T(8,128)(2,1)} %copy.24), channel_id=1, source_target_pairs={{0,8},{8,0},{1,9},{9,1},{2,10},{10,2},{3,11},{11,3},{4,12},{12,4},... | collective-permute-start | bytes 8650760 | tf_op jit(solution)/shard_map/ppermute | solution.py:14
  131.2 8.7 %all-to-all-start.2 = ((f32[8,8,1280]{2,1,0:T(8,128)}), f32[8,8,1280]{2,1,0:T(8,128)}, u32[]{:S(2)}, u32[]{:S(2)}) async-start(f32[8,8,1280]{2,1,0:T(8,128)} %broadcast_in_dim.19), calls=%async_computation.2 | async-start | bytes 655360 | tf_op jit(solution)/shard_map/all_to_all | solution.py:37
  140.1 3.3 %collective-permute-start.9 = (bf16[312,512]{1,0:T(8,128)(2,1)}, bf16[312,512]{1,0:T(8,128)(2,1)S(1)}, u32[]{:S(2)}, u32[]{:S(2)}) collective-permute-start(bf16[312,512]{1,0:T(8,128)(2,1)} %copy-done.14), channel_id=1, source_target_pairs={{0,1},{1,2},{2,3},{3,0},{4,5},{5,6},{6,7},{7,4},{8,9},{9,10},{10,1... | collective-permute-start | bytes 958472 | tf_op jit(solution)/shard_map/ppermute | solution.py:19
  143.3 4.2 %collective-permute-start.10 = (bf16[312,512]{1,0:T(8,128)(2,1)}, bf16[312,512]{1,0:T(8,128)(2,1)S(1)}, u32[]{:S(2)}, u32[]{:S(2)}) collective-permute-start(bf16[312,512]{1,0:T(8,128)(2,1)} %copy-done.14), channel_id=1, source_target_pairs={{0,2},{1,3},{2,0},{3,1},{4,6},{5,7},{6,4},{7,5},{8,10},{9,11},{10,... | collective-permute-start | bytes 958472 | tf_op jit(solution)/shard_map/ppermute | solution.py:19
  147.6 3.0 %collective-permute-start.11 = (bf16[312,512]{1,0:T(8,128)(2,1)}, bf16[312,512]{1,0:T(8,128)(2,1)S(1)}, u32[]{:S(2)}, u32[]{:S(2)}) collective-permute-start(bf16[312,512]{1,0:T(8,128)(2,1)} %copy-done.14), channel_id=1, source_target_pairs={{0,3},{1,0},{2,1},{3,2},{4,7},{5,4},{6,5},{7,6},{8,11},{9,8},{10,9... | collective-permute-start | bytes 958472 | tf_op jit(solution)/shard_map/ppermute | solution.py:19
  150.5 2.2 select_bitcast_fusion.1
  153.8 2.0 copy-done
  161.1 1.3 fusion.62
  163.7 6.9 %all-to-all-start.3 = ((f32[8,1,616]{2,1,0:T(1,128)}), f32[8,1,616]{2,1,0:T(1,128)S(1)}, u32[]{:S(2)}, u32[]{:S(2)}) async-start(f32[8,1,616]{2,1,0:T(1,128)} %broadcast_in_dim.20), calls=%async_computation.3 | async-start | bytes 40960 | tf_op jit(solution)/shard_map/all_to_all | solution.py:37
  170.6 1.6 slice.27
  172.2 1.3 concatenate.13
  173.8 10.6 %all-to-all-done.3 = f32[8,1,616]{2,1,0:T(1,128)S(1)} async-done(((f32[8,1,616]{2,1,0:T(1,128)}), f32[8,1,616]{2,1,0:T(1,128)S(1)}, u32[]{:S(2)}, u32[]{:S(2)}) %all-to-all-start.3) | async-done | bytes 19744 | tf_op jit(solution)/shard_map/all_to_all | solution.py:37
  184.5 1.6 multiply_reduce_fusion
  187.3 3.4 %all-to-all-start.4 = ((f32[8,8,1280]{2,1,0:T(8,128)}), f32[8,8,1280]{2,1,0:T(8,128)S(1)}, u32[]{:S(2)}, u32[]{:S(2)}) async-start(f32[8,8,1280]{2,1,0:T(8,128)} %broadcast_in_dim.21), calls=%async_computation.4 | async-start | bytes 655360 | tf_op jit(solution)/shard_map/all_to_all | solution.py:37
  192.1 13.8 %all-to-all-done.4 = f32[8,8,1280]{2,1,0:T(8,128)S(1)} async-done(((f32[8,8,1280]{2,1,0:T(8,128)}), f32[8,8,1280]{2,1,0:T(8,128)S(1)}, u32[]{:S(2)}, u32[]{:S(2)}) %all-to-all-start.4) | async-done | bytes 327712 | tf_op jit(solution)/shard_map/all_to_all | solution.py:37
  206.1 4.1 %fusion.43 = f32[8,512]{1,0:T(8,128)S(1)} fusion(f32[64,8,1280]{2,1,0:T(8,128)} %all-gather.3.cloned.1.call-done, s32[8]{0:T(128)S(1)} %iota_add_fusion.1, f32[]{:T(128)} %bitcast.114, f32[]{:T(128)} %bitcast, f32[8,1280]{1,0:T(8,128)S(1)} %reduce_sum.94, f32[8]{0:T(128)S(1)} %add_sqrt_fusion), kind=kOutput, calls=%fused_computation.31 | convolution fusion | flops 62957568 | bytes 2678856 | tf_op jit(solution)/shard_map/dot_general | solution.py:115
  210.2 1.4 multiply_reduce_fusion.3
  213.0 19.7 %all-to-all-start.5 = ((f16[8,8,1280]{2,1,0:T(8,128)(2,1)}), f16[8,8,1280]{2,1,0:T(8,128)(2,1)S(1)}, u32[]{:S(2)}, u32[]{:S(2)}) async-start(f16[8,8,1280]{2,1,0:T(8,128)(2,1)} %broadcast_in_dim.22), calls=%async_computation.5 | async-start | bytes 327680 | tf_op jit(solution)/shard_map/all_to_all | solution.py:37
  232.8 1.3 reshape.171
  234.0 9.3 %all-to-all-done.5 = f16[8,8,1280]{2,1,0:T(8,128)(2,1)S(1)} async-done(((f16[8,8,1280]{2,1,0:T(8,128)(2,1)}), f16[8,8,1280]{2,1,0:T(8,128)(2,1)S(1)}, u32[]{:S(2)}, u32[]{:S(2)}) %all-to-all-start.5) | async-done | bytes 163872 | tf_op jit(solution)/shard_map/all_to_all | solution.py:37
  244.3 4.3 %all-to-all-start.6 = ((f16[4,8,8,1280]{3,2,1,0:T(8,128)(2,1)}), f16[4,8,8,1280]{3,2,1,0:T(8,128)(2,1)S(1)}, u32[]{:S(2)}, u32[]{:S(2)}) async-start(f16[4,8,8,1280]{3,2,1,0:T(8,128)(2,1)} %broadcast_in_dim.23), calls=%async_computation.6 | async-start | bytes 1310720 | tf_op jit(solution)/shard_map/all_to_all | solution.py:37
  248.6 2.2 convolution_reduce_fusion
  250.8 5.4 %all-to-all-done.6 = f16[4,8,8,1280]{3,2,1,0:T(8,128)(2,1)S(1)} async-done(((f16[4,8,8,1280]{3,2,1,0:T(8,128)(2,1)}), f16[4,8,8,1280]{3,2,1,0:T(8,128)(2,1)S(1)}, u32[]{:S(2)}, u32[]{:S(2)}) %all-to-all-start.6) | async-done | bytes 655392 | tf_op jit(solution)/shard_map/all_to_all | solution.py:37
  256.2 6.7 %collective-permute-start.13 = (f16[4,8,8,1280]{3,2,1,0:T(8,128)(2,1)S(1)}, f16[4,8,8,1280]{3,2,1,0:T(8,128)(2,1)}, u32[]{:S(2)}, u32[]{:S(2)}) collective-permute-start(f16[4,8,8,1280]{3,2,1,0:T(8,128)(2,1)S(1)} %all-to-all-done.6), channel_id=1, source_target_pairs={{0,8},{8,0},{1,9},{9,1},{2,10},{10,2},{3,11},{11,3},{4,12},{12,4},... | collective-permute-start | bytes 1966088 | tf_op jit(solution)/shard_map/ppermute | solution.py:14
  262.9 2.3 fusion.63
  265.2 1.9 collective-permute-start.12
  267.1 1.0 fusion.56
  270.0 2.1 fusion.50
  272.1 1.8 multiply_reduce_fusion.2
  (111 shorter events, 15.2 us)
Async XLA Ops:
  7.2 25.8 %copy-start.3 = (bf16[616,512]{1,0:T(8,128)(2,1)S(1)}, bf16[616,512]{1,0:T(8,128)(2,1)}, u32[]{:S(2)}) copy-start(bf16[616,512]{1,0:T(8,128)(2,1)} %param.9) | copy-start | bytes 1892356
  9.2 47.7 %all-to-all-start = ((bf16[8,88,512]{2,1,0:T(8,128)(2,1)}), bf16[8,88,512]{2,1,0:T(8,128)(2,1)S(1)}, u32[]{:S(2)}, u32[]{:S(2)}) async-start(bf16[8,88,512]{2,1,0:T(8,128)(2,1)} %broadcast_in_dim.17), calls=%async_computation | async-start | bytes 1441792 | tf_op jit(solution)/shard_map/all_to_all | solution.py:37
  22.2 28.5 %collective-permute-start.1 = (bf16[616,512]{1,0:T(8,128)(2,1)}, bf16[616,512]{1,0:T(8,128)(2,1)S(1)}, u32[]{:S(2)}, u32[]{:S(2)}) collective-permute-start(bf16[616,512]{1,0:T(8,128)(2,1)} %param.9), channel_id=1, source_target_pairs={{0,1},{1,2},{2,3},{3,0},{4,5},{5,6},{6,7},{7,4},{8,9},{9,10},{10,1... | collective-permute-start | bytes 1892360 | tf_op jit(solution)/shard_map/ppermute | solution.py:19
  25.4 29.6 %collective-permute-start.2 = (bf16[616,512]{1,0:T(8,128)(2,1)}, bf16[616,512]{1,0:T(8,128)(2,1)S(1)}, u32[]{:S(2)}, u32[]{:S(2)}) collective-permute-start(bf16[616,512]{1,0:T(8,128)(2,1)} %param.9), channel_id=1, source_target_pairs={{0,2},{1,3},{2,0},{3,1},{4,6},{5,7},{6,4},{7,5},{8,10},{9,11},{10,... | collective-permute-start | bytes 1892360 | tf_op jit(solution)/shard_map/ppermute | solution.py:19
  30.0 26.9 %collective-permute-start.3 = (bf16[616,512]{1,0:T(8,128)(2,1)}, bf16[616,512]{1,0:T(8,128)(2,1)S(1)}, u32[]{:S(2)}, u32[]{:S(2)}) collective-permute-start(bf16[616,512]{1,0:T(8,128)(2,1)} %param.9), channel_id=1, source_target_pairs={{0,3},{1,0},{2,1},{3,2},{4,7},{5,4},{6,5},{7,6},{8,11},{9,8},{10,9... | collective-permute-start | bytes 1892360 | tf_op jit(solution)/shard_map/ppermute | solution.py:19
  33.0 17.8 %collective-permute-start = (bf16[304,512]{1,0:T(8,128)(2,1)S(1)}, bf16[304,512]{1,0:T(8,128)(2,1)S(1)}, u32[]{:S(2)}, u32[]{:S(2)}) collective-permute-start(bf16[304,512]{1,0:T(8,128)(2,1)S(1)} %slice.18), channel_id=1, source_target_pairs={{0,4},{4,0},{1,5},{5,1},{2,6},{6,2},{3,7},{7,3},{8,12},{12,8},{9,1... | collective-permute-start | bytes 933896 | tf_op jit(solution)/shard_map/ppermute | solution.py:14
  50.8 4.3 %copy-start.16 = (bf16[304,512]{1,0:T(8,128)(2,1)}, bf16[304,512]{1,0:T(8,128)(2,1)S(1)}, u32[]{:S(2)}) copy-start(bf16[304,512]{1,0:T(8,128)(2,1)S(1)} %collective-permute-done) | copy-start | bytes 933892
  50.8 7.9 %copy-start.4 = (bf16[616,512]{1,0:T(8,128)(2,1)}, bf16[616,512]{1,0:T(8,128)(2,1)S(1)}, u32[]{:S(2)}) copy-start(bf16[616,512]{1,0:T(8,128)(2,1)S(1)} %collective-permute-done.1) | copy-start | bytes 1892356
  55.1 3.6 %copy-start.6 = (bf16[616,512]{1,0:T(8,128)(2,1)}, bf16[616,512]{1,0:T(8,128)(2,1)S(1)}, u32[]{:S(2)}) copy-start(bf16[616,512]{1,0:T(8,128)(2,1)S(1)} %collective-permute-done.2) | copy-start | bytes 1892356
  56.8 1.9 copy-start.8
  58.7 38.1 %all-to-all-start.1 = ((bf16[4,8,88,512]{3,2,1,0:T(8,128)(2,1)}), bf16[4,8,88,512]{3,2,1,0:T(8,128)(2,1)S(1)}, u32[]{:S(2)}, u32[]{:S(2)}) async-start(bf16[4,8,88,512]{3,2,1,0:T(8,128)(2,1)} %broadcast_in_dim.18), calls=%async_computation.1 | async-start | bytes 5767168 | tf_op jit(solution)/shard_map/all_to_all | solution.py:37
  62.8 67.0 %copy-start.11 = (f32[8,1280]{1,0:T(8,128)S(1)}, f32[8,1280]{1,0:T(8,128)}, u32[]{:S(2)}) copy-start(f32[8,1280]{1,0:T(8,128)} %param.15) | copy-start | bytes 122884
  62.8 28.8 %collective-permute-start.7 = (bf16[312,512]{1,0:T(8,128)(2,1)S(1)}, bf16[312,512]{1,0:T(8,128)(2,1)S(1)}, u32[]{:S(2)}, u32[]{:S(2)}) collective-permute-start(bf16[312,512]{1,0:T(8,128)(2,1)S(1)} %slice.19), channel_id=1, source_target_pairs={{0,4},{4,0},{1,5},{5,1},{2,6},{6,2},{3,7},{7,3},{8,12},{12,8},{9,1... | collective-permute-start | bytes 958472 | tf_op jit(solution)/shard_map/ppermute | solution.py:14
  79.6 12.1 %collective-permute-start.4 = (bf16[304,512]{1,0:T(8,128)(2,1)}, bf16[304,512]{1,0:T(8,128)(2,1)S(1)}, u32[]{:S(2)}, u32[]{:S(2)}) collective-permute-start(bf16[304,512]{1,0:T(8,128)(2,1)} %copy-done.16), channel_id=1, source_target_pairs={{0,1},{1,2},{2,3},{3,0},{4,5},{5,6},{6,7},{7,4},{8,9},{9,10},{10,1... | collective-permute-start | bytes 933896 | tf_op jit(solution)/shard_map/ppermute | solution.py:19
  83.4 11.1 %collective-permute-start.5 = (bf16[304,512]{1,0:T(8,128)(2,1)}, bf16[304,512]{1,0:T(8,128)(2,1)S(1)}, u32[]{:S(2)}, u32[]{:S(2)}) collective-permute-start(bf16[304,512]{1,0:T(8,128)(2,1)} %copy-done.16), channel_id=1, source_target_pairs={{0,2},{1,3},{2,0},{3,1},{4,6},{5,7},{6,4},{7,5},{8,10},{9,11},{10,... | collective-permute-start | bytes 933896 | tf_op jit(solution)/shard_map/ppermute | solution.py:19
  88.6 8.1 %collective-permute-start.6 = (bf16[304,512]{1,0:T(8,128)(2,1)}, bf16[304,512]{1,0:T(8,128)(2,1)}, u32[]{:S(2)}, u32[]{:S(2)}) collective-permute-start(bf16[304,512]{1,0:T(8,128)(2,1)} %copy-done.16), channel_id=1, source_target_pairs={{0,3},{1,0},{2,1},{3,2},{4,7},{5,4},{6,5},{7,6},{8,11},{9,8},{10,9... | collective-permute-start | bytes 933896 | tf_op jit(solution)/shard_map/ppermute | solution.py:19
  91.6 2.9 %copy-start.14 = (bf16[312,512]{1,0:T(8,128)(2,1)}, bf16[312,512]{1,0:T(8,128)(2,1)S(1)}, u32[]{:S(2)}) copy-start(bf16[312,512]{1,0:T(8,128)(2,1)S(1)} %collective-permute-done.7) | copy-start | bytes 958468
  91.6 2.9 %copy-start.18 = (bf16[304,512]{1,0:T(8,128)(2,1)}, bf16[304,512]{1,0:T(8,128)(2,1)S(1)}, u32[]{:S(2)}) copy-start(bf16[304,512]{1,0:T(8,128)(2,1)S(1)} %collective-permute-done.4) | copy-start | bytes 933892
  94.5 0.7 copy-start.20
  96.8 33.2 %copy-start.12 = (f32[8,1280]{1,0:T(8,128)S(1)}, f32[8,1280]{1,0:T(8,128)}, u32[]{:S(2)}) copy-start(f32[8,1280]{1,0:T(8,128)} %param.15) | copy-start | bytes 122884
  98.7 51.9 %collective-permute-start.8 = (bf16[4,8,88,512]{3,2,0,1:T(8,128)(2,1)}, bf16[4,8,88,512]{3,2,0,1:T(8,128)(2,1)}, u32[]{:S(2)}, u32[]{:S(2)}) collective-permute-start(bf16[4,8,88,512]{3,2,0,1:T(8,128)(2,1)} %copy.24), channel_id=1, source_target_pairs={{0,8},{8,0},{1,9},{9,1},{2,10},{10,2},{3,11},{11,3},{4,12},{12,4},... | collective-permute-start | bytes 8650760 | tf_op jit(solution)/shard_map/ppermute | solution.py:14
  131.2 31.8 %all-to-all-start.2 = ((f32[8,8,1280]{2,1,0:T(8,128)}), f32[8,8,1280]{2,1,0:T(8,128)}, u32[]{:S(2)}, u32[]{:S(2)}) async-start(f32[8,8,1280]{2,1,0:T(8,128)} %broadcast_in_dim.19), calls=%async_computation.2 | async-start | bytes 655360 | tf_op jit(solution)/shard_map/all_to_all | solution.py:37
  139.9 66.1 %all-gather.3.cloned.1.call-start = ((), (), s32[]{:S(2)}) async-start(), calls=%async_computation.7 | async-start | bytes 2949120 | tf_op jit(solution)/shard_map/all_gather | solution.py:90
  140.1 18.5 %collective-permute-start.9 = (bf16[312,512]{1,0:T(8,128)(2,1)}, bf16[312,512]{1,0:T(8,128)(2,1)S(1)}, u32[]{:S(2)}, u32[]{:S(2)}) collective-permute-start(bf16[312,512]{1,0:T(8,128)(2,1)} %copy-done.14), channel_id=1, source_target_pairs={{0,1},{1,2},{2,3},{3,0},{4,5},{5,6},{6,7},{7,4},{8,9},{9,10},{10,1... | collective-permute-start | bytes 958472 | tf_op jit(solution)/shard_map/ppermute | solution.py:19
  143.3 16.7 %collective-permute-start.10 = (bf16[312,512]{1,0:T(8,128)(2,1)}, bf16[312,512]{1,0:T(8,128)(2,1)S(1)}, u32[]{:S(2)}, u32[]{:S(2)}) collective-permute-start(bf16[312,512]{1,0:T(8,128)(2,1)} %copy-done.14), channel_id=1, source_target_pairs={{0,2},{1,3},{2,0},{3,1},{4,6},{5,7},{6,4},{7,5},{8,10},{9,11},{10,... | collective-permute-start | bytes 958472 | tf_op jit(solution)/shard_map/ppermute | solution.py:19
  147.6 14.9 %collective-permute-start.11 = (bf16[312,512]{1,0:T(8,128)(2,1)}, bf16[312,512]{1,0:T(8,128)(2,1)S(1)}, u32[]{:S(2)}, u32[]{:S(2)}) collective-permute-start(bf16[312,512]{1,0:T(8,128)(2,1)} %copy-done.14), channel_id=1, source_target_pairs={{0,3},{1,0},{2,1},{3,2},{4,7},{5,4},{6,5},{7,6},{8,11},{9,8},{10,9... | collective-permute-start | bytes 958472 | tf_op jit(solution)/shard_map/ppermute | solution.py:19
  153.3 2.5 copy-start
  153.3 2.5 copy-start.9
  155.8 1.1 copy-start.7
  155.8 1.6 copy-start.15
  155.8 1.9 copy-start.21
  156.9 1.2 copy-start.5
  157.7 1.2 copy-start.10
  158.9 1.4 copy-start.19
  159.5 1.2 copy-start.17
  162.4 8.2 %copy-start.26 = (s32[8]{0:T(128)S(1)}, s32[8]{0:T(128)}, u32[]{:S(2)}) copy-start(s32[8]{0:T(128)} %param.13) | copy-start | bytes 100
  163.7 20.7 %all-to-all-start.3 = ((f32[8,1,616]{2,1,0:T(1,128)}), f32[8,1,616]{2,1,0:T(1,128)S(1)}, u32[]{:S(2)}, u32[]{:S(2)}) async-start(f32[8,1,616]{2,1,0:T(1,128)} %broadcast_in_dim.20), calls=%async_computation.3 | async-start | bytes 40960 | tf_op jit(solution)/shard_map/all_to_all | solution.py:37
  172.2 12.2 %copy-start.23 = (f32[512]{0:T(512)S(1)}, f32[512]{0:T(512)}, u32[]{:S(2)}) copy-start(f32[512]{0:T(512)} %param.12) | copy-start | bytes 6148
  187.3 18.6 %all-to-all-start.4 = ((f32[8,8,1280]{2,1,0:T(8,128)}), f32[8,8,1280]{2,1,0:T(8,128)S(1)}, u32[]{:S(2)}, u32[]{:S(2)}) async-start(f32[8,8,1280]{2,1,0:T(8,128)} %broadcast_in_dim.21), calls=%async_computation.4 | async-start | bytes 655360 | tf_op jit(solution)/shard_map/all_to_all | solution.py:37
  206.1 4.1 %copy-start.1 = (f32[64,8,1280]{2,1,0:T(8,128)S(1)}, f32[64,8,1280]{2,1,0:T(8,128)}, u32[]{:S(2)}) copy-start(f32[64,8,1280]{2,1,0:T(8,128)} %all-gather.3.cloned.1.call-done) | copy-start | bytes 7864324
  213.0 30.4 %all-to-all-start.5 = ((f16[8,8,1280]{2,1,0:T(8,128)(2,1)}), f16[8,8,1280]{2,1,0:T(8,128)(2,1)S(1)}, u32[]{:S(2)}, u32[]{:S(2)}) async-start(f16[8,8,1280]{2,1,0:T(8,128)(2,1)} %broadcast_in_dim.22), calls=%async_computation.5 | async-start | bytes 327680 | tf_op jit(solution)/shard_map/all_to_all | solution.py:37
  232.7 15.8 %copy-start.22 = (bf16[8,1280]{1,0:T(8,128)(2,1)S(1)}, bf16[8,1280]{1,0:T(8,128)(2,1)}, u32[]{:S(2)}) copy-start(bf16[8,1280]{1,0:T(8,128)(2,1)} %get-tuple-element.31) | copy-start | bytes 61444
  234.0 28.9 %copy-start.2 = (f32[64,8,1280]{2,1,0:T(8,128)S(1)}, f32[64,8,1280]{2,1,0:T(8,128)}, u32[]{:S(2)}) copy-start(f32[64,8,1280]{2,1,0:T(8,128)} %all-gather.3.cloned.1.call-done) | copy-start | bytes 7864324
  244.3 11.9 %all-to-all-start.6 = ((f16[4,8,8,1280]{3,2,1,0:T(8,128)(2,1)}), f16[4,8,8,1280]{3,2,1,0:T(8,128)(2,1)S(1)}, u32[]{:S(2)}, u32[]{:S(2)}) async-start(f16[4,8,8,1280]{3,2,1,0:T(8,128)(2,1)} %broadcast_in_dim.23), calls=%async_computation.6 | async-start | bytes 1310720 | tf_op jit(solution)/shard_map/all_to_all | solution.py:37
  256.2 13.8 %collective-permute-start.13 = (f16[4,8,8,1280]{3,2,1,0:T(8,128)(2,1)S(1)}, f16[4,8,8,1280]{3,2,1,0:T(8,128)(2,1)}, u32[]{:S(2)}, u32[]{:S(2)}) collective-permute-start(f16[4,8,8,1280]{3,2,1,0:T(8,128)(2,1)S(1)} %all-to-all-done.6), channel_id=1, source_target_pairs={{0,8},{8,0},{1,9},{9,1},{2,10},{10,2},{3,11},{11,3},{4,12},{12,4},... | collective-permute-start | bytes 1966088 | tf_op jit(solution)/shard_map/ppermute | solution.py:14
  262.9 11.1 %copy-start.13 = (f32[8,1280]{1,0:T(8,128)S(1)}, f32[8,1280]{1,0:T(8,128)}, u32[]{:S(2)}) copy-start(f32[8,1280]{1,0:T(8,128)} %param.15) | copy-start | bytes 122884
  262.9 11.1 %copy-start.25 = (f32[8]{0:T(128)S(1)}, f32[8]{0:T(128)}, u32[]{:S(2)}) copy-start(f32[8]{0:T(128)} %copy-done.24) | copy-start | bytes 100
  265.2 3.6 %collective-permute-start.12 = (f32[]{:T(128)}, f32[]{:T(128)}, u32[]{:S(2)}, u32[]{:S(2)}) collective-permute-start(f32[]{:T(128)} %fusion.63), channel_id=1, source_target_pairs={{0,8},{8,0},{1,9},{9,1},{2,10},{10,2},{3,11},{11,3},{4,12},{12,4},... | collective-permute-start | bytes 20 | tf_op jit(solution)/shard_map/ppermute | solution.py:14
  (1 other events, 0.5 us)
Sparse Core Ops, SparseCore 0:
  163.2 32.6 all-gather.2

commit v2 on v1

--- a/solution.py
+++ b/solution.py
@@ -23,11 +23,11 @@
     return [v] + [shift(v, "y", s) for s in (1, 2, 3)]
 
 
-def add_products(total, blocks, weights, y):
+def in_order(blocks, y):
+    whole = jnp.zeros((blocks[0].shape[0], 2048), BF16)
     for back, block in enumerate(blocks):
-        w = lax.dynamic_index_in_dim(weights, (y - back) % 4, 0, keepdims=False)
-        total = total + jnp.dot(block, w, preferred_element_type=F32)
-    return total
+        whole = lax.dynamic_update_slice(whole, block, (0, (y - back) % 4 * 512))
+    return whole
 
 
 def gather(v, axes):
@@ -35,6 +35,11 @@
     for a in axes:
         n *= SIZES[a]
     return lax.all_to_all(jnp.broadcast_to(v[None], (n,) + v.shape), axes, 0, 0)
+
+
+def unscaled(message):
+    message = message.reshape(256, 1408).astype(F32)
+    return message[:, :1280] * jnp.exp2(message[:, 1280:1281])
 
 
 def split(v, n):
@@ -64,24 +69,25 @@
     rows = gather(rows, ("zl",))
     near = around_y(attention)
     rows, far_a, near = lax.optimization_barrier((rows, far_a, near))
+    near = in_order(near, y)
     far_b = swap(attention[half:], "zh")
     far_a = around_y(far_a)
     rows = gather(rows, ("x",))
-    rows, far_a, far_b = lax.optimization_barrier((rows, far_a, far_b))
+    rows, far_a, far_b, near = lax.optimization_barrier((rows, in_order(far_a, y), far_b, near))
     other = swap(rows, "c")
     far_b = around_y(far_b)
+    other, picture = lax.optimization_barrier((other, picture))
     pictures = gather(picture, ("zl",))
     first, second = jnp.where(c == 0, rows, other), jnp.where(c == 0, other, rows)
     both = jnp.stack([first, second], axis=2).transpose(1, 0, 2, 3, 4)
-    weight = both[:, :, :, :64].reshape(2, 4, 512, 512)
+    weight = both[:, :, :, :64].reshape(2, 2048, 512)
     full_adapter = both[:, :, :, 64:84].reshape(1280, 512)
 
     near_w = lax.dynamic_index_in_dim(weight, zh, 0, keepdims=False)
     far_w = lax.dynamic_index_in_dim(weight, 1 - zh, 0, keepdims=False)
-    hidden = residual.astype(F32)
-    hidden = add_products(hidden, near, near_w, y)
-    top = add_products(hidden[:half], far_a, far_w, y)
-    low = add_products(hidden[half:], far_b, far_w, y)
+    hidden = residual.astype(F32) + jnp.dot(near, near_w, preferred_element_type=F32)
+    top = hidden[:half] + jnp.dot(far_a, far_w, preferred_element_type=F32)
+    low = hidden[half:] + jnp.dot(in_order(far_b, y), far_w, preferred_element_type=F32)
     hidden = jnp.concatenate([top, low], axis=0)
 
     squares = jnp.sum(hidden * hidden, axis=1)
@@ -97,14 +103,17 @@
     partial_text = lax.dot_general(
         pooled, full_adapter, (((1,), (1,)), ((), ())), preferred_element_type=F32
     )
-    raw_text = jnp.sum(gather(partial_text, TP), axis=0)
+    raw_text = jnp.sum(gather(partial_text, ("y",)), axis=0)
+    raw_text = raw_text + swap(raw_text, "zh")
     text_norm = jnp.sqrt(jnp.sum(raw_text * raw_text, axis=1, keepdims=True) + 1e-06)
     text_unit = raw_text / text_norm
 
-    texts = gather(gather(text_unit.astype(F16), ("zl",)), ("x",))
-    other_texts = swap(texts, "c")
-    texts = texts.reshape(256, 1280).astype(F32)
-    other_texts = other_texts.reshape(256, 1280).astype(F32)
+    largest = jnp.max(jnp.abs(text_unit), axis=1, keepdims=True)
+    power = jnp.floor(jnp.log2(jnp.clip(largest, 1e-36, 1.0)))
+    message = jnp.concatenate([text_unit * jnp.exp2(-power), jnp.broadcast_to(power, (captions, 128))], axis=1)
+    texts = gather(message.astype(F16), ("zl",))
+    texts, text_unit = lax.optimization_barrier((texts, text_unit))
+    texts = gather(texts, ("x",))
 
     logit_scale = jnp.exp(log_scale[0])
     bias_value = logit_bias[0]
@@ -122,11 +131,17 @@
     pooled_grad = jnp.dot(parts, full_adapter, preferred_element_type=F32)
     pooled_grad = jnp.sum(pooled_grad.reshape(3, captions, 512), axis=0)
 
+    texts, pooled_grad = lax.optimization_barrier((texts, pooled_grad))
+    other_texts = swap(texts, "c")
+    texts = unscaled(texts)
+
     t = jnp.arange(256, dtype=jnp.int32)
     pair_of = (t // 64 * 2 + c) * 64 + t % 64
     half_labels = (column_ids[None, :] == pair_of[:, None]).astype(F32)
     half_logits = logit_scale * jnp.dot(texts, every_image.T, precision=lax.Precision.HIGH) + bias_value
     half_total = -jnp.sum(jax.nn.log_sigmoid((2.0 * half_labels - 1.0) * half_logits))
+    other_texts, half_total = lax.optimization_barrier((other_texts, half_total))
+    other_texts = unscaled(other_texts)
     pair_total = half_total + swap(half_total, "c")
     mean_loss = (pair_total / (512 * 512)).reshape(1)
 

time: 284 us -> 294 us (1.035)
  starting transfers between devices: 158 us -> 147 us
  local copies, waits for them, and re-layouts: 17.2 us -> 25.5 us
  waiting for transfers between devices: 59.9 us -> 67.5 us
  blocking collectives: 0 us -> 7.36 us
  matrix products: 21.7 us -> 18.4 us
    all_to_all x7 -> x6, starting transfers between devices: 60.2 us -> 45.5 us  [gather(): return lax.all_to_all(jnp.broadcast_to(v[None], (n,) + v.shape), axes, 0, 0)]
    ppermute x5 -> x6, waiting for transfers between devices: 9.82 us -> 20.7 us  [swap(): return lax.ppermute(v, axis, [(0, 1), (1, 0)])]
    all_to_all x7 -> x6, waiting for transfers between devices: 39.1 us -> 30.1 us  [gather(): return lax.all_to_all(jnp.broadcast_to(v[None], (n,) + v.shape), axes, 0, 0)]
    all_to_all x0 -> x1, blocking collectives: none -> 7.36 us  [gather(): return lax.all_to_all(jnp.broadcast_to(v[None], (n,) + v.shape), axes, 0, 0)]
    ppermute x9, waiting for transfers between devices: 11 us -> 16.7 us  [shift(): return lax.ppermute(v, axis, [(i, (i + by) % n) for i in range(n)])]
    ppermute x5 -> x6, starting transfers between devices: 64.4 us -> 68.2 us  [swap(): return lax.ppermute(v, axis, [(0, 1), (1, 0)])]
    unnamed x54 -> x46, local copies, waits for them, and re-layouts: 3.83 us -> 6.94 us
  transfers between devices with their start and end apart: 22 -> 22, of which waited for: 10 -> 13; matrix products, arithmetic and copies ran while one was open for 9% -> 11% of each run, Pallas kernels for 0% -> 0%
where the time goes in v2:
time: 294 us; the launch traced here: 292 us
  starting transfers between devices  147 us (50%)
  waiting for transfers between devices  67.5 us (23%)
  local copies, waits for them, and re-layouts  25.5 us (9%)
  between operations  18.5 us (6%)
  matrix products  18.4 us (6%)
  other arithmetic  7.67 us (3%)
  blocking collectives  7.36 us (3%)
    ppermute x6, starting transfers between devices, swap(): return lax.ppermute(v, axis, [(0, 1), (1, 0)])  68.2 us
    all_to_all x6, starting transfers between devices, gather(): return lax.all_to_all(jnp.broadcast_to(v[None], (n,) + v.shape), axes, 0, 0)  45.5 us
    ppermute x9, starting transfers between devices, shift(): return lax.ppermute(v, axis, [(i, (i + by) % n) for i in range(n)])  33.6 us
    all_to_all x6, waiting for transfers between devices, gather(): return lax.all_to_all(jnp.broadcast_to(v[None], (n,) + v.shape), axes, 0, 0)  30.1 us
    ppermute x6, waiting for transfers between devices, swap(): return lax.ppermute(v, axis, [(0, 1), (1, 0)])  20.7 us
    ppermute x9, waiting for transfers between devices, shift(): return lax.ppermute(v, axis, [(i, (i + by) % n) for i in range(n)])  16.7 us
    all_to_all x1, blocking collectives, gather(): return lax.all_to_all(jnp.broadcast_to(v[None], (n,) + v.shape), axes, 0, 0)  7.36 us
    unnamed x46, local copies, waits for them, and re-layouts  6.94 us
  transfers between devices with their start and end apart: 22, of which 13 were waited for; matrix products, arithmetic and copies ran while one was open for 11% of the time, Pallas kernels for 0%

profile of v2, /device:TPU:1, one launch (start us, length us, event | category | flops | bytes accessed | tf_op | source)
XLA Modules:
  0.0 292.2 jit_solution(6364220564905461262)
XLA Ops:
  9.2 13.1 %all-to-all-start = ((bf16[8,88,512]{2,1,0:T(8,128)(2,1)}), bf16[8,88,512]{2,1,0:T(8,128)(2,1)S(1)}, u32[]{:S(2)}, u32[]{:S(2)}) async-start(bf16[8,88,512]{2,1,0:T(8,128)(2,1)} %broadcast_in_dim.23), calls=%async_computation | async-start | bytes 1441792 | tf_op jit(solution)/shard_map/all_to_all | solution.py:37
  22.3 3.2 %collective-permute-start.1 = (bf16[616,512]{1,0:T(8,128)(2,1)S(1)}, bf16[616,512]{1,0:T(8,128)(2,1)S(1)}, u32[]{:S(2)}, u32[]{:S(2)}) collective-permute-start(bf16[616,512]{1,0:T(8,128)(2,1)S(1)} %copy-done.4), channel_id=1, source_target_pairs={{0,1},{1,2},{2,3},{3,0},{4,5},{5,6},{6,7},{7,4},{8,9},{9,10},{10,1... | collective-permute-start | bytes 1892360 | tf_op jit(solution)/shard_map/ppermute | solution.py:19
  25.5 4.5 %collective-permute-start.2 = (bf16[616,512]{1,0:T(8,128)(2,1)S(1)}, bf16[616,512]{1,0:T(8,128)(2,1)S(1)}, u32[]{:S(2)}, u32[]{:S(2)}) collective-permute-start(bf16[616,512]{1,0:T(8,128)(2,1)S(1)} %copy-done.4), channel_id=1, source_target_pairs={{0,2},{1,3},{2,0},{3,1},{4,6},{5,7},{6,4},{7,5},{8,10},{9,11},{10,... | collective-permute-start | bytes 1892360 | tf_op jit(solution)/shard_map/ppermute | solution.py:19
  30.0 3.0 %collective-permute-start.3 = (bf16[616,512]{1,0:T(8,128)(2,1)S(1)}, bf16[616,512]{1,0:T(8,128)(2,1)S(1)}, u32[]{:S(2)}, u32[]{:S(2)}) collective-permute-start(bf16[616,512]{1,0:T(8,128)(2,1)S(1)} %copy-done.4), channel_id=1, source_target_pairs={{0,3},{1,0},{2,1},{3,2},{4,7},{5,4},{6,5},{7,6},{8,11},{9,8},{10,9... | collective-permute-start | bytes 1892360 | tf_op jit(solution)/shard_map/ppermute | solution.py:19
  33.0 7.9 %collective-permute-start = (bf16[304,512]{1,0:T(8,128)(2,1)S(1)}, bf16[304,512]{1,0:T(8,128)(2,1)S(1)}, u32[]{:S(2)}, u32[]{:S(2)}) collective-permute-start(bf16[304,512]{1,0:T(8,128)(2,1)S(1)} %slice.30), channel_id=1, source_target_pairs={{0,4},{4,0},{1,5},{5,1},{2,6},{6,2},{3,7},{7,3},{8,12},{12,8},{9,1... | collective-permute-start | bytes 933896 | tf_op jit(solution)/shard_map/ppermute | solution.py:14
  41.0 9.8 %collective-permute-done = bf16[304,512]{1,0:T(8,128)(2,1)S(1)} collective-permute-done((bf16[304,512]{1,0:T(8,128)(2,1)S(1)}, bf16[304,512]{1,0:T(8,128)(2,1)S(1)}, u32[]{:S(2)}, u32[]{:S(2)}) %collective-permute-start) | collective-permute-done | bytes 311328 | tf_op jit(solution)/shard_map/ppermute | solution.py:14
  50.8 4.1 %collective-permute-done.2 = bf16[616,512]{1,0:T(8,128)(2,1)S(1)} collective-permute-done((bf16[616,512]{1,0:T(8,128)(2,1)S(1)}, bf16[616,512]{1,0:T(8,128)(2,1)S(1)}, u32[]{:S(2)}, u32[]{:S(2)}) %collective-permute-start.2) | collective-permute-done | bytes 630816 | tf_op jit(solution)/shard_map/ppermute | solution.py:19
  54.9 1.7 collective-permute-done.3
  56.6 1.8 broadcast_in_dim.24
  58.4 4.0 %all-to-all-start.1 = ((bf16[4,8,88,512]{3,2,1,0:T(8,128)(2,1)}), bf16[4,8,88,512]{3,2,1,0:T(8,128)(2,1)S(1)}, u32[]{:S(2)}, u32[]{:S(2)}) async-start(bf16[4,8,88,512]{3,2,1,0:T(8,128)(2,1)} %broadcast_in_dim.24), calls=%async_computation.1 | async-start | bytes 5767168 | tf_op jit(solution)/shard_map/all_to_all | solution.py:37
  63.2 17.1 %collective-permute-start.7 = (bf16[312,512]{1,0:T(8,128)(2,1)}, bf16[312,512]{1,0:T(8,128)(2,1)}, u32[]{:S(2)}, u32[]{:S(2)}) collective-permute-start(bf16[312,512]{1,0:T(8,128)(2,1)} %slice.31), channel_id=1, source_target_pairs={{0,4},{4,0},{1,5},{5,1},{2,6},{6,2},{3,7},{7,3},{8,12},{12,8},{9,1... | collective-permute-start | bytes 958472 | tf_op jit(solution)/shard_map/ppermute | solution.py:14
  80.3 4.0 %collective-permute-start.4 = (bf16[304,512]{1,0:T(8,128)(2,1)}, bf16[304,512]{1,0:T(8,128)(2,1)S(1)}, u32[]{:S(2)}, u32[]{:S(2)}) collective-permute-start(bf16[304,512]{1,0:T(8,128)(2,1)} %copy-done.18), channel_id=1, source_target_pairs={{0,1},{1,2},{2,3},{3,0},{4,5},{5,6},{6,7},{7,4},{8,9},{9,10},{10,1... | collective-permute-start | bytes 933896 | tf_op jit(solution)/shard_map/ppermute | solution.py:19
  84.4 5.1 %collective-permute-start.5 = (bf16[304,512]{1,0:T(8,128)(2,1)}, bf16[304,512]{1,0:T(8,128)(2,1)S(1)}, u32[]{:S(2)}, u32[]{:S(2)}) collective-permute-start(bf16[304,512]{1,0:T(8,128)(2,1)} %copy-done.18), channel_id=1, source_target_pairs={{0,2},{1,3},{2,0},{3,1},{4,6},{5,7},{6,4},{7,5},{8,10},{9,11},{10,... | collective-permute-start | bytes 933896 | tf_op jit(solution)/shard_map/ppermute | solution.py:19
  89.5 3.0 %collective-permute-start.6 = (bf16[304,512]{1,0:T(8,128)(2,1)}, bf16[304,512]{1,0:T(8,128)(2,1)S(1)}, u32[]{:S(2)}, u32[]{:S(2)}) collective-permute-start(bf16[304,512]{1,0:T(8,128)(2,1)} %copy-done.18), channel_id=1, source_target_pairs={{0,3},{1,0},{2,1},{3,2},{4,7},{5,4},{6,5},{7,6},{8,11},{9,8},{10,9... | collective-permute-start | bytes 933896 | tf_op jit(solution)/shard_map/ppermute | solution.py:19
  95.7 2.0 collective-permute-done.6
  98.8 1.9 copy.26
  100.6 28.5 %collective-permute-start.8 = (bf16[4,8,88,512]{3,2,0,1:T(8,128)(2,1)}, bf16[4,8,88,512]{3,2,0,1:T(8,128)(2,1)}, u32[]{:S(2)}, u32[]{:S(2)}) collective-permute-start(bf16[4,8,88,512]{3,2,0,1:T(8,128)(2,1)} %copy.26), channel_id=1, source_target_pairs={{0,8},{8,0},{1,9},{9,1},{2,10},{10,2},{3,11},{11,3},{4,12},{12,4},... | collective-permute-start | bytes 8650760 | tf_op jit(solution)/shard_map/ppermute | solution.py:14
  129.3 3.2 %collective-permute-start.9 = (bf16[312,512]{1,0:T(8,128)(2,1)}, bf16[312,512]{1,0:T(8,128)(2,1)}, u32[]{:S(2)}, u32[]{:S(2)}) collective-permute-start(bf16[312,512]{1,0:T(8,128)(2,1)} %collective-permute-done.7), channel_id=1, source_target_pairs={{0,1},{1,2},{2,3},{3,0},{4,5},{5,6},{6,7},{7,4},{8,9},{9,10},{10,1... | collective-permute-start | bytes 958472 | tf_op jit(solution)/shard_map/ppermute | solution.py:19
  132.5 4.5 %collective-permute-start.10 = (bf16[312,512]{1,0:T(8,128)(2,1)}, bf16[312,512]{1,0:T(8,128)(2,1)S(1)}, u32[]{:S(2)}, u32[]{:S(2)}) collective-permute-start(bf16[312,512]{1,0:T(8,128)(2,1)} %collective-permute-done.7), channel_id=1, source_target_pairs={{0,2},{1,3},{2,0},{3,1},{4,6},{5,7},{6,4},{7,5},{8,10},{9,11},{10,... | collective-permute-start | bytes 958472 | tf_op jit(solution)/shard_map/ppermute | solution.py:19
  137.1 3.0 %collective-permute-start.11 = (bf16[312,512]{1,0:T(8,128)(2,1)}, bf16[312,512]{1,0:T(8,128)(2,1)S(1)}, u32[]{:S(2)}, u32[]{:S(2)}) collective-permute-start(bf16[312,512]{1,0:T(8,128)(2,1)} %collective-permute-done.7), channel_id=1, source_target_pairs={{0,3},{1,0},{2,1},{3,2},{4,7},{5,4},{6,5},{7,6},{8,11},{9,8},{10,9... | collective-permute-start | bytes 958472 | tf_op jit(solution)/shard_map/ppermute | solution.py:19
  143.0 6.8 %collective-permute-done.10 = bf16[312,512]{1,0:T(8,128)(2,1)S(1)} collective-permute-done((bf16[312,512]{1,0:T(8,128)(2,1)}, bf16[312,512]{1,0:T(8,128)(2,1)S(1)}, u32[]{:S(2)}, u32[]{:S(2)}) %collective-permute-start.10) | collective-permute-done | bytes 319520 | tf_op jit(solution)/shard_map/ppermute | solution.py:19
  149.9 1.1 collective-permute-done.11
  152.1 2.2 select_bitcast_fusion.1
  154.8 2.5 slice.40
  157.4 1.6 copy-done
  159.7 8.6 %all-to-all-start.2 = ((f32[8,8,1280]{2,1,0:T(8,128)}), f32[8,8,1280]{2,1,0:T(8,128)S(1)}, u32[]{:S(2)}, u32[]{:S(2)}) async-start(f32[8,8,1280]{2,1,0:T(8,128)} %broadcast_in_dim.28), calls=%async_computation.2 | async-start | bytes 655360 | tf_op jit(solution)/shard_map/all_to_all | solution.py:37
  168.4 3.3 %fusion.19 = f32[616,512]{1,0:T(8,128)S(1)} fusion(bf16[616,2048]{1,0:T(8,128)(2,1)S(1)} %copy-done.6, bf16[2,2048,512]{2,1,0:T(8,128)(2,1)} %bitcast.86, s32[]{:T(128)S(6)} %select_n.109, bf16[616,512]{1,0:T(8,128)(2,1)} %param.10), kind=kOutput, calls=%fused_computation.22 | convolution fusion | flops 1292476416 | bytes 6512644 | tf_op jit(solution)/shard_map/dot_general | solution.py:88
  174.1 9.9 %all-to-all-done.2 = f32[8,8,1280]{2,1,0:T(8,128)S(1)} async-done(((f32[8,8,1280]{2,1,0:T(8,128)}), f32[8,8,1280]{2,1,0:T(8,128)S(1)}, u32[]{:S(2)}, u32[]{:S(2)}) %all-to-all-start.2) | async-done | bytes 327712 | tf_op jit(solution)/shard_map/all_to_all | solution.py:37
  185.4 8.1 %all-to-all-start.3 = ((f32[8,1,616]{2,1,0:T(1,128)}), f32[8,1,616]{2,1,0:T(1,128)S(1)}, u32[]{:S(2)}, u32[]{:S(2)}) async-start(f32[8,1,616]{2,1,0:T(1,128)} %broadcast_in_dim.29), calls=%async_computation.3 | async-start | bytes 40960 | tf_op jit(solution)/shard_map/all_to_all | solution.py:37
  193.5 1.6 slice.43
  195.1 1.2 concatenate.23
  196.6 10.7 %all-to-all-done.3 = f32[8,1,616]{2,1,0:T(1,128)S(1)} async-done(((f32[8,1,616]{2,1,0:T(1,128)}), f32[8,1,616]{2,1,0:T(1,128)S(1)}, u32[]{:S(2)}, u32[]{:S(2)}) %all-to-all-start.3) | async-done | bytes 19744 | tf_op jit(solution)/shard_map/all_to_all | solution.py:37
  207.4 1.6 multiply_reduce_fusion
  209.5 7.4 %all_to_all.36 = f32[4,8,1280]{2,1,0:T(8,128)S(1)} all-to-all(f32[4,8,1280]{2,1,0:T(8,128)S(1)} %broadcast_in_dim.30), channel_id=1, replica_groups=mesh['zl'=8,'x'=4,'c'=2,'zh'=2,'y'=4] {'y'}, dimensions={0} | all-to-all | bytes 327680 | tf_op jit(solution)/shard_map/all_to_all | solution.py:37
  216.9 3.1 %collective-permute-start.12 = (f32[8,1280]{1,0:T(8,128)S(1)}, f32[8,1280]{1,0:T(8,128)S(1)}, u32[]{:S(2)}, u32[]{:S(2)}) collective-permute-start(f32[8,1280]{1,0:T(8,128)S(1)} %reduce_sum.94), channel_id=1, source_target_pairs={{0,4},{4,0},{1,5},{5,1},{2,6},{6,2},{3,7},{7,3},{8,12},{12,8},{9,1... | collective-permute-start | bytes 122888 | tf_op jit(solution)/shard_map/ppermute | solution.py:14
  220.0 10.9 %collective-permute-done.12 = f32[8,1280]{1,0:T(8,128)S(1)} collective-permute-done((f32[8,1280]{1,0:T(8,128)S(1)}, f32[8,1280]{1,0:T(8,128)S(1)}, u32[]{:S(2)}, u32[]{:S(2)}) %collective-permute-start.12) | collective-permute-done | bytes 40992 | tf_op jit(solution)/shard_map/ppermute | solution.py:14
  232.1 7.7 %all-to-all-start.5 = ((f16[8,8,1408]{2,1,0:T(8,128)(2,1)}), f16[8,8,1408]{2,1,0:T(8,128)(2,1)S(1)}, u32[]{:S(2)}, u32[]{:S(2)}) async-start(f16[8,8,1408]{2,1,0:T(8,128)(2,1)} %broadcast_in_dim.31), calls=%async_computation.5 | async-start | bytes 360448 | tf_op jit(solution)/shard_map/all_to_all | solution.py:37
  241.2 1.2 reshape.175
  242.4 8.2 %all-to-all-done.5 = f16[8,8,1408]{2,1,0:T(8,128)(2,1)S(1)} async-done(((f16[8,8,1408]{2,1,0:T(8,128)(2,1)}), f16[8,8,1408]{2,1,0:T(8,128)(2,1)S(1)}, u32[]{:S(2)}, u32[]{:S(2)}) %all-to-all-start.5) | async-done | bytes 180256 | tf_op jit(solution)/shard_map/all_to_all | solution.py:37
  251.5 4.0 %all-to-all-start.6 = ((f16[4,8,8,1408]{3,2,1,0:T(8,128)(2,1)}), f16[4,8,8,1408]{3,2,1,0:T(8,128)(2,1)S(1)}, u32[]{:S(2)}, u32[]{:S(2)}) async-start(f16[4,8,8,1408]{3,2,1,0:T(8,128)(2,1)} %broadcast_in_dim.32), calls=%async_computation.6 | async-start | bytes 1441792 | tf_op jit(solution)/shard_map/all_to_all | solution.py:37
  255.6 4.1 %fusion.53 = f32[8,512]{1,0:T(8,128)S(1)} fusion(f32[8,1280]{1,0:T(8,128)S(1)} %get-tuple-element.37, f32[64,8,1280]{2,1,0:T(8,128)} %all-gather.3.cloned.1.call-done, s32[8]{0:T(128)S(1)} %iota_add_fusion.1, f32[]{:T(128)} %bitcast.82, f32[]{:T(128)} %bitcast.8), kind=kOutput, calls=%fused_computation.40 | convolution fusion | flops 62947328 | bytes 2678824 | tf_op jit(solution)/shard_map/dot_general | solution.py:124
  259.7 1.4 multiply_reduce_fusion.3
  262.1 1.4 all-to-all-done.6
  263.7 9.7 %collective-permute-start.13 = (f16[4,8,8,1408]{3,2,1,0:T(8,128)(2,1)S(1)}, f16[4,8,8,1408]{3,2,1,0:T(8,128)(2,1)S(1)}, u32[]{:S(2)}, u32[]{:S(2)}) collective-permute-start(f16[4,8,8,1408]{3,2,1,0:T(8,128)(2,1)S(1)} %all-to-all-done.6), channel_id=1, source_target_pairs={{0,8},{8,0},{1,9},{9,1},{2,10},{10,2},{3,11},{11,3},{4,12},{12,4},... | collective-permute-start | bytes 2162696 | tf_op jit(solution)/shard_map/ppermute | solution.py:14
  273.5 1.2 fusion.61
  275.5 2.4 fusion.74
  278.2 1.9 collective-permute-start.14
  280.1 1.2 fusion.67
  (119 shorter events, 23.4 us)
Async XLA Ops:
  7.2 15.1 %copy-start.4 = (bf16[616,512]{1,0:T(8,128)(2,1)S(1)}, bf16[616,512]{1,0:T(8,128)(2,1)}, u32[]{:S(2)}) copy-start(bf16[616,512]{1,0:T(8,128)(2,1)} %param.9) | copy-start | bytes 1892356
  9.2 47.4 %all-to-all-start = ((bf16[8,88,512]{2,1,0:T(8,128)(2,1)}), bf16[8,88,512]{2,1,0:T(8,128)(2,1)S(1)}, u32[]{:S(2)}, u32[]{:S(2)}) async-start(bf16[8,88,512]{2,1,0:T(8,128)(2,1)} %broadcast_in_dim.23), calls=%async_computation | async-start | bytes 1441792 | tf_op jit(solution)/shard_map/all_to_all | solution.py:37
  22.3 28.5 %collective-permute-start.1 = (bf16[616,512]{1,0:T(8,128)(2,1)S(1)}, bf16[616,512]{1,0:T(8,128)(2,1)S(1)}, u32[]{:S(2)}, u32[]{:S(2)}) collective-permute-start(bf16[616,512]{1,0:T(8,128)(2,1)S(1)} %copy-done.4), channel_id=1, source_target_pairs={{0,1},{1,2},{2,3},{3,0},{4,5},{5,6},{6,7},{7,4},{8,9},{9,10},{10,1... | collective-permute-start | bytes 1892360 | tf_op jit(solution)/shard_map/ppermute | solution.py:19
  25.5 29.4 %collective-permute-start.2 = (bf16[616,512]{1,0:T(8,128)(2,1)S(1)}, bf16[616,512]{1,0:T(8,128)(2,1)S(1)}, u32[]{:S(2)}, u32[]{:S(2)}) collective-permute-start(bf16[616,512]{1,0:T(8,128)(2,1)S(1)} %copy-done.4), channel_id=1, source_target_pairs={{0,2},{1,3},{2,0},{3,1},{4,6},{5,7},{6,4},{7,5},{8,10},{9,11},{10,... | collective-permute-start | bytes 1892360 | tf_op jit(solution)/shard_map/ppermute | solution.py:19
  30.0 26.5 %collective-permute-start.3 = (bf16[616,512]{1,0:T(8,128)(2,1)S(1)}, bf16[616,512]{1,0:T(8,128)(2,1)S(1)}, u32[]{:S(2)}, u32[]{:S(2)}) collective-permute-start(bf16[616,512]{1,0:T(8,128)(2,1)S(1)} %copy-done.4), channel_id=1, source_target_pairs={{0,3},{1,0},{2,1},{3,2},{4,7},{5,4},{6,5},{7,6},{8,11},{9,8},{10,9... | collective-permute-start | bytes 1892360 | tf_op jit(solution)/shard_map/ppermute | solution.py:19
  33.0 17.7 %collective-permute-start = (bf16[304,512]{1,0:T(8,128)(2,1)S(1)}, bf16[304,512]{1,0:T(8,128)(2,1)S(1)}, u32[]{:S(2)}, u32[]{:S(2)}) collective-permute-start(bf16[304,512]{1,0:T(8,128)(2,1)S(1)} %slice.30), channel_id=1, source_target_pairs={{0,4},{4,0},{1,5},{5,1},{2,6},{6,2},{3,7},{7,3},{8,12},{12,8},{9,1... | collective-permute-start | bytes 933896 | tf_op jit(solution)/shard_map/ppermute | solution.py:14
  50.8 4.1 %copy-start.18 = (bf16[304,512]{1,0:T(8,128)(2,1)}, bf16[304,512]{1,0:T(8,128)(2,1)S(1)}, u32[]{:S(2)}) copy-start(bf16[304,512]{1,0:T(8,128)(2,1)S(1)} %collective-permute-done) | copy-start | bytes 933892
  50.8 7.6 %copy-start.12 = (bf16[616,512]{1,0:T(8,128)(2,1)}, bf16[616,512]{1,0:T(8,128)(2,1)S(1)}, u32[]{:S(2)}) copy-start(bf16[616,512]{1,0:T(8,128)(2,1)S(1)} %collective-permute-done.1) | copy-start | bytes 1892356
  54.9 3.5 %copy-start.14 = (bf16[616,512]{1,0:T(8,128)(2,1)}, bf16[616,512]{1,0:T(8,128)(2,1)S(1)}, u32[]{:S(2)}) copy-start(bf16[616,512]{1,0:T(8,128)(2,1)S(1)} %collective-permute-done.2) | copy-start | bytes 1892356
  56.6 1.8 copy-start.16
  58.4 40.4 %all-to-all-start.1 = ((bf16[4,8,88,512]{3,2,1,0:T(8,128)(2,1)}), bf16[4,8,88,512]{3,2,1,0:T(8,128)(2,1)S(1)}, u32[]{:S(2)}, u32[]{:S(2)}) async-start(bf16[4,8,88,512]{3,2,1,0:T(8,128)(2,1)} %broadcast_in_dim.24), calls=%async_computation.1 | async-start | bytes 5767168 | tf_op jit(solution)/shard_map/all_to_all | solution.py:37
  63.2 35.6 %collective-permute-start.7 = (bf16[312,512]{1,0:T(8,128)(2,1)}, bf16[312,512]{1,0:T(8,128)(2,1)}, u32[]{:S(2)}, u32[]{:S(2)}) collective-permute-start(bf16[312,512]{1,0:T(8,128)(2,1)} %slice.31), channel_id=1, source_target_pairs={{0,4},{4,0},{1,5},{5,1},{2,6},{6,2},{3,7},{7,3},{8,12},{12,8},{9,1... | collective-permute-start | bytes 958472 | tf_op jit(solution)/shard_map/ppermute | solution.py:14
  80.3 12.6 %copy-start.13 = (bf16[616,512]{1,0:T(8,128)(2,1)S(1)}, bf16[616,512]{1,0:T(8,128)(2,1)}, u32[]{:S(2)}) copy-start(bf16[616,512]{1,0:T(8,128)(2,1)} %copy-done.12) | copy-start | bytes 1892356
  80.3 14.8 %collective-permute-start.4 = (bf16[304,512]{1,0:T(8,128)(2,1)}, bf16[304,512]{1,0:T(8,128)(2,1)S(1)}, u32[]{:S(2)}, u32[]{:S(2)}) collective-permute-start(bf16[304,512]{1,0:T(8,128)(2,1)} %copy-done.18), channel_id=1, source_target_pairs={{0,1},{1,2},{2,3},{3,0},{4,5},{5,6},{6,7},{7,4},{8,9},{9,10},{10,1... | collective-permute-start | bytes 933896 | tf_op jit(solution)/shard_map/ppermute | solution.py:19
  84.4 11.0 %collective-permute-start.5 = (bf16[304,512]{1,0:T(8,128)(2,1)}, bf16[304,512]{1,0:T(8,128)(2,1)S(1)}, u32[]{:S(2)}, u32[]{:S(2)}) collective-permute-start(bf16[304,512]{1,0:T(8,128)(2,1)} %copy-done.18), channel_id=1, source_target_pairs={{0,2},{1,3},{2,0},{3,1},{4,6},{5,7},{6,4},{7,5},{8,10},{9,11},{10,... | collective-permute-start | bytes 933896 | tf_op jit(solution)/shard_map/ppermute | solution.py:19
  89.5 8.1 %collective-permute-start.6 = (bf16[304,512]{1,0:T(8,128)(2,1)}, bf16[304,512]{1,0:T(8,128)(2,1)S(1)}, u32[]{:S(2)}, u32[]{:S(2)}) collective-permute-start(bf16[304,512]{1,0:T(8,128)(2,1)} %copy-done.18), channel_id=1, source_target_pairs={{0,3},{1,0},{2,1},{3,2},{4,7},{5,4},{6,5},{7,6},{8,11},{9,8},{10,9... | collective-permute-start | bytes 933896 | tf_op jit(solution)/shard_map/ppermute | solution.py:19
  92.8 1.1 copy-start.15
  92.9 1.2 copy-start.17
  94.1 1.0 copy-start.19
  94.2 1.5 copy-start.5
  97.7 1.1 copy-start.10
  98.8 30.4 %copy-start.20 = (f32[8,1280]{1,0:T(8,128)S(1)}, f32[8,1280]{1,0:T(8,128)}, u32[]{:S(2)}) copy-start(f32[8,1280]{1,0:T(8,128)} %param.15) | copy-start | bytes 122884
  100.6 51.5 %collective-permute-start.8 = (bf16[4,8,88,512]{3,2,0,1:T(8,128)(2,1)}, bf16[4,8,88,512]{3,2,0,1:T(8,128)(2,1)}, u32[]{:S(2)}, u32[]{:S(2)}) collective-permute-start(bf16[4,8,88,512]{3,2,0,1:T(8,128)(2,1)} %copy.26), channel_id=1, source_target_pairs={{0,8},{8,0},{1,9},{9,1},{2,10},{10,2},{3,11},{11,3},{4,12},{12,4},... | collective-permute-start | bytes 8650760 | tf_op jit(solution)/shard_map/ppermute | solution.py:14
  129.3 12.7 %collective-permute-start.9 = (bf16[312,512]{1,0:T(8,128)(2,1)}, bf16[312,512]{1,0:T(8,128)(2,1)}, u32[]{:S(2)}, u32[]{:S(2)}) collective-permute-start(bf16[312,512]{1,0:T(8,128)(2,1)} %collective-permute-done.7), channel_id=1, source_target_pairs={{0,1},{1,2},{2,3},{3,0},{4,5},{5,6},{6,7},{7,4},{8,9},{9,10},{10,1... | collective-permute-start | bytes 958472 | tf_op jit(solution)/shard_map/ppermute | solution.py:19
  132.5 17.3 %collective-permute-start.10 = (bf16[312,512]{1,0:T(8,128)(2,1)}, bf16[312,512]{1,0:T(8,128)(2,1)S(1)}, u32[]{:S(2)}, u32[]{:S(2)}) collective-permute-start(bf16[312,512]{1,0:T(8,128)(2,1)} %collective-permute-done.7), channel_id=1, source_target_pairs={{0,2},{1,3},{2,0},{3,1},{4,6},{5,7},{6,4},{7,5},{8,10},{9,11},{10,... | collective-permute-start | bytes 958472 | tf_op jit(solution)/shard_map/ppermute | solution.py:19
  137.1 13.9 %collective-permute-start.11 = (bf16[312,512]{1,0:T(8,128)(2,1)}, bf16[312,512]{1,0:T(8,128)(2,1)S(1)}, u32[]{:S(2)}, u32[]{:S(2)}) collective-permute-start(bf16[312,512]{1,0:T(8,128)(2,1)} %collective-permute-done.7), channel_id=1, source_target_pairs={{0,3},{1,0},{2,1},{3,2},{4,7},{5,4},{6,5},{7,6},{8,11},{9,8},{10,9... | collective-permute-start | bytes 958472 | tf_op jit(solution)/shard_map/ppermute | solution.py:19
  151.0 1.1 copy-start.8
  154.8 4.1 %copy-start = (bf16[8,4,2,88,512]{4,3,2,1,0:T(8,128)(2,1)}, bf16[8,4,2,88,512]{4,3,2,1,0:T(8,128)(2,1)S(1)}, u32[]{:S(2)}) copy-start(bf16[8,4,2,88,512]{4,3,2,1,0:T(8,128)(2,1)S(1)} %maximum_bitcast_fusion) | copy-start | bytes 17301508
  154.8 13.5 %copy-start.6 = (bf16[616,2048]{1,0:T(8,128)(2,1)S(1)}, bf16[616,2048]{1,0:T(8,128)(2,1)}, u32[]{:S(2)}) copy-start(bf16[616,2048]{1,0:T(8,128)(2,1)} %copy-done.5) | copy-start | bytes 7569412
  159.7 24.3 %all-to-all-start.2 = ((f32[8,8,1280]{2,1,0:T(8,128)}), f32[8,8,1280]{2,1,0:T(8,128)S(1)}, u32[]{:S(2)}, u32[]{:S(2)}) async-start(f32[8,8,1280]{2,1,0:T(8,128)} %broadcast_in_dim.28), calls=%async_computation.2 | async-start | bytes 655360 | tf_op jit(solution)/shard_map/all_to_all | solution.py:37
  168.3 87.3 %all-gather.3.cloned.1.call-start = ((), (), s32[]{:S(2)}) async-start(), calls=%async_computation.7 | async-start | bytes 2949120 | tf_op jit(solution)/shard_map/all_gather | solution.py:96
  168.3 3.4 %copy-start.3 = (bf16[8,4,2,64,512]{4,3,2,1,0:T(8,128)(2,1)S(1)}, bf16[8,4,2,64,512]{4,3,2,1,0:T(8,128)(2,1)}, u32[]{:S(2)}) copy-start(bf16[8,4,2,64,512]{4,3,2,1,0:T(8,128)(2,1)} %slice.40) | copy-start | bytes 12582916
  168.4 3.4 %copy-start.11 = (bf16[304,2048]{1,0:T(8,128)(2,1)S(1)}, bf16[304,2048]{1,0:T(8,128)(2,1)}, u32[]{:S(2)}) copy-start(bf16[304,2048]{1,0:T(8,128)(2,1)} %copy-done.10) | copy-start | bytes 3735556
  171.7 1.3 copy-start.9
  173.9 19.6 %copy-start.22 = (s32[8]{0:T(128)S(1)}, s32[8]{0:T(128)}, u32[]{:S(2)}) copy-start(s32[8]{0:T(128)} %param.13) | copy-start | bytes 100
  184.0 0.7 copy-start.7
  185.4 21.9 %all-to-all-start.3 = ((f32[8,1,616]{2,1,0:T(1,128)}), f32[8,1,616]{2,1,0:T(1,128)S(1)}, u32[]{:S(2)}, u32[]{:S(2)}) async-start(f32[8,1,616]{2,1,0:T(1,128)} %broadcast_in_dim.29), calls=%async_computation.3 | async-start | bytes 40960 | tf_op jit(solution)/shard_map/all_to_all | solution.py:37
  196.3 11.1 %copy-start.21 = (f32[512]{0:T(512)S(1)}, f32[512]{0:T(512)}, u32[]{:S(2)}) copy-start(f32[512]{0:T(512)} %param.12) | copy-start | bytes 6148
  216.9 14.0 %collective-permute-start.12 = (f32[8,1280]{1,0:T(8,128)S(1)}, f32[8,1280]{1,0:T(8,128)S(1)}, u32[]{:S(2)}, u32[]{:S(2)}) collective-permute-start(f32[8,1280]{1,0:T(8,128)S(1)} %reduce_sum.94), channel_id=1, source_target_pairs={{0,4},{4,0},{1,5},{5,1},{2,6},{6,2},{3,7},{7,3},{8,12},{12,8},{9,1... | collective-permute-start | bytes 122888 | tf_op jit(solution)/shard_map/ppermute | solution.py:14
  232.1 18.4 %all-to-all-start.5 = ((f16[8,8,1408]{2,1,0:T(8,128)(2,1)}), f16[8,8,1408]{2,1,0:T(8,128)(2,1)S(1)}, u32[]{:S(2)}, u32[]{:S(2)}) async-start(f16[8,8,1408]{2,1,0:T(8,128)(2,1)} %broadcast_in_dim.31), calls=%async_computation.5 | async-start | bytes 360448 | tf_op jit(solution)/shard_map/all_to_all | solution.py:37
  251.5 12.0 %all-to-all-start.6 = ((f16[4,8,8,1408]{3,2,1,0:T(8,128)(2,1)}), f16[4,8,8,1408]{3,2,1,0:T(8,128)(2,1)S(1)}, u32[]{:S(2)}, u32[]{:S(2)}) async-start(f16[4,8,8,1408]{3,2,1,0:T(8,128)(2,1)} %broadcast_in_dim.32), calls=%async_computation.6 | async-start | bytes 1441792 | tf_op jit(solution)/shard_map/all_to_all | solution.py:37
  255.6 4.1 %copy-start.1 = (f32[64,8,1280]{2,1,0:T(8,128)S(1)}, f32[64,8,1280]{2,1,0:T(8,128)}, u32[]{:S(2)}) copy-start(f32[64,8,1280]{2,1,0:T(8,128)} %all-gather.3.cloned.1.call-done) | copy-start | bytes 7864324
  259.7 1.5 copy-start.2
  263.7 14.2 %collective-permute-start.13 = (f16[4,8,8,1408]{3,2,1,0:T(8,128)(2,1)S(1)}, f16[4,8,8,1408]{3,2,1,0:T(8,128)(2,1)S(1)}, u32[]{:S(2)}, u32[]{:S(2)}) collective-permute-start(f16[4,8,8,1408]{3,2,1,0:T(8,128)(2,1)S(1)} %all-to-all-done.6), channel_id=1, source_target_pairs={{0,8},{8,0},{1,9},{9,1},{2,10},{10,2},{3,11},{11,3},{4,12},{12,4},... | collective-permute-start | bytes 2162696 | tf_op jit(solution)/shard_map/ppermute | solution.py:14
  278.2 4.8 %collective-permute-start.14 = (f32[]{:T(128)}, f32[]{:T(128)}, u32[]{:S(2)}, u32[]{:S(2)}) collective-permute-start(f32[]{:T(128)} %fusion.74), channel_id=1, source_target_pairs={{0,8},{8,0},{1,9},{9,1},{2,10},{10,2},{3,11},{11,3},{4,12},{12,4},... | collective-permute-start | bytes 20 | tf_op jit(solution)/shard_map/ppermute | solution.py:14
Sparse Core Ops, SparseCore 0:
  184.9 33.2 all-gather.2

commit v3 on v2

--- a/solution.py
+++ b/solution.py
@@ -76,7 +76,6 @@
     rows, far_a, far_b, near = lax.optimization_barrier((rows, in_order(far_a, y), far_b, near))
     other = swap(rows, "c")
     far_b = around_y(far_b)
-    other, picture = lax.optimization_barrier((other, picture))
     pictures = gather(picture, ("zl",))
     first, second = jnp.where(c == 0, rows, other), jnp.where(c == 0, other, rows)
     both = jnp.stack([first, second], axis=2).transpose(1, 0, 2, 3, 4)

time: 294 us -> 277 us (0.942)
  waiting for transfers between devices: 67.5 us -> 52.8 us
    all_to_all x6, waiting for transfers between devices: 30.1 us -> 20.3 us  [gather(): return lax.all_to_all(jnp.broadcast_to(v[None], (n,) + v.shape), axes, 0, 0)]
    ppermute x9, waiting for transfers between devices: 16.7 us -> 11.7 us  [shift(): return lax.ppermute(v, axis, [(i, (i + by) % n) for i in range(n)])]
    unnamed x46 -> x38, local copies, waits for them, and re-layouts: 6.94 us -> 6.34 us
  transfers between devices with their start and end apart: 22 -> 22, of which waited for: 13 -> 9; matrix products, arithmetic and copies ran while one was open for 11% -> 13% of each run, Pallas kernels for 0% -> 0%
where the time goes in v3:
time: 277 us; the launch traced here: 276 us
  starting transfers between devices  148 us (53%)
  waiting for transfers between devices  52.8 us (19%)
  local copies, waits for them, and re-layouts  25.1 us (9%)
  between operations  18.5 us (7%)
  matrix products  16.6 us (6%)
  other arithmetic  7.65 us (3%)
  blocking collectives  7.4 us (3%)
    ppermute x6, starting transfers between devices, swap(): return lax.ppermute(v, axis, [(0, 1), (1, 0)])  68.2 us
    all_to_all x6, starting transfers between devices, gather(): return lax.all_to_all(jnp.broadcast_to(v[None], (n,) + v.shape), axes, 0, 0)  46.3 us
    ppermute x9, starting transfers between devices, shift(): return lax.ppermute(v, axis, [(i, (i + by) % n) for i in range(n)])  33.6 us
    ppermute x6, waiting for transfers between devices, swap(): return lax.ppermute(v, axis, [(0, 1), (1, 0)])  20.7 us
    all_to_all x6, waiting for transfers between devices, gather(): return lax.all_to_all(jnp.broadcast_to(v[None], (n,) + v.shape), axes, 0, 0)  20.3 us
    ppermute x9, waiting for transfers between devices, shift(): return lax.ppermute(v, axis, [(i, (i + by) % n) for i in range(n)])  11.7 us
    all_to_all x1, blocking collectives, gather(): return lax.all_to_all(jnp.broadcast_to(v[None], (n,) + v.shape), axes, 0, 0)  7.4 us
    unnamed x38, local copies, waits for them, and re-layouts  6.34 us
  transfers between devices with their start and end apart: 22, of which 9 were waited for; matrix products, arithmetic and copies ran while one was open for 13% of the time, Pallas kernels for 0%

profile of v3, /device:TPU:1, one launch (start us, length us, event | category | flops | bytes accessed | tf_op | source)
XLA Modules:
  0.0 276.1 jit_solution(10636905371249973683)
XLA Ops:
  9.2 13.1 %all-to-all-start = ((bf16[8,88,512]{2,1,0:T(8,128)(2,1)}), bf16[8,88,512]{2,1,0:T(8,128)(2,1)S(1)}, u32[]{:S(2)}, u32[]{:S(2)}) async-start(bf16[8,88,512]{2,1,0:T(8,128)(2,1)} %broadcast_in_dim.23), calls=%async_computation | async-start | bytes 1441792 | tf_op jit(solution)/shard_map/all_to_all | solution.py:37
  22.3 3.2 %collective-permute-start.1 = (bf16[616,512]{1,0:T(8,128)(2,1)S(1)}, bf16[616,512]{1,0:T(8,128)(2,1)S(1)}, u32[]{:S(2)}, u32[]{:S(2)}) collective-permute-start(bf16[616,512]{1,0:T(8,128)(2,1)S(1)} %copy-done.3), channel_id=1, source_target_pairs={{0,1},{1,2},{2,3},{3,0},{4,5},{5,6},{6,7},{7,4},{8,9},{9,10},{10,1... | collective-permute-start | bytes 1892360 | tf_op jit(solution)/shard_map/ppermute | solution.py:19
  25.5 4.5 %collective-permute-start.2 = (bf16[616,512]{1,0:T(8,128)(2,1)S(1)}, bf16[616,512]{1,0:T(8,128)(2,1)S(1)}, u32[]{:S(2)}, u32[]{:S(2)}) collective-permute-start(bf16[616,512]{1,0:T(8,128)(2,1)S(1)} %copy-done.3), channel_id=1, source_target_pairs={{0,2},{1,3},{2,0},{3,1},{4,6},{5,7},{6,4},{7,5},{8,10},{9,11},{10,... | collective-permute-start | bytes 1892360 | tf_op jit(solution)/shard_map/ppermute | solution.py:19
  30.0 3.0 %collective-permute-start.3 = (bf16[616,512]{1,0:T(8,128)(2,1)S(1)}, bf16[616,512]{1,0:T(8,128)(2,1)S(1)}, u32[]{:S(2)}, u32[]{:S(2)}) collective-permute-start(bf16[616,512]{1,0:T(8,128)(2,1)S(1)} %copy-done.3), channel_id=1, source_target_pairs={{0,3},{1,0},{2,1},{3,2},{4,7},{5,4},{6,5},{7,6},{8,11},{9,8},{10,9... | collective-permute-start | bytes 1892360 | tf_op jit(solution)/shard_map/ppermute | solution.py:19
  33.0 7.9 %collective-permute-start = (bf16[304,512]{1,0:T(8,128)(2,1)S(1)}, bf16[304,512]{1,0:T(8,128)(2,1)}, u32[]{:S(2)}, u32[]{:S(2)}) collective-permute-start(bf16[304,512]{1,0:T(8,128)(2,1)S(1)} %slice.30), channel_id=1, source_target_pairs={{0,4},{4,0},{1,5},{5,1},{2,6},{6,2},{3,7},{7,3},{8,12},{12,8},{9,1... | collective-permute-start | bytes 933896 | tf_op jit(solution)/shard_map/ppermute | solution.py:14
  41.0 9.9 %collective-permute-done = bf16[304,512]{1,0:T(8,128)(2,1)} collective-permute-done((bf16[304,512]{1,0:T(8,128)(2,1)S(1)}, bf16[304,512]{1,0:T(8,128)(2,1)}, u32[]{:S(2)}, u32[]{:S(2)}) %collective-permute-start) | collective-permute-done | bytes 311328 | tf_op jit(solution)/shard_map/ppermute | solution.py:14
  50.9 4.0 %collective-permute-done.2 = bf16[616,512]{1,0:T(8,128)(2,1)S(1)} collective-permute-done((bf16[616,512]{1,0:T(8,128)(2,1)S(1)}, bf16[616,512]{1,0:T(8,128)(2,1)S(1)}, u32[]{:S(2)}, u32[]{:S(2)}) %collective-permute-start.2) | collective-permute-done | bytes 630816 | tf_op jit(solution)/shard_map/ppermute | solution.py:19
  54.9 1.7 collective-permute-done.3
  56.6 1.8 broadcast_in_dim.24
  58.4 4.0 %all-to-all-start.1 = ((bf16[4,8,88,512]{3,2,1,0:T(8,128)(2,1)}), bf16[4,8,88,512]{3,2,1,0:T(8,128)(2,1)S(1)}, u32[]{:S(2)}, u32[]{:S(2)}) async-start(bf16[4,8,88,512]{3,2,1,0:T(8,128)(2,1)} %broadcast_in_dim.24), calls=%async_computation.1 | async-start | bytes 5767168 | tf_op jit(solution)/shard_map/all_to_all | solution.py:37
  63.2 17.1 %collective-permute-start.7 = (bf16[312,512]{1,0:T(8,128)(2,1)}, bf16[312,512]{1,0:T(8,128)(2,1)}, u32[]{:S(2)}, u32[]{:S(2)}) collective-permute-start(bf16[312,512]{1,0:T(8,128)(2,1)} %slice.31), channel_id=1, source_target_pairs={{0,4},{4,0},{1,5},{5,1},{2,6},{6,2},{3,7},{7,3},{8,12},{12,8},{9,1... | collective-permute-start | bytes 958472 | tf_op jit(solution)/shard_map/ppermute | solution.py:14
  80.4 4.0 %collective-permute-start.4 = (bf16[304,512]{1,0:T(8,128)(2,1)}, bf16[304,512]{1,0:T(8,128)(2,1)S(1)}, u32[]{:S(2)}, u32[]{:S(2)}) collective-permute-start(bf16[304,512]{1,0:T(8,128)(2,1)} %collective-permute-done), channel_id=1, source_target_pairs={{0,1},{1,2},{2,3},{3,0},{4,5},{5,6},{6,7},{7,4},{8,9},{9,10},{10,1... | collective-permute-start | bytes 933896 | tf_op jit(solution)/shard_map/ppermute | solution.py:19
  84.4 5.1 %collective-permute-start.5 = (bf16[304,512]{1,0:T(8,128)(2,1)}, bf16[304,512]{1,0:T(8,128)(2,1)S(1)}, u32[]{:S(2)}, u32[]{:S(2)}) collective-permute-start(bf16[304,512]{1,0:T(8,128)(2,1)} %collective-permute-done), channel_id=1, source_target_pairs={{0,2},{1,3},{2,0},{3,1},{4,6},{5,7},{6,4},{7,5},{8,10},{9,11},{10,... | collective-permute-start | bytes 933896 | tf_op jit(solution)/shard_map/ppermute | solution.py:19
  89.5 3.0 %collective-permute-start.6 = (bf16[304,512]{1,0:T(8,128)(2,1)}, bf16[304,512]{1,0:T(8,128)(2,1)S(1)}, u32[]{:S(2)}, u32[]{:S(2)}) collective-permute-start(bf16[304,512]{1,0:T(8,128)(2,1)} %collective-permute-done), channel_id=1, source_target_pairs={{0,3},{1,0},{2,1},{3,2},{4,7},{5,4},{6,5},{7,6},{8,11},{9,8},{10,9... | collective-permute-start | bytes 933896 | tf_op jit(solution)/shard_map/ppermute | solution.py:19
  94.4 1.2 constant_dynamic-update-slice_fusion.11
  95.7 2.0 collective-permute-done.6
  97.7 1.1 copy-done.7
  98.9 1.9 copy.26
  100.8 27.9 %collective-permute-start.8 = (bf16[4,8,88,512]{3,2,0,1:T(8,128)(2,1)}, bf16[4,8,88,512]{3,2,0,1:T(8,128)(2,1)}, u32[]{:S(2)}, u32[]{:S(2)}) collective-permute-start(bf16[4,8,88,512]{3,2,0,1:T(8,128)(2,1)} %copy.26), channel_id=1, source_target_pairs={{0,8},{8,0},{1,9},{9,1},{2,10},{10,2},{3,11},{11,3},{4,12},{12,4},... | collective-permute-start | bytes 8650760 | tf_op jit(solution)/shard_map/ppermute | solution.py:14
  128.9 3.2 %collective-permute-start.9 = (bf16[312,512]{1,0:T(8,128)(2,1)}, bf16[312,512]{1,0:T(8,128)(2,1)}, u32[]{:S(2)}, u32[]{:S(2)}) collective-permute-start(bf16[312,512]{1,0:T(8,128)(2,1)} %collective-permute-done.7), channel_id=1, source_target_pairs={{0,1},{1,2},{2,3},{3,0},{4,5},{5,6},{6,7},{7,4},{8,9},{9,10},{10,1... | collective-permute-start | bytes 958472 | tf_op jit(solution)/shard_map/ppermute | solution.py:19
  132.1 4.5 %collective-permute-start.10 = (bf16[312,512]{1,0:T(8,128)(2,1)}, bf16[312,512]{1,0:T(8,128)(2,1)}, u32[]{:S(2)}, u32[]{:S(2)}) collective-permute-start(bf16[312,512]{1,0:T(8,128)(2,1)} %collective-permute-done.7), channel_id=1, source_target_pairs={{0,2},{1,3},{2,0},{3,1},{4,6},{5,7},{6,4},{7,5},{8,10},{9,11},{10,... | collective-permute-start | bytes 958472 | tf_op jit(solution)/shard_map/ppermute | solution.py:19
  137.4 8.9 %all-to-all-start.2 = ((f32[8,8,1280]{2,1,0:T(8,128)}), f32[8,8,1280]{2,1,0:T(8,128)S(1)}, u32[]{:S(2)}, u32[]{:S(2)}) async-start(f32[8,8,1280]{2,1,0:T(8,128)} %broadcast_in_dim.28), calls=%async_computation.2 | async-start | bytes 655360 | tf_op jit(solution)/shard_map/all_to_all | solution.py:37
  146.4 3.0 %collective-permute-start.11 = (bf16[312,512]{1,0:T(8,128)(2,1)}, bf16[312,512]{1,0:T(8,128)(2,1)S(1)}, u32[]{:S(2)}, u32[]{:S(2)}) collective-permute-start(bf16[312,512]{1,0:T(8,128)(2,1)} %collective-permute-done.7), channel_id=1, source_target_pairs={{0,3},{1,0},{2,1},{3,2},{4,7},{5,4},{6,5},{7,6},{8,11},{9,8},{10,9... | collective-permute-start | bytes 958472 | tf_op jit(solution)/shard_map/ppermute | solution.py:19
  149.6 1.0 constant_dynamic-update-slice_fusion.3
  152.6 4.1 %collective-permute-done.11 = bf16[312,512]{1,0:T(8,128)(2,1)S(1)} collective-permute-done((bf16[312,512]{1,0:T(8,128)(2,1)}, bf16[312,512]{1,0:T(8,128)(2,1)S(1)}, u32[]{:S(2)}, u32[]{:S(2)}) %collective-permute-start.11) | collective-permute-done | bytes 319520 | tf_op jit(solution)/shard_map/ppermute | solution.py:19
  156.8 2.2 select_bitcast_fusion.1
  160.1 2.4 copy-done
  163.5 1.5 fusion.19
  168.3 7.0 %all-to-all-start.3 = ((f32[8,1,616]{2,1,0:T(1,128)}), f32[8,1,616]{2,1,0:T(1,128)S(1)}, u32[]{:S(2)}, u32[]{:S(2)}) async-start(f32[8,1,616]{2,1,0:T(1,128)} %broadcast_in_dim.29), calls=%async_computation.3 | async-start | bytes 40960 | tf_op jit(solution)/shard_map/all_to_all | solution.py:37
  175.4 1.6 slice.43
  177.0 1.2 concatenate.23
  178.5 10.7 %all-to-all-done.3 = f32[8,1,616]{2,1,0:T(1,128)S(1)} async-done(((f32[8,1,616]{2,1,0:T(1,128)}), f32[8,1,616]{2,1,0:T(1,128)S(1)}, u32[]{:S(2)}, u32[]{:S(2)}) %all-to-all-start.3) | async-done | bytes 19744 | tf_op jit(solution)/shard_map/all_to_all | solution.py:37
  189.4 1.6 multiply_reduce_fusion
  191.5 7.4 %all_to_all.36 = f32[4,8,1280]{2,1,0:T(8,128)S(1)} all-to-all(f32[4,8,1280]{2,1,0:T(8,128)S(1)} %broadcast_in_dim.30), channel_id=1, replica_groups=mesh['zl'=8,'x'=4,'c'=2,'zh'=2,'y'=4] {'y'}, dimensions={0} | all-to-all | bytes 327680 | tf_op jit(solution)/shard_map/all_to_all | solution.py:37
  198.9 3.0 %collective-permute-start.12 = (f32[8,1280]{1,0:T(8,128)S(1)}, f32[8,1280]{1,0:T(8,128)S(1)}, u32[]{:S(2)}, u32[]{:S(2)}) collective-permute-start(f32[8,1280]{1,0:T(8,128)S(1)} %reduce_sum.94), channel_id=1, source_target_pairs={{0,4},{4,0},{1,5},{5,1},{2,6},{6,2},{3,7},{7,3},{8,12},{12,8},{9,1... | collective-permute-start | bytes 122888 | tf_op jit(solution)/shard_map/ppermute | solution.py:14
  201.9 10.8 %collective-permute-done.12 = f32[8,1280]{1,0:T(8,128)S(1)} collective-permute-done((f32[8,1280]{1,0:T(8,128)S(1)}, f32[8,1280]{1,0:T(8,128)S(1)}, u32[]{:S(2)}, u32[]{:S(2)}) %collective-permute-start.12) | collective-permute-done | bytes 40992 | tf_op jit(solution)/shard_map/ppermute | solution.py:14
  213.9 9.0 %all-to-all-start.5 = ((f16[8,8,1408]{2,1,0:T(8,128)(2,1)}), f16[8,8,1408]{2,1,0:T(8,128)(2,1)S(1)}, u32[]{:S(2)}, u32[]{:S(2)}) async-start(f16[8,8,1408]{2,1,0:T(8,128)(2,1)} %broadcast_in_dim.31), calls=%async_computation.5 | async-start | bytes 360448 | tf_op jit(solution)/shard_map/all_to_all | solution.py:37
  224.2 1.2 reshape.175
  225.5 8.2 %all-to-all-done.5 = f16[8,8,1408]{2,1,0:T(8,128)(2,1)S(1)} async-done(((f16[8,8,1408]{2,1,0:T(8,128)(2,1)}), f16[8,8,1408]{2,1,0:T(8,128)(2,1)S(1)}, u32[]{:S(2)}, u32[]{:S(2)}) %all-to-all-start.5) | async-done | bytes 180256 | tf_op jit(solution)/shard_map/all_to_all | solution.py:37
  234.6 4.3 %all-to-all-start.6 = ((f16[4,8,8,1408]{3,2,1,0:T(8,128)(2,1)}), f16[4,8,8,1408]{3,2,1,0:T(8,128)(2,1)S(1)}, u32[]{:S(2)}, u32[]{:S(2)}) async-start(f16[4,8,8,1408]{3,2,1,0:T(8,128)(2,1)} %broadcast_in_dim.32), calls=%async_computation.6 | async-start | bytes 1441792 | tf_op jit(solution)/shard_map/all_to_all | solution.py:37
  238.8 4.1 %fusion.53 = f32[8,512]{1,0:T(8,128)S(1)} fusion(f32[8,1280]{1,0:T(8,128)S(1)} %get-tuple-element.33, f32[64,8,1280]{2,1,0:T(8,128)} %all-gather.3.cloned.1.call-done, s32[8]{0:T(128)S(1)} %iota_add_fusion.1, f32[]{:T(128)} %bitcast.82, f32[]{:T(128)} %bitcast.8), kind=kOutput, calls=%fused_computation.40 | convolution fusion | flops 62947328 | bytes 2678824 | tf_op jit(solution)/shard_map/dot_general | solution.py:123
  243.0 1.4 multiply_reduce_fusion.3
  245.4 1.4 all-to-all-done.6
  247.0 10.3 %collective-permute-start.13 = (f16[4,8,8,1408]{3,2,1,0:T(8,128)(2,1)S(1)}, f16[4,8,8,1408]{3,2,1,0:T(8,128)(2,1)S(1)}, u32[]{:S(2)}, u32[]{:S(2)}) collective-permute-start(f16[4,8,8,1408]{3,2,1,0:T(8,128)(2,1)S(1)} %all-to-all-done.6), channel_id=1, source_target_pairs={{0,8},{8,0},{1,9},{9,1},{2,10},{10,2},{3,11},{11,3},{4,12},{12,4},... | collective-permute-start | bytes 2162696 | tf_op jit(solution)/shard_map/ppermute | solution.py:14
  257.4 1.2 fusion.61
  259.4 2.4 fusion.74
  262.1 1.9 collective-permute-start.14
  264.0 1.2 fusion.67
  (111 shorter events, 20.3 us)
Async XLA Ops:
  7.2 15.1 %copy-start.3 = (bf16[616,512]{1,0:T(8,128)(2,1)S(1)}, bf16[616,512]{1,0:T(8,128)(2,1)}, u32[]{:S(2)}) copy-start(bf16[616,512]{1,0:T(8,128)(2,1)} %param.9) | copy-start | bytes 1892356
  9.2 47.4 %all-to-all-start = ((bf16[8,88,512]{2,1,0:T(8,128)(2,1)}), bf16[8,88,512]{2,1,0:T(8,128)(2,1)S(1)}, u32[]{:S(2)}, u32[]{:S(2)}) async-start(bf16[8,88,512]{2,1,0:T(8,128)(2,1)} %broadcast_in_dim.23), calls=%async_computation | async-start | bytes 1441792 | tf_op jit(solution)/shard_map/all_to_all | solution.py:37
  22.3 28.6 %collective-permute-start.1 = (bf16[616,512]{1,0:T(8,128)(2,1)S(1)}, bf16[616,512]{1,0:T(8,128)(2,1)S(1)}, u32[]{:S(2)}, u32[]{:S(2)}) collective-permute-start(bf16[616,512]{1,0:T(8,128)(2,1)S(1)} %copy-done.3), channel_id=1, source_target_pairs={{0,1},{1,2},{2,3},{3,0},{4,5},{5,6},{6,7},{7,4},{8,9},{9,10},{10,1... | collective-permute-start | bytes 1892360 | tf_op jit(solution)/shard_map/ppermute | solution.py:19
  25.5 29.4 %collective-permute-start.2 = (bf16[616,512]{1,0:T(8,128)(2,1)S(1)}, bf16[616,512]{1,0:T(8,128)(2,1)S(1)}, u32[]{:S(2)}, u32[]{:S(2)}) collective-permute-start(bf16[616,512]{1,0:T(8,128)(2,1)S(1)} %copy-done.3), channel_id=1, source_target_pairs={{0,2},{1,3},{2,0},{3,1},{4,6},{5,7},{6,4},{7,5},{8,10},{9,11},{10,... | collective-permute-start | bytes 1892360 | tf_op jit(solution)/shard_map/ppermute | solution.py:19
  30.0 26.5 %collective-permute-start.3 = (bf16[616,512]{1,0:T(8,128)(2,1)S(1)}, bf16[616,512]{1,0:T(8,128)(2,1)S(1)}, u32[]{:S(2)}, u32[]{:S(2)}) collective-permute-start(bf16[616,512]{1,0:T(8,128)(2,1)S(1)} %copy-done.3), channel_id=1, source_target_pairs={{0,3},{1,0},{2,1},{3,2},{4,7},{5,4},{6,5},{7,6},{8,11},{9,8},{10,9... | collective-permute-start | bytes 1892360 | tf_op jit(solution)/shard_map/ppermute | solution.py:19
  33.0 17.9 %collective-permute-start = (bf16[304,512]{1,0:T(8,128)(2,1)S(1)}, bf16[304,512]{1,0:T(8,128)(2,1)}, u32[]{:S(2)}, u32[]{:S(2)}) collective-permute-start(bf16[304,512]{1,0:T(8,128)(2,1)S(1)} %slice.30), channel_id=1, source_target_pairs={{0,4},{4,0},{1,5},{5,1},{2,6},{6,2},{3,7},{7,3},{8,12},{12,8},{9,1... | collective-permute-start | bytes 933896 | tf_op jit(solution)/shard_map/ppermute | solution.py:14
  50.9 7.5 %copy-start.9 = (bf16[616,512]{1,0:T(8,128)(2,1)}, bf16[616,512]{1,0:T(8,128)(2,1)S(1)}, u32[]{:S(2)}) copy-start(bf16[616,512]{1,0:T(8,128)(2,1)S(1)} %collective-permute-done.1) | copy-start | bytes 1892356
  54.9 3.5 %copy-start.11 = (bf16[616,512]{1,0:T(8,128)(2,1)}, bf16[616,512]{1,0:T(8,128)(2,1)S(1)}, u32[]{:S(2)}) copy-start(bf16[616,512]{1,0:T(8,128)(2,1)S(1)} %collective-permute-done.2) | copy-start | bytes 1892356
  56.6 1.8 copy-start.13
  58.4 40.5 %all-to-all-start.1 = ((bf16[4,8,88,512]{3,2,1,0:T(8,128)(2,1)}), bf16[4,8,88,512]{3,2,1,0:T(8,128)(2,1)S(1)}, u32[]{:S(2)}, u32[]{:S(2)}) async-start(bf16[4,8,88,512]{3,2,1,0:T(8,128)(2,1)} %broadcast_in_dim.24), calls=%async_computation.1 | async-start | bytes 5767168 | tf_op jit(solution)/shard_map/all_to_all | solution.py:37
  63.2 35.7 %collective-permute-start.7 = (bf16[312,512]{1,0:T(8,128)(2,1)}, bf16[312,512]{1,0:T(8,128)(2,1)}, u32[]{:S(2)}, u32[]{:S(2)}) collective-permute-start(bf16[312,512]{1,0:T(8,128)(2,1)} %slice.31), channel_id=1, source_target_pairs={{0,4},{4,0},{1,5},{5,1},{2,6},{6,2},{3,7},{7,3},{8,12},{12,8},{9,1... | collective-permute-start | bytes 958472 | tf_op jit(solution)/shard_map/ppermute | solution.py:14
  80.3 12.6 %copy-start.10 = (bf16[616,512]{1,0:T(8,128)(2,1)S(1)}, bf16[616,512]{1,0:T(8,128)(2,1)}, u32[]{:S(2)}) copy-start(bf16[616,512]{1,0:T(8,128)(2,1)} %copy-done.9) | copy-start | bytes 1892356
  80.4 15.3 %collective-permute-start.4 = (bf16[304,512]{1,0:T(8,128)(2,1)}, bf16[304,512]{1,0:T(8,128)(2,1)S(1)}, u32[]{:S(2)}, u32[]{:S(2)}) collective-permute-start(bf16[304,512]{1,0:T(8,128)(2,1)} %collective-permute-done), channel_id=1, source_target_pairs={{0,1},{1,2},{2,3},{3,0},{4,5},{5,6},{6,7},{7,4},{8,9},{9,10},{10,1... | collective-permute-start | bytes 933896 | tf_op jit(solution)/shard_map/ppermute | solution.py:19
  84.4 11.3 %collective-permute-start.5 = (bf16[304,512]{1,0:T(8,128)(2,1)}, bf16[304,512]{1,0:T(8,128)(2,1)S(1)}, u32[]{:S(2)}, u32[]{:S(2)}) collective-permute-start(bf16[304,512]{1,0:T(8,128)(2,1)} %collective-permute-done), channel_id=1, source_target_pairs={{0,2},{1,3},{2,0},{3,1},{4,6},{5,7},{6,4},{7,5},{8,10},{9,11},{10,... | collective-permute-start | bytes 933896 | tf_op jit(solution)/shard_map/ppermute | solution.py:19
  89.5 8.1 %collective-permute-start.6 = (bf16[304,512]{1,0:T(8,128)(2,1)}, bf16[304,512]{1,0:T(8,128)(2,1)S(1)}, u32[]{:S(2)}, u32[]{:S(2)}) collective-permute-start(bf16[304,512]{1,0:T(8,128)(2,1)} %collective-permute-done), channel_id=1, source_target_pairs={{0,3},{1,0},{2,1},{3,2},{4,7},{5,4},{6,5},{7,6},{8,11},{9,8},{10,9... | collective-permute-start | bytes 933896 | tf_op jit(solution)/shard_map/ppermute | solution.py:19
  92.8 1.1 copy-start.12
  93.0 1.2 copy-start.14
  94.2 1.5 copy-start.4
  97.7 1.1 copy-start.7
  98.9 29.8 %copy-start.15 = (f32[8,1280]{1,0:T(8,128)S(1)}, f32[8,1280]{1,0:T(8,128)}, u32[]{:S(2)}) copy-start(f32[8,1280]{1,0:T(8,128)} %param.15) | copy-start | bytes 122884
  100.8 56.0 %collective-permute-start.8 = (bf16[4,8,88,512]{3,2,0,1:T(8,128)(2,1)}, bf16[4,8,88,512]{3,2,0,1:T(8,128)(2,1)}, u32[]{:S(2)}, u32[]{:S(2)}) collective-permute-start(bf16[4,8,88,512]{3,2,0,1:T(8,128)(2,1)} %copy.26), channel_id=1, source_target_pairs={{0,8},{8,0},{1,9},{9,1},{2,10},{10,2},{3,11},{11,3},{4,12},{12,4},... | collective-permute-start | bytes 8650760 | tf_op jit(solution)/shard_map/ppermute | solution.py:14
  128.9 21.7 %collective-permute-start.9 = (bf16[312,512]{1,0:T(8,128)(2,1)}, bf16[312,512]{1,0:T(8,128)(2,1)}, u32[]{:S(2)}, u32[]{:S(2)}) collective-permute-start(bf16[312,512]{1,0:T(8,128)(2,1)} %collective-permute-done.7), channel_id=1, source_target_pairs={{0,1},{1,2},{2,3},{3,0},{4,5},{5,6},{6,7},{7,4},{8,9},{9,10},{10,1... | collective-permute-start | bytes 958472 | tf_op jit(solution)/shard_map/ppermute | solution.py:19
  132.1 19.5 %collective-permute-start.10 = (bf16[312,512]{1,0:T(8,128)(2,1)}, bf16[312,512]{1,0:T(8,128)(2,1)}, u32[]{:S(2)}, u32[]{:S(2)}) collective-permute-start(bf16[312,512]{1,0:T(8,128)(2,1)} %collective-permute-done.7), channel_id=1, source_target_pairs={{0,2},{1,3},{2,0},{3,1},{4,6},{5,7},{6,4},{7,5},{8,10},{9,11},{10,... | collective-permute-start | bytes 958472 | tf_op jit(solution)/shard_map/ppermute | solution.py:19
  137.4 29.4 %all-to-all-start.2 = ((f32[8,8,1280]{2,1,0:T(8,128)}), f32[8,8,1280]{2,1,0:T(8,128)S(1)}, u32[]{:S(2)}, u32[]{:S(2)}) async-start(f32[8,8,1280]{2,1,0:T(8,128)} %broadcast_in_dim.28), calls=%async_computation.2 | async-start | bytes 655360 | tf_op jit(solution)/shard_map/all_to_all | solution.py:37
  146.4 92.4 %all-gather.3.cloned.1.call-start = ((), (), s32[]{:S(2)}) async-start(), calls=%async_computation.7 | async-start | bytes 2949120 | tf_op jit(solution)/shard_map/all_gather | solution.py:95
  146.4 10.3 %collective-permute-start.11 = (bf16[312,512]{1,0:T(8,128)(2,1)}, bf16[312,512]{1,0:T(8,128)(2,1)S(1)}, u32[]{:S(2)}, u32[]{:S(2)}) collective-permute-start(bf16[312,512]{1,0:T(8,128)(2,1)} %collective-permute-done.7), channel_id=1, source_target_pairs={{0,3},{1,0},{2,1},{3,2},{4,7},{5,4},{6,5},{7,6},{8,11},{9,8},{10,9... | collective-permute-start | bytes 958472 | tf_op jit(solution)/shard_map/ppermute | solution.py:19
  159.5 2.9 %copy-start = (bf16[8,4,2,88,512]{4,3,2,1,0:T(8,128)(2,1)}, bf16[8,4,2,88,512]{4,3,2,1,0:T(8,128)(2,1)S(1)}, u32[]{:S(2)}) copy-start(bf16[8,4,2,88,512]{4,3,2,1,0:T(8,128)(2,1)S(1)} %maximum_bitcast_fusion) | copy-start | bytes 17301508
  159.5 3.6 %copy-start.5 = (bf16[616,2048]{1,0:T(8,128)(2,1)S(1)}, bf16[616,2048]{1,0:T(8,128)(2,1)}, u32[]{:S(2)}) copy-start(bf16[616,2048]{1,0:T(8,128)(2,1)} %copy-done.4) | copy-start | bytes 7569412
  159.5 3.9 %copy-start.18 = (bf16[616,512]{1,0:T(8,128)(2,1)S(1)}, bf16[616,512]{1,0:T(8,128)(2,1)}, u32[]{:S(2)}) copy-start(bf16[616,512]{1,0:T(8,128)(2,1)} %param.10) | copy-start | bytes 1892356
  163.5 1.5 copy-start.8
  166.7 8.7 %copy-start.17 = (s32[8]{0:T(128)S(1)}, s32[8]{0:T(128)}, u32[]{:S(2)}) copy-start(s32[8]{0:T(128)} %param.13) | copy-start | bytes 100
  166.9 0.7 copy-start.6
  168.3 21.0 %all-to-all-start.3 = ((f32[8,1,616]{2,1,0:T(1,128)}), f32[8,1,616]{2,1,0:T(1,128)S(1)}, u32[]{:S(2)}, u32[]{:S(2)}) async-start(f32[8,1,616]{2,1,0:T(1,128)} %broadcast_in_dim.29), calls=%async_computation.3 | async-start | bytes 40960 | tf_op jit(solution)/shard_map/all_to_all | solution.py:37
  178.2 11.2 %copy-start.16 = (f32[512]{0:T(512)S(1)}, f32[512]{0:T(512)}, u32[]{:S(2)}) copy-start(f32[512]{0:T(512)} %param.12) | copy-start | bytes 6148
  198.9 13.7 %collective-permute-start.12 = (f32[8,1280]{1,0:T(8,128)S(1)}, f32[8,1280]{1,0:T(8,128)S(1)}, u32[]{:S(2)}, u32[]{:S(2)}) collective-permute-start(f32[8,1280]{1,0:T(8,128)S(1)} %reduce_sum.94), channel_id=1, source_target_pairs={{0,4},{4,0},{1,5},{5,1},{2,6},{6,2},{3,7},{7,3},{8,12},{12,8},{9,1... | collective-permute-start | bytes 122888 | tf_op jit(solution)/shard_map/ppermute | solution.py:14
  213.9 19.8 %all-to-all-start.5 = ((f16[8,8,1408]{2,1,0:T(8,128)(2,1)}), f16[8,8,1408]{2,1,0:T(8,128)(2,1)S(1)}, u32[]{:S(2)}, u32[]{:S(2)}) async-start(f16[8,8,1408]{2,1,0:T(8,128)(2,1)} %broadcast_in_dim.31), calls=%async_computation.5 | async-start | bytes 360448 | tf_op jit(solution)/shard_map/all_to_all | solution.py:37
  234.6 12.3 %all-to-all-start.6 = ((f16[4,8,8,1408]{3,2,1,0:T(8,128)(2,1)}), f16[4,8,8,1408]{3,2,1,0:T(8,128)(2,1)S(1)}, u32[]{:S(2)}, u32[]{:S(2)}) async-start(f16[4,8,8,1408]{3,2,1,0:T(8,128)(2,1)} %broadcast_in_dim.32), calls=%async_computation.6 | async-start | bytes 1441792 | tf_op jit(solution)/shard_map/all_to_all | solution.py:37
  238.8 4.1 %copy-start.1 = (f32[64,8,1280]{2,1,0:T(8,128)S(1)}, f32[64,8,1280]{2,1,0:T(8,128)}, u32[]{:S(2)}) copy-start(f32[64,8,1280]{2,1,0:T(8,128)} %all-gather.3.cloned.1.call-done) | copy-start | bytes 7864324
  243.0 1.5 copy-start.2
  247.0 14.9 %collective-permute-start.13 = (f16[4,8,8,1408]{3,2,1,0:T(8,128)(2,1)S(1)}, f16[4,8,8,1408]{3,2,1,0:T(8,128)(2,1)S(1)}, u32[]{:S(2)}, u32[]{:S(2)}) collective-permute-start(f16[4,8,8,1408]{3,2,1,0:T(8,128)(2,1)S(1)} %all-to-all-done.6), channel_id=1, source_target_pairs={{0,8},{8,0},{1,9},{9,1},{2,10},{10,2},{3,11},{11,3},{4,12},{12,4},... | collective-permute-start | bytes 2162696 | tf_op jit(solution)/shard_map/ppermute | solution.py:14
  262.1 4.8 %collective-permute-start.14 = (f32[]{:T(128)}, f32[]{:T(128)}, u32[]{:S(2)}, u32[]{:S(2)}) collective-permute-start(f32[]{:T(128)} %fusion.74), channel_id=1, source_target_pairs={{0,8},{8,0},{1,9},{9,1},{2,10},{10,2},{3,11},{11,3},{4,12},{12,4},... | collective-permute-start | bytes 20 | tf_op jit(solution)/shard_map/ppermute | solution.py:14
Sparse Core Ops, SparseCore 0:
  167.8 33.8 all-gather.2

commit v4 on v3

--- a/solution.py
+++ b/solution.py
@@ -65,8 +65,7 @@
     picture = images / image_norm
 
     far_a = swap(attention[:half], "zh")
-    rows = jnp.concatenate([out_weight, adapter.T, jnp.zeros((4, 512), BF16)], axis=0)
-    rows = gather(rows, ("zl",))
+    rows = gather(out_weight, ("zl",))
     near = around_y(attention)
     rows, far_a, near = lax.optimization_barrier((rows, far_a, near))
     near = in_order(near, y)
@@ -76,11 +75,14 @@
     rows, far_a, far_b, near = lax.optimization_barrier((rows, in_order(far_a, y), far_b, near))
     other = swap(rows, "c")
     far_b = around_y(far_b)
-    pictures = gather(picture, ("zl",))
+    high, low = split(picture, 2)
+    packed = [high[:, :512], high[:, 512:1024], low[:, :512], low[:, 512:1024]]
+    packed += [jnp.concatenate([high[:, 1024:], low[:, 1024:]], axis=1)]
+    packed = jnp.concatenate(packed + [adapter.T, jnp.zeros((4, 512), BF16)], axis=0)
+    packed = gather(packed, ("zl",))
     first, second = jnp.where(c == 0, rows, other), jnp.where(c == 0, other, rows)
     both = jnp.stack([first, second], axis=2).transpose(1, 0, 2, 3, 4)
-    weight = both[:, :, :, :64].reshape(2, 2048, 512)
-    full_adapter = both[:, :, :, 64:84].reshape(1280, 512)
+    weight = both.reshape(2, 2048, 512)
 
     near_w = lax.dynamic_index_in_dim(weight, zh, 0, keepdims=False)
     far_w = lax.dynamic_index_in_dim(weight, 1 - zh, 0, keepdims=False)
@@ -90,9 +92,16 @@
     hidden = jnp.concatenate([top, low], axis=0)
 
     squares = jnp.sum(hidden * hidden, axis=1)
-    squares, pictures = lax.optimization_barrier((squares, pictures))
+    squares, packed = lax.optimization_barrier((squares, packed))
+    full_adapter = lax.all_gather(packed[:, 40:], ("x", "c"))
+    full_adapter = full_adapter[:, :, :20].transpose(1, 0, 2, 3).reshape(1280, 512)
     squares = jnp.sum(gather(squares, TP), axis=0)
-    every_image = lax.all_gather(pictures, ("x", "c")).reshape(512, 1280)
+    squares, packed = lax.optimization_barrier((squares, packed[:, :40]))
+    packed = lax.all_gather(packed, ("x", "c"))
+    parts = [packed[:, :, 8 * i : 8 * i + 8].reshape(512, 512) for i in range(5)]
+    high = jnp.concatenate([parts[0], parts[1], parts[4][:, :256]], axis=1)
+    low = jnp.concatenate([parts[2], parts[3], parts[4][:, 256:]], axis=1)
+    every_image = high.astype(F32) + low.astype(F32)
     normed = hidden * lax.rsqrt(squares / 4096 + 1e-05)[:, None] * norm_gain[None, :]
     normed = normed.reshape(captions, seq_len, 512)
     positions = jnp.arange(seq_len, dtype=jnp.int32)

time: 277 us -> 279 us (level)
  waiting for transfers between devices: 52.8 us -> 63.1 us
  starting transfers between devices: 148 us -> 144 us
    all_gather x1 -> x2, waiting for transfers between devices: 0.01 us -> 12.2 us  [the longest x1 12.2 us: local(): full_adapter = lax.all_gather(packed[:, 40:], ('x', 'c'))]
    ppermute x6, waiting for transfers between devices: 20.7 us -> 11.5 us  [swap(): return lax.ppermute(v, axis, [(0, 1), (1, 0)])]
    all_to_all x6, waiting for transfers between devices: 20.3 us -> 26.5 us  [gather(): return lax.all_to_all(jnp.broadcast_to(v[None], (n,) + v.shape), axes, 0, 0)]
    ppermute x9, starting transfers between devices: 33.6 us -> 28.9 us  [shift(): return lax.ppermute(v, axis, [(i, (i + by) % n) for i in range(n)])]
    unnamed x38 -> x44, local copies, waits for them, and re-layouts: 6.34 us -> 4.61 us
  transfers between devices with their start and end apart: 22 -> 23, of which waited for: 9 -> 13; matrix products, arithmetic and copies ran while one was open for 13% -> 11% of each run, Pallas kernels for 0% -> 0%
where the time goes in v4:
time: 279 us; the launch traced here: 277 us
  starting transfers between devices  144 us (52%)
  waiting for transfers between devices  63.1 us (23%)
  local copies, waits for them, and re-layouts  22.5 us (8%)
  between operations  18.6 us (7%)
  matrix products  15 us (5%)
  blocking collectives  8.91 us (3%)
  other arithmetic  4.89 us (2%)
    ppermute x6, starting transfers between devices, swap(): return lax.ppermute(v, axis, [(0, 1), (1, 0)])  70.2 us
    all_to_all x6, starting transfers between devices, gather(): return lax.all_to_all(jnp.broadcast_to(v[None], (n,) + v.shape), axes, 0, 0)  45.1 us
    ppermute x9, starting transfers between devices, shift(): return lax.ppermute(v, axis, [(i, (i + by) % n) for i in range(n)])  28.9 us
    all_to_all x6, waiting for transfers between devices, gather(): return lax.all_to_all(jnp.broadcast_to(v[None], (n,) + v.shape), axes, 0, 0)  26.5 us
    ppermute x9, waiting for transfers between devices, shift(): return lax.ppermute(v, axis, [(i, (i + by) % n) for i in range(n)])  12.9 us
    all_gather x1, waiting for transfers between devices, local(): full_adapter = lax.all_gather(packed[:, 40:], ('x', 'c'))  12.2 us
    ppermute x6, waiting for transfers between devices, swap(): return lax.ppermute(v, axis, [(0, 1), (1, 0)])  11.5 us
    all_to_all x1, blocking collectives, gather(): return lax.all_to_all(jnp.broadcast_to(v[None], (n,) + v.shape), axes, 0, 0)  8.91 us
  transfers between devices with their start and end apart: 23, of which 13 were waited for; matrix products, arithmetic and copies ran while one was open for 11% of the time, Pallas kernels for 0%

profile of v4, /device:TPU:1, one launch (start us, length us, event | category | flops | bytes accessed | tf_op | source)
XLA Modules:
  0.0 277.4 jit_solution(11067637404941360211)
XLA Ops:
  7.2 1.7 broadcast_in_dim.22
  8.9 13.1 %all-to-all-start = ((bf16[8,64,512]{2,1,0:T(8,128)(2,1)}), bf16[8,64,512]{2,1,0:T(8,128)(2,1)S(1)}, u32[]{:S(2)}, u32[]{:S(2)}) async-start(bf16[8,64,512]{2,1,0:T(8,128)(2,1)} %broadcast_in_dim.22), calls=%async_computation | async-start | bytes 1048576 | tf_op jit(solution)/shard_map/all_to_all | solution.py:37
  22.0 3.2 %collective-permute-start.1 = (bf16[616,512]{1,0:T(8,128)(2,1)S(1)}, bf16[616,512]{1,0:T(8,128)(2,1)S(1)}, u32[]{:S(2)}, u32[]{:S(2)}) collective-permute-start(bf16[616,512]{1,0:T(8,128)(2,1)S(1)} %copy-done), channel_id=1, source_target_pairs={{0,1},{1,2},{2,3},{3,0},{4,5},{5,6},{6,7},{7,4},{8,9},{9,10},{10,1... | collective-permute-start | bytes 1892360 | tf_op jit(solution)/shard_map/ppermute | solution.py:19
  25.2 4.5 %collective-permute-start.2 = (bf16[616,512]{1,0:T(8,128)(2,1)S(1)}, bf16[616,512]{1,0:T(8,128)(2,1)S(1)}, u32[]{:S(2)}, u32[]{:S(2)}) collective-permute-start(bf16[616,512]{1,0:T(8,128)(2,1)S(1)} %copy-done), channel_id=1, source_target_pairs={{0,2},{1,3},{2,0},{3,1},{4,6},{5,7},{6,4},{7,5},{8,10},{9,11},{10,... | collective-permute-start | bytes 1892360 | tf_op jit(solution)/shard_map/ppermute | solution.py:19
  29.7 3.0 %collective-permute-start.3 = (bf16[616,512]{1,0:T(8,128)(2,1)S(1)}, bf16[616,512]{1,0:T(8,128)(2,1)S(1)}, u32[]{:S(2)}, u32[]{:S(2)}) collective-permute-start(bf16[616,512]{1,0:T(8,128)(2,1)S(1)} %copy-done), channel_id=1, source_target_pairs={{0,3},{1,0},{2,1},{3,2},{4,7},{5,4},{6,5},{7,6},{8,11},{9,8},{10,9... | collective-permute-start | bytes 1892360 | tf_op jit(solution)/shard_map/ppermute | solution.py:19
  32.8 7.9 %collective-permute-start = (bf16[304,512]{1,0:T(8,128)(2,1)S(1)}, bf16[304,512]{1,0:T(8,128)(2,1)S(1)}, u32[]{:S(2)}, u32[]{:S(2)}) collective-permute-start(bf16[304,512]{1,0:T(8,128)(2,1)S(1)} %slice.72), channel_id=1, source_target_pairs={{0,4},{4,0},{1,5},{5,1},{2,6},{6,2},{3,7},{7,3},{8,12},{12,8},{9,1... | collective-permute-start | bytes 933896 | tf_op jit(solution)/shard_map/ppermute | solution.py:14
  40.7 9.9 %collective-permute-done = bf16[304,512]{1,0:T(8,128)(2,1)S(1)} collective-permute-done((bf16[304,512]{1,0:T(8,128)(2,1)S(1)}, bf16[304,512]{1,0:T(8,128)(2,1)S(1)}, u32[]{:S(2)}, u32[]{:S(2)}) %collective-permute-start) | collective-permute-done | bytes 311328 | tf_op jit(solution)/shard_map/ppermute | solution.py:14
  50.6 4.0 %collective-permute-done.2 = bf16[616,512]{1,0:T(8,128)(2,1)S(1)} collective-permute-done((bf16[616,512]{1,0:T(8,128)(2,1)S(1)}, bf16[616,512]{1,0:T(8,128)(2,1)S(1)}, u32[]{:S(2)}, u32[]{:S(2)}) %collective-permute-start.2) | collective-permute-done | bytes 630816 | tf_op jit(solution)/shard_map/ppermute | solution.py:19
  54.6 1.7 collective-permute-done.3
  56.3 1.6 broadcast_in_dim.23
  57.9 4.0 %all-to-all-start.1 = ((bf16[4,8,64,512]{3,2,1,0:T(8,128)(2,1)}), bf16[4,8,64,512]{3,2,1,0:T(8,128)(2,1)S(1)}, u32[]{:S(2)}, u32[]{:S(2)}) async-start(bf16[4,8,64,512]{3,2,1,0:T(8,128)(2,1)} %broadcast_in_dim.23), calls=%async_computation.1 | async-start | bytes 4194304 | tf_op jit(solution)/shard_map/all_to_all | solution.py:37
  62.7 7.9 %collective-permute-start.7 = (bf16[312,512]{1,0:T(8,128)(2,1)}, bf16[312,512]{1,0:T(8,128)(2,1)}, u32[]{:S(2)}, u32[]{:S(2)}) collective-permute-start(bf16[312,512]{1,0:T(8,128)(2,1)} %slice.73), channel_id=1, source_target_pairs={{0,4},{4,0},{1,5},{5,1},{2,6},{6,2},{3,7},{7,3},{8,12},{12,8},{9,1... | collective-permute-start | bytes 958472 | tf_op jit(solution)/shard_map/ppermute | solution.py:14
  70.7 5.2 %collective-permute-start.4 = (bf16[304,512]{1,0:T(8,128)(2,1)}, bf16[304,512]{1,0:T(8,128)(2,1)S(1)}, u32[]{:S(2)}, u32[]{:S(2)}) collective-permute-start(bf16[304,512]{1,0:T(8,128)(2,1)} %copy-done.16), channel_id=1, source_target_pairs={{0,1},{1,2},{2,3},{3,0},{4,5},{5,6},{6,7},{7,4},{8,9},{9,10},{10,1... | collective-permute-start | bytes 933896 | tf_op jit(solution)/shard_map/ppermute | solution.py:19
  75.9 3.2 %collective-permute-start.5 = (bf16[304,512]{1,0:T(8,128)(2,1)}, bf16[304,512]{1,0:T(8,128)(2,1)S(1)}, u32[]{:S(2)}, u32[]{:S(2)}) collective-permute-start(bf16[304,512]{1,0:T(8,128)(2,1)} %copy-done.16), channel_id=1, source_target_pairs={{0,2},{1,3},{2,0},{3,1},{4,6},{5,7},{6,4},{7,5},{8,10},{9,11},{10,... | collective-permute-start | bytes 933896 | tf_op jit(solution)/shard_map/ppermute | solution.py:19
  79.1 3.0 %collective-permute-start.6 = (bf16[304,512]{1,0:T(8,128)(2,1)}, bf16[304,512]{1,0:T(8,128)(2,1)S(1)}, u32[]{:S(2)}, u32[]{:S(2)}) collective-permute-start(bf16[304,512]{1,0:T(8,128)(2,1)} %copy-done.16), channel_id=1, source_target_pairs={{0,3},{1,0},{2,1},{3,2},{4,7},{5,4},{6,5},{7,6},{8,11},{9,8},{10,9... | collective-permute-start | bytes 933896 | tf_op jit(solution)/shard_map/ppermute | solution.py:19
  85.3 1.7 collective-permute-done.6
  87.0 1.1 copy-done.4
  88.1 1.5 copy.28
  89.6 32.2 %collective-permute-start.8 = (bf16[4,8,64,512]{3,2,0,1:T(8,128)(2,1)}, bf16[4,8,64,512]{3,2,0,1:T(8,128)(2,1)}, u32[]{:S(2)}, u32[]{:S(2)}) collective-permute-start(bf16[4,8,64,512]{3,2,0,1:T(8,128)(2,1)} %copy.28), channel_id=1, source_target_pairs={{0,8},{8,0},{1,9},{9,1},{2,10},{10,2},{3,11},{11,3},{4,12},{12,4},... | collective-permute-start | bytes 6291464 | tf_op jit(solution)/shard_map/ppermute | solution.py:14
  122.0 1.9 collective-permute-start.9
  124.0 1.9 collective-permute-start.10
  126.9 8.0 %all-to-all-start.2 = ((bf16[8,64,512]{2,1,0:T(8,128)(2,1)}), bf16[8,64,512]{2,1,0:T(8,128)(2,1)S(1)}, u32[]{:S(2)}, u32[]{:S(2)}) async-start(bf16[8,64,512]{2,1,0:T(8,128)(2,1)} %broadcast_in_dim.28), calls=%async_computation.2 | async-start | bytes 1048576 | tf_op jit(solution)/shard_map/all_to_all | solution.py:37
  134.9 3.0 %collective-permute-start.11 = (bf16[312,512]{1,0:T(8,128)(2,1)}, bf16[312,512]{1,0:T(8,128)(2,1)S(1)}, u32[]{:S(2)}, u32[]{:S(2)}) collective-permute-start(bf16[312,512]{1,0:T(8,128)(2,1)} %collective-permute-done.7), channel_id=1, source_target_pairs={{0,3},{1,0},{2,1},{3,2},{4,7},{5,4},{6,5},{7,6},{8,11},{9,8},{10,9... | collective-permute-start | bytes 958472 | tf_op jit(solution)/shard_map/ppermute | solution.py:19
  139.0 2.3 collective-permute-done.9
  141.4 1.0 constant_dynamic-update-slice_fusion.1
  142.4 2.8 %collective-permute-done.11 = bf16[312,512]{1,0:T(8,128)(2,1)S(1)} collective-permute-done((bf16[312,512]{1,0:T(8,128)(2,1)}, bf16[312,512]{1,0:T(8,128)(2,1)S(1)}, u32[]{:S(2)}, u32[]{:S(2)}) %collective-permute-start.11) | collective-permute-done | bytes 319520 | tf_op jit(solution)/shard_map/ppermute | solution.py:19
  145.3 1.9 select_bitcast_fusion.1
  147.5 1.3 copy-done.2
  149.0 1.5 fusion.14
  152.4 3.5 %all-to-all-done.2 = bf16[8,64,512]{2,1,0:T(8,128)(2,1)S(1)} async-done(((bf16[8,64,512]{2,1,0:T(8,128)(2,1)}), bf16[8,64,512]{2,1,0:T(8,128)(2,1)S(1)}, u32[]{:S(2)}, u32[]{:S(2)}) %all-to-all-start.2) | async-done | bytes 524320 | tf_op jit(solution)/shard_map/all_to_all | solution.py:37
  157.2 7.3 %all-to-all-start.3 = ((f32[8,1,616]{2,1,0:T(1,128)}), f32[8,1,616]{2,1,0:T(1,128)S(1)}, u32[]{:S(2)}, u32[]{:S(2)}) async-start(f32[8,1,616]{2,1,0:T(1,128)} %broadcast_in_dim.29), calls=%async_computation.3 | async-start | bytes 40960 | tf_op jit(solution)/shard_map/all_to_all | solution.py:37
  165.3 13.0 %all-to-all-done.3 = f32[8,1,616]{2,1,0:T(1,128)S(1)} async-done(((f32[8,1,616]{2,1,0:T(1,128)}), f32[8,1,616]{2,1,0:T(1,128)S(1)}, u32[]{:S(2)}, u32[]{:S(2)}) %all-to-all-start.3) | async-done | bytes 19744 | tf_op jit(solution)/shard_map/all_to_all | solution.py:37
  179.3 12.2 %all-gather.5.cloned.1.call-done = bf16[64,24,512]{2,1,0:T(8,128)(2,1)} async-done(((bf16[8,24,512]{2,1,0:T(8,128)(2,1)}), bf16[64,24,512]{2,1,0:T(8,128)(2,1)}) %all-gather.5.cloned.1.call-update) | async-done | bytes 1572880 | tf_op jit(solution)/shard_map/all_gather | solution.py:96
  191.5 1.5 slice_bitcast_fusion
  194.0 8.9 %all_to_all.36 = f32[4,8,1280]{2,1,0:T(8,128)S(1)} all-to-all(f32[4,8,1280]{2,1,0:T(8,128)S(1)} %broadcast_in_dim.30), channel_id=1, replica_groups=mesh['zl'=8,'x'=4,'c'=2,'zh'=2,'y'=4] {'y'}, dimensions={0} | all-to-all | bytes 327680 | tf_op jit(solution)/shard_map/all_to_all | solution.py:37
  202.9 12.5 %collective-permute-start.12 = (f32[8,1280]{1,0:T(8,128)S(1)}, f32[8,1280]{1,0:T(8,128)S(1)}, u32[]{:S(2)}, u32[]{:S(2)}) collective-permute-start(f32[8,1280]{1,0:T(8,128)S(1)} %reduce_sum.94), channel_id=1, source_target_pairs={{0,4},{4,0},{1,5},{5,1},{2,6},{6,2},{3,7},{7,3},{8,12},{12,8},{9,1... | collective-permute-start | bytes 122888 | tf_op jit(solution)/shard_map/ppermute | solution.py:14
  215.4 1.6 collective-permute-done.12
  218.2 9.1 %all-to-all-start.5 = ((f16[8,8,1408]{2,1,0:T(8,128)(2,1)}), f16[8,8,1408]{2,1,0:T(8,128)(2,1)S(1)}, u32[]{:S(2)}, u32[]{:S(2)}) async-start(f16[8,8,1408]{2,1,0:T(8,128)(2,1)} %broadcast_in_dim.31), calls=%async_computation.5 | async-start | bytes 360448 | tf_op jit(solution)/shard_map/all_to_all | solution.py:37
  229.0 9.2 %all-to-all-done.5 = f16[8,8,1408]{2,1,0:T(8,128)(2,1)S(1)} async-done(((f16[8,8,1408]{2,1,0:T(8,128)(2,1)}), f16[8,8,1408]{2,1,0:T(8,128)(2,1)S(1)}, u32[]{:S(2)}, u32[]{:S(2)}) %all-to-all-start.5) | async-done | bytes 180256 | tf_op jit(solution)/shard_map/all_to_all | solution.py:37
  239.1 3.7 %all-to-all-start.6 = ((f16[4,8,8,1408]{3,2,1,0:T(8,128)(2,1)}), f16[4,8,8,1408]{3,2,1,0:T(8,128)(2,1)S(1)}, u32[]{:S(2)}, u32[]{:S(2)}) async-start(f16[4,8,8,1408]{3,2,1,0:T(8,128)(2,1)} %broadcast_in_dim.32), calls=%async_computation.6 | async-start | bytes 1441792 | tf_op jit(solution)/shard_map/all_to_all | solution.py:37
  242.8 2.0 fusion.78
  244.9 2.3 fusion.28
  247.2 1.6 multiply_reduce_fusion.3
  250.8 7.7 %collective-permute-start.13 = (f16[4,8,8,1408]{3,2,1,0:T(8,128)(2,1)S(1)}, f16[4,8,8,1408]{3,2,1,0:T(8,128)(2,1)S(1)}, u32[]{:S(2)}, u32[]{:S(2)}) collective-permute-start(f16[4,8,8,1408]{3,2,1,0:T(8,128)(2,1)S(1)} %all-to-all-done.6), channel_id=1, source_target_pairs={{0,8},{8,0},{1,9},{9,1},{2,10},{10,2},{3,11},{11,3},{4,12},{12,4},... | collective-permute-start | bytes 2162696 | tf_op jit(solution)/shard_map/ppermute | solution.py:14
  258.6 1.2 fusion.34
  260.7 2.4 fusion.47
  263.4 1.9 collective-permute-start.14
  265.3 1.2 fusion.40
  (127 shorter events, 20.0 us)
Async XLA Ops:
  7.2 14.8 %copy-start = (bf16[616,512]{1,0:T(8,128)(2,1)S(1)}, bf16[616,512]{1,0:T(8,128)(2,1)}, u32[]{:S(2)}) copy-start(bf16[616,512]{1,0:T(8,128)(2,1)} %param.9) | copy-start | bytes 1892356
  8.9 47.4 %all-to-all-start = ((bf16[8,64,512]{2,1,0:T(8,128)(2,1)}), bf16[8,64,512]{2,1,0:T(8,128)(2,1)S(1)}, u32[]{:S(2)}, u32[]{:S(2)}) async-start(bf16[8,64,512]{2,1,0:T(8,128)(2,1)} %broadcast_in_dim.22), calls=%async_computation | async-start | bytes 1048576 | tf_op jit(solution)/shard_map/all_to_all | solution.py:37
  22.0 28.6 %collective-permute-start.1 = (bf16[616,512]{1,0:T(8,128)(2,1)S(1)}, bf16[616,512]{1,0:T(8,128)(2,1)S(1)}, u32[]{:S(2)}, u32[]{:S(2)}) collective-permute-start(bf16[616,512]{1,0:T(8,128)(2,1)S(1)} %copy-done), channel_id=1, source_target_pairs={{0,1},{1,2},{2,3},{3,0},{4,5},{5,6},{6,7},{7,4},{8,9},{9,10},{10,1... | collective-permute-start | bytes 1892360 | tf_op jit(solution)/shard_map/ppermute | solution.py:19
  25.2 29.4 %collective-permute-start.2 = (bf16[616,512]{1,0:T(8,128)(2,1)S(1)}, bf16[616,512]{1,0:T(8,128)(2,1)S(1)}, u32[]{:S(2)}, u32[]{:S(2)}) collective-permute-start(bf16[616,512]{1,0:T(8,128)(2,1)S(1)} %copy-done), channel_id=1, source_target_pairs={{0,2},{1,3},{2,0},{3,1},{4,6},{5,7},{6,4},{7,5},{8,10},{9,11},{10,... | collective-permute-start | bytes 1892360 | tf_op jit(solution)/shard_map/ppermute | solution.py:19
  29.7 26.5 %collective-permute-start.3 = (bf16[616,512]{1,0:T(8,128)(2,1)S(1)}, bf16[616,512]{1,0:T(8,128)(2,1)S(1)}, u32[]{:S(2)}, u32[]{:S(2)}) collective-permute-start(bf16[616,512]{1,0:T(8,128)(2,1)S(1)} %copy-done), channel_id=1, source_target_pairs={{0,3},{1,0},{2,1},{3,2},{4,7},{5,4},{6,5},{7,6},{8,11},{9,8},{10,9... | collective-permute-start | bytes 1892360 | tf_op jit(solution)/shard_map/ppermute | solution.py:19
  32.8 17.8 %collective-permute-start = (bf16[304,512]{1,0:T(8,128)(2,1)S(1)}, bf16[304,512]{1,0:T(8,128)(2,1)S(1)}, u32[]{:S(2)}, u32[]{:S(2)}) collective-permute-start(bf16[304,512]{1,0:T(8,128)(2,1)S(1)} %slice.72), channel_id=1, source_target_pairs={{0,4},{4,0},{1,5},{5,1},{2,6},{6,2},{3,7},{7,3},{8,12},{12,8},{9,1... | collective-permute-start | bytes 933896 | tf_op jit(solution)/shard_map/ppermute | solution.py:14
  50.6 4.0 %copy-start.16 = (bf16[304,512]{1,0:T(8,128)(2,1)}, bf16[304,512]{1,0:T(8,128)(2,1)S(1)}, u32[]{:S(2)}) copy-start(bf16[304,512]{1,0:T(8,128)(2,1)S(1)} %collective-permute-done) | copy-start | bytes 933892
  54.6 3.3 %copy-start.6 = (bf16[616,512]{1,0:T(8,128)(2,1)}, bf16[616,512]{1,0:T(8,128)(2,1)S(1)}, u32[]{:S(2)}) copy-start(bf16[616,512]{1,0:T(8,128)(2,1)S(1)} %collective-permute-done.2) | copy-start | bytes 1892356
  56.3 1.6 copy-start.8
  57.9 30.2 %all-to-all-start.1 = ((bf16[4,8,64,512]{3,2,1,0:T(8,128)(2,1)}), bf16[4,8,64,512]{3,2,1,0:T(8,128)(2,1)S(1)}, u32[]{:S(2)}, u32[]{:S(2)}) async-start(bf16[4,8,64,512]{3,2,1,0:T(8,128)(2,1)} %broadcast_in_dim.23), calls=%async_computation.1 | async-start | bytes 4194304 | tf_op jit(solution)/shard_map/all_to_all | solution.py:37
  62.7 25.4 %collective-permute-start.7 = (bf16[312,512]{1,0:T(8,128)(2,1)}, bf16[312,512]{1,0:T(8,128)(2,1)}, u32[]{:S(2)}, u32[]{:S(2)}) collective-permute-start(bf16[312,512]{1,0:T(8,128)(2,1)} %slice.73), channel_id=1, source_target_pairs={{0,4},{4,0},{1,5},{5,1},{2,6},{6,2},{3,7},{7,3},{8,12},{12,8},{9,1... | collective-permute-start | bytes 958472 | tf_op jit(solution)/shard_map/ppermute | solution.py:14
  70.7 14.0 %collective-permute-start.4 = (bf16[304,512]{1,0:T(8,128)(2,1)}, bf16[304,512]{1,0:T(8,128)(2,1)S(1)}, u32[]{:S(2)}, u32[]{:S(2)}) collective-permute-start(bf16[304,512]{1,0:T(8,128)(2,1)} %copy-done.16), channel_id=1, source_target_pairs={{0,1},{1,2},{2,3},{3,0},{4,5},{5,6},{6,7},{7,4},{8,9},{9,10},{10,1... | collective-permute-start | bytes 933896 | tf_op jit(solution)/shard_map/ppermute | solution.py:19
  75.9 9.4 %collective-permute-start.5 = (bf16[304,512]{1,0:T(8,128)(2,1)}, bf16[304,512]{1,0:T(8,128)(2,1)S(1)}, u32[]{:S(2)}, u32[]{:S(2)}) collective-permute-start(bf16[304,512]{1,0:T(8,128)(2,1)} %copy-done.16), channel_id=1, source_target_pairs={{0,2},{1,3},{2,0},{3,1},{4,6},{5,7},{6,4},{7,5},{8,10},{9,11},{10,... | collective-permute-start | bytes 933896 | tf_op jit(solution)/shard_map/ppermute | solution.py:19
  79.1 7.9 %collective-permute-start.6 = (bf16[304,512]{1,0:T(8,128)(2,1)}, bf16[304,512]{1,0:T(8,128)(2,1)S(1)}, u32[]{:S(2)}, u32[]{:S(2)}) collective-permute-start(bf16[304,512]{1,0:T(8,128)(2,1)} %copy-done.16), channel_id=1, source_target_pairs={{0,3},{1,0},{2,1},{3,2},{4,7},{5,4},{6,5},{7,6},{8,11},{9,8},{10,9... | collective-permute-start | bytes 933896 | tf_op jit(solution)/shard_map/ppermute | solution.py:19
  82.4 1.1 copy-start.7
  82.5 1.2 copy-start.9
  83.7 1.0 copy-start.17
  83.8 1.5 copy-start.1
  87.0 1.1 copy-start.4
  88.1 33.7 %copy-start.3 = (f32[8,1280]{1,0:T(8,128)S(1)}, f32[8,1280]{1,0:T(8,128)}, u32[]{:S(2)}) copy-start(f32[8,1280]{1,0:T(8,128)} %param.15) | copy-start | bytes 122884
  88.1 37.9 %copy-start.18 = (bf16[512,20]{0,1:T(8,128)(2,1)S(1)}, bf16[512,20]{0,1:T(8,128)(2,1)}, u32[]{:S(2)}) copy-start(bf16[512,20]{0,1:T(8,128)(2,1)} %param.14) | copy-start | bytes 61444
  89.6 55.6 %collective-permute-start.8 = (bf16[4,8,64,512]{3,2,0,1:T(8,128)(2,1)}, bf16[4,8,64,512]{3,2,0,1:T(8,128)(2,1)}, u32[]{:S(2)}, u32[]{:S(2)}) collective-permute-start(bf16[4,8,64,512]{3,2,0,1:T(8,128)(2,1)} %copy.28), channel_id=1, source_target_pairs={{0,8},{8,0},{1,9},{9,1},{2,10},{10,2},{3,11},{11,3},{4,12},{12,4},... | collective-permute-start | bytes 6291464 | tf_op jit(solution)/shard_map/ppermute | solution.py:14
  122.0 19.3 %collective-permute-start.9 = (bf16[312,512]{1,0:T(8,128)(2,1)}, bf16[312,512]{1,0:T(8,128)(2,1)S(1)}, u32[]{:S(2)}, u32[]{:S(2)}) collective-permute-start(bf16[312,512]{1,0:T(8,128)(2,1)} %collective-permute-done.7), channel_id=1, source_target_pairs={{0,1},{1,2},{2,3},{3,0},{4,5},{5,6},{6,7},{7,4},{8,9},{9,10},{10,1... | collective-permute-start | bytes 958472 | tf_op jit(solution)/shard_map/ppermute | solution.py:19
  124.0 17.4 %collective-permute-start.10 = (bf16[312,512]{1,0:T(8,128)(2,1)}, bf16[312,512]{1,0:T(8,128)(2,1)}, u32[]{:S(2)}, u32[]{:S(2)}) collective-permute-start(bf16[312,512]{1,0:T(8,128)(2,1)} %collective-permute-done.7), channel_id=1, source_target_pairs={{0,2},{1,3},{2,0},{3,1},{4,6},{5,7},{6,4},{7,5},{8,10},{9,11},{10,... | collective-permute-start | bytes 958472 | tf_op jit(solution)/shard_map/ppermute | solution.py:19
  126.9 29.0 %all-to-all-start.2 = ((bf16[8,64,512]{2,1,0:T(8,128)(2,1)}), bf16[8,64,512]{2,1,0:T(8,128)(2,1)S(1)}, u32[]{:S(2)}, u32[]{:S(2)}) async-start(bf16[8,64,512]{2,1,0:T(8,128)(2,1)} %broadcast_in_dim.28), calls=%async_computation.2 | async-start | bytes 1048576 | tf_op jit(solution)/shard_map/all_to_all | solution.py:37
  134.8 56.7 %all-gather.5.cloned.1.call-start = ((), (), s32[]{:S(2)}) async-start(), calls=%async_computation.7 | async-start | bytes 1769472 | tf_op jit(solution)/shard_map/all_gather | solution.py:96
  134.9 10.3 %collective-permute-start.11 = (bf16[312,512]{1,0:T(8,128)(2,1)}, bf16[312,512]{1,0:T(8,128)(2,1)S(1)}, u32[]{:S(2)}, u32[]{:S(2)}) collective-permute-start(bf16[312,512]{1,0:T(8,128)(2,1)} %collective-permute-done.7), channel_id=1, source_target_pairs={{0,3},{1,0},{2,1},{3,2},{4,7},{5,4},{6,5},{7,6},{8,11},{9,8},{10,9... | collective-permute-start | bytes 958472 | tf_op jit(solution)/shard_map/ppermute | solution.py:19
  147.1 1.7 copy-start.2
  147.1 1.8 copy-start.21
  149.0 1.5 copy-start.5
  152.3 26.0 %copy-start.20 = (s32[8]{0:T(128)S(1)}, s32[8]{0:T(128)}, u32[]{:S(2)}) copy-start(s32[8]{0:T(128)} %param.13) | copy-start | bytes 100
  157.2 21.1 %all-to-all-start.3 = ((f32[8,1,616]{2,1,0:T(1,128)}), f32[8,1,616]{2,1,0:T(1,128)S(1)}, u32[]{:S(2)}, u32[]{:S(2)}) async-start(f32[8,1,616]{2,1,0:T(1,128)} %broadcast_in_dim.29), calls=%async_computation.3 | async-start | bytes 40960 | tf_op jit(solution)/shard_map/all_to_all | solution.py:37
  164.5 78.3 %all-gather.7.cloned.1.call-start = ((), (), s32[]{:S(2)}) async-start(), calls=%async_computation.8 | async-start | bytes 2949120 | tf_op jit(solution)/shard_map/all_gather | solution.py:100
  178.3 0.7 copy-start.19
  202.9 14.1 %collective-permute-start.12 = (f32[8,1280]{1,0:T(8,128)S(1)}, f32[8,1280]{1,0:T(8,128)S(1)}, u32[]{:S(2)}, u32[]{:S(2)}) collective-permute-start(f32[8,1280]{1,0:T(8,128)S(1)} %reduce_sum.94), channel_id=1, source_target_pairs={{0,4},{4,0},{1,5},{5,1},{2,6},{6,2},{3,7},{7,3},{8,12},{12,8},{9,1... | collective-permute-start | bytes 122888 | tf_op jit(solution)/shard_map/ppermute | solution.py:14
  218.2 20.0 %all-to-all-start.5 = ((f16[8,8,1408]{2,1,0:T(8,128)(2,1)}), f16[8,8,1408]{2,1,0:T(8,128)(2,1)S(1)}, u32[]{:S(2)}, u32[]{:S(2)}) async-start(f16[8,8,1408]{2,1,0:T(8,128)(2,1)} %broadcast_in_dim.31), calls=%async_computation.5 | async-start | bytes 360448 | tf_op jit(solution)/shard_map/all_to_all | solution.py:37
  239.1 11.4 %all-to-all-start.6 = ((f16[4,8,8,1408]{3,2,1,0:T(8,128)(2,1)}), f16[4,8,8,1408]{3,2,1,0:T(8,128)(2,1)S(1)}, u32[]{:S(2)}, u32[]{:S(2)}) async-start(f16[4,8,8,1408]{3,2,1,0:T(8,128)(2,1)} %broadcast_in_dim.32), calls=%async_computation.6 | async-start | bytes 1441792 | tf_op jit(solution)/shard_map/all_to_all | solution.py:37
  244.8 2.4 copy-start.10
  244.8 2.4 copy-start.12
  244.8 2.4 copy-start.14
  250.7 9.9 %copy-start.11 = (bf16[8,8,8,512]{3,2,1,0:T(8,128)(2,1)S(1)}, bf16[8,8,8,512]{3,2,1,0:T(8,128)(2,1)}, u32[]{:S(2)}) copy-start(bf16[8,8,8,512]{3,2,1,0:T(8,128)(2,1)} %copy-done.10) | copy-start | bytes 1572868
  250.7 9.9 %copy-start.13 = (bf16[8,8,8,512]{3,2,1,0:T(8,128)(2,1)S(1)}, bf16[8,8,8,512]{3,2,1,0:T(8,128)(2,1)}, u32[]{:S(2)}) copy-start(bf16[8,8,8,512]{3,2,1,0:T(8,128)(2,1)} %copy-done.12) | copy-start | bytes 1572868
  250.7 9.9 %copy-start.15 = (bf16[8,8,8,512]{3,2,1,0:T(8,128)(2,1)S(1)}, bf16[8,8,8,512]{3,2,1,0:T(8,128)(2,1)}, u32[]{:S(2)}) copy-start(bf16[8,8,8,512]{3,2,1,0:T(8,128)(2,1)} %copy-done.14) | copy-start | bytes 1572868
  250.8 12.3 %collective-permute-start.13 = (f16[4,8,8,1408]{3,2,1,0:T(8,128)(2,1)S(1)}, f16[4,8,8,1408]{3,2,1,0:T(8,128)(2,1)S(1)}, u32[]{:S(2)}, u32[]{:S(2)}) collective-permute-start(f16[4,8,8,1408]{3,2,1,0:T(8,128)(2,1)S(1)} %all-to-all-done.6), channel_id=1, source_target_pairs={{0,8},{8,0},{1,9},{9,1},{2,10},{10,2},{3,11},{11,3},{4,12},{12,4},... | collective-permute-start | bytes 2162696 | tf_op jit(solution)/shard_map/ppermute | solution.py:14
  263.4 4.8 %collective-permute-start.14 = (f32[]{:T(128)}, f32[]{:T(128)}, u32[]{:S(2)}, u32[]{:S(2)}) collective-permute-start(f32[]{:T(128)} %fusion.47), channel_id=1, source_target_pairs={{0,8},{8,0},{1,9},{9,1},{2,10},{10,2},{3,11},{11,3},{4,12},{12,4},... | collective-permute-start | bytes 20 | tf_op jit(solution)/shard_map/ppermute | solution.py:14
Sparse Core Ops, SparseCore 0:
  156.7 34.7 all-gather.4
  193.6 34.0 all-gather.6

commit v5 on v4

--- a/solution.py
+++ b/solution.py
@@ -35,6 +35,11 @@
     for a in axes:
         n *= SIZES[a]
     return lax.all_to_all(jnp.broadcast_to(v[None], (n,) + v.shape), axes, 0, 0)
+
+
+def power_of(v, axis):
+    largest = jnp.max(jnp.abs(v), axis=axis, keepdims=True)
+    return jnp.floor(jnp.log2(jnp.clip(largest, 1e-36, 1.0)))
 
 
 def unscaled(message):
@@ -75,10 +80,12 @@
     rows, far_a, far_b, near = lax.optimization_barrier((rows, in_order(far_a, y), far_b, near))
     other = swap(rows, "c")
     far_b = around_y(far_b)
-    high, low = split(picture, 2)
-    packed = [high[:, :512], high[:, 512:1024], low[:, :512], low[:, 512:1024]]
-    packed += [jnp.concatenate([high[:, 1024:], low[:, 1024:]], axis=1)]
-    packed = jnp.concatenate(packed + [adapter.T, jnp.zeros((4, 512), BF16)], axis=0)
+    power, block_power = power_of(picture, 1), power_of(adapter.astype(F32), None)
+    scaled = picture * jnp.exp2(-power)
+    tail = jnp.concatenate([scaled[:, 1024:], jnp.broadcast_to(power, (captions, 256))], axis=1)
+    columns = adapter.T.astype(F32) * jnp.exp2(-block_power)
+    packed = [scaled[:, :512], scaled[:, 512:1024], tail, columns, jnp.broadcast_to(block_power, (4, 512))]
+    packed = jnp.concatenate(packed, axis=0).astype(F16)
     packed = gather(packed, ("zl",))
     first, second = jnp.where(c == 0, rows, other), jnp.where(c == 0, other, rows)
     both = jnp.stack([first, second], axis=2).transpose(1, 0, 2, 3, 4)
@@ -93,15 +100,16 @@
 
     squares = jnp.sum(hidden * hidden, axis=1)
     squares, packed = lax.optimization_barrier((squares, packed))
-    full_adapter = lax.all_gather(packed[:, 40:], ("x", "c"))
-    full_adapter = full_adapter[:, :, :20].transpose(1, 0, 2, 3).reshape(1280, 512)
+    full_adapter = lax.all_gather(packed[:, 24:], ("x", "c"))
+    full_adapter = full_adapter.astype(F32)
+    full_adapter = (full_adapter[:, :, :20] * jnp.exp2(full_adapter[:, :, 20:21])).astype(BF16)
+    full_adapter = full_adapter.transpose(1, 0, 2, 3).reshape(1280, 512)
     squares = jnp.sum(gather(squares, TP), axis=0)
-    squares, packed = lax.optimization_barrier((squares, packed[:, :40]))
+    squares, packed = lax.optimization_barrier((squares, packed[:, :24]))
     packed = lax.all_gather(packed, ("x", "c"))
-    parts = [packed[:, :, 8 * i : 8 * i + 8].reshape(512, 512) for i in range(5)]
-    high = jnp.concatenate([parts[0], parts[1], parts[4][:, :256]], axis=1)
-    low = jnp.concatenate([parts[2], parts[3], parts[4][:, 256:]], axis=1)
-    every_image = high.astype(F32) + low.astype(F32)
+    parts = [packed[:, :, 8 * i : 8 * i + 8].reshape(512, 512).astype(F32) for i in range(3)]
+    every_image = jnp.concatenate([parts[0], parts[1], parts[2][:, :256]], axis=1)
+    every_image = every_image * jnp.exp2(parts[2][:, 256:257])
     normed = hidden * lax.rsqrt(squares / 4096 + 1e-05)[:, None] * norm_gain[None, :]
     normed = normed.reshape(captions, seq_len, 512)
     positions = jnp.arange(seq_len, dtype=jnp.int32)
@@ -116,8 +124,7 @@
     text_norm = jnp.sqrt(jnp.sum(raw_text * raw_text, axis=1, keepdims=True) + 1e-06)
     text_unit = raw_text / text_norm
 
-    largest = jnp.max(jnp.abs(text_unit), axis=1, keepdims=True)
-    power = jnp.floor(jnp.log2(jnp.clip(largest, 1e-36, 1.0)))
+    power = power_of(text_unit, 1)
     message = jnp.concatenate([text_unit * jnp.exp2(-power), jnp.broadcast_to(power, (captions, 128))], axis=1)
     texts = gather(message.astype(F16), ("zl",))
     texts, text_unit = lax.optimization_barrier((texts, text_unit))

time: 279 us -> 291 us (1.043)
  blocking collectives: 8.91 us -> 30.2 us
  waiting for transfers between devices: 63.1 us -> 47.6 us
  between operations: 18.6 us -> 5.9 us
  other arithmetic: 4.89 us -> 14 us
  starting transfers between devices: 144 us -> 151 us
    all_gather x0 -> x2, blocking collectives: none -> 30.2 us  [the longest x1 15.4 us: local(): full_adapter = lax.all_gather(packed[:, 24:], ('x', 'c'))]
    all_gather x2 -> x0, waiting for transfers between devices: 12.2 us -> none  [the longest x1 12.2 us: local(): full_adapter = lax.all_gather(packed[:, 40:], ('x', 'c'))]
    all_to_all x1 -> x0, blocking collectives: 8.91 us -> none  [gather(): return lax.all_to_all(jnp.broadcast_to(v[None], (n,) + v.shape), axes, 0, 0)]
    all_to_all x6 -> x7, waiting for transfers between devices: 26.5 us -> 20.1 us  [gather(): return lax.all_to_all(jnp.broadcast_to(v[None], (n,) + v.shape), axes, 0, 0)]
    all_to_all x6 -> x7, starting transfers between devices: 45.1 us -> 50.4 us  [gather(): return lax.all_to_all(jnp.broadcast_to(v[None], (n,) + v.shape), axes, 0, 0)]
    ppermute x9, waiting for transfers between devices: 12.9 us -> 17.6 us  [shift(): return lax.ppermute(v, axis, [(i, (i + by) % n) for i in range(n)])]
    ppermute x9, starting transfers between devices: 28.9 us -> 32.9 us  [shift(): return lax.ppermute(v, axis, [(i, (i + by) % n) for i in range(n)])]
    convert_element_type x0 -> x4, other arithmetic: none -> 3.05 us  [the longest x3 2.65 us: local(): packed[:, :, 8 * i:8 * i + 8].reshape(512, 512).astype(F32)]
  transfers between devices with their start and end apart: 23 -> 22, of which waited for: 13 -> 11; matrix products, arithmetic and copies ran while one was open for 11% -> 10% of each run, Pallas kernels for 0% -> 0%
where the time goes in v5:
time: 291 us; the launch traced here: 290 us
  starting transfers between devices  151 us (52%)
  waiting for transfers between devices  47.6 us (16%)
  blocking collectives  30.2 us (10%)
  local copies, waits for them, and re-layouts  23.5 us (8%)
  matrix products  17.7 us (6%)
  other arithmetic  14 us (5%)
  between operations  5.9 us (2%)
    ppermute x6, starting transfers between devices, swap(): return lax.ppermute(v, axis, [(0, 1), (1, 0)])  67.5 us
    all_to_all x7, starting transfers between devices, gather(): return lax.all_to_all(jnp.broadcast_to(v[None], (n,) + v.shape), axes, 0, 0)  50.4 us
    ppermute x9, starting transfers between devices, shift(): return lax.ppermute(v, axis, [(i, (i + by) % n) for i in range(n)])  32.9 us
    all_to_all x7, waiting for transfers between devices, gather(): return lax.all_to_all(jnp.broadcast_to(v[None], (n,) + v.shape), axes, 0, 0)  20.1 us
    ppermute x9, waiting for transfers between devices, shift(): return lax.ppermute(v, axis, [(i, (i + by) % n) for i in range(n)])  17.6 us
    all_gather x1, blocking collectives, local(): full_adapter = lax.all_gather(packed[:, 24:], ('x', 'c'))  15.4 us
    all_gather x1, blocking collectives, local(): packed = lax.all_gather(packed, ('x', 'c'))  14.8 us
    ppermute x6, waiting for transfers between devices, swap(): return lax.ppermute(v, axis, [(0, 1), (1, 0)])  9.89 us
  transfers between devices with their start and end apart: 22, of which 11 were waited for; matrix products, arithmetic and copies ran while one was open for 10% of the time, Pallas kernels for 0%

profile of v5, /device:TPU:1, one launch (start us, length us, event | category | flops | bytes accessed | tf_op | source)
XLA Modules:
  0.0 289.6 jit_solution(8660693152227630586)
XLA Ops:
  0.6 1.8 broadcast_in_dim.26
  2.4 13.1 %all-to-all-start = ((bf16[8,64,512]{2,1,0:T(8,128)(2,1)}), bf16[8,64,512]{2,1,0:T(8,128)(2,1)S(1)}, u32[]{:S(2)}, u32[]{:S(2)}) async-start(bf16[8,64,512]{2,1,0:T(8,128)(2,1)} %broadcast_in_dim.26), calls=%async_computation | async-start | bytes 1048576 | tf_op jit(solution)/shard_map/all_to_all | solution.py:37
  15.5 3.2 %collective-permute-start.1 = (bf16[616,512]{1,0:T(8,128)(2,1)S(1)}, bf16[616,512]{1,0:T(8,128)(2,1)S(1)}, u32[]{:S(2)}, u32[]{:S(2)}) collective-permute-start(bf16[616,512]{1,0:T(8,128)(2,1)S(1)} %copy-done), channel_id=1, source_target_pairs={{0,1},{1,2},{2,3},{3,0},{4,5},{5,6},{6,7},{7,4},{8,9},{9,10},{10,1... | collective-permute-start | bytes 1892360 | tf_op jit(solution)/shard_map/ppermute | solution.py:19
  18.7 4.5 %collective-permute-start.2 = (bf16[616,512]{1,0:T(8,128)(2,1)S(1)}, bf16[616,512]{1,0:T(8,128)(2,1)S(1)}, u32[]{:S(2)}, u32[]{:S(2)}) collective-permute-start(bf16[616,512]{1,0:T(8,128)(2,1)S(1)} %copy-done), channel_id=1, source_target_pairs={{0,2},{1,3},{2,0},{3,1},{4,6},{5,7},{6,4},{7,5},{8,10},{9,11},{10,... | collective-permute-start | bytes 1892360 | tf_op jit(solution)/shard_map/ppermute | solution.py:19
  23.2 3.0 %collective-permute-start.3 = (bf16[616,512]{1,0:T(8,128)(2,1)S(1)}, bf16[616,512]{1,0:T(8,128)(2,1)S(1)}, u32[]{:S(2)}, u32[]{:S(2)}) collective-permute-start(bf16[616,512]{1,0:T(8,128)(2,1)S(1)} %copy-done), channel_id=1, source_target_pairs={{0,3},{1,0},{2,1},{3,2},{4,7},{5,4},{6,5},{7,6},{8,11},{9,8},{10,9... | collective-permute-start | bytes 1892360 | tf_op jit(solution)/shard_map/ppermute | solution.py:19
  26.2 7.9 %collective-permute-start = (bf16[304,512]{1,0:T(8,128)(2,1)S(1)}, bf16[304,512]{1,0:T(8,128)(2,1)S(1)}, u32[]{:S(2)}, u32[]{:S(2)}) collective-permute-start(bf16[304,512]{1,0:T(8,128)(2,1)S(1)} %slice.63), channel_id=1, source_target_pairs={{0,4},{4,0},{1,5},{5,1},{2,6},{6,2},{3,7},{7,3},{8,12},{12,8},{9,1... | collective-permute-start | bytes 933896 | tf_op jit(solution)/shard_map/ppermute | solution.py:14
  34.2 9.9 %collective-permute-done = bf16[304,512]{1,0:T(8,128)(2,1)S(1)} collective-permute-done((bf16[304,512]{1,0:T(8,128)(2,1)S(1)}, bf16[304,512]{1,0:T(8,128)(2,1)S(1)}, u32[]{:S(2)}, u32[]{:S(2)}) %collective-permute-start) | collective-permute-done | bytes 311328 | tf_op jit(solution)/shard_map/ppermute | solution.py:14
  44.1 4.0 %collective-permute-done.2 = bf16[616,512]{1,0:T(8,128)(2,1)S(1)} collective-permute-done((bf16[616,512]{1,0:T(8,128)(2,1)S(1)}, bf16[616,512]{1,0:T(8,128)(2,1)S(1)}, u32[]{:S(2)}, u32[]{:S(2)}) %collective-permute-start.2) | collective-permute-done | bytes 630816 | tf_op jit(solution)/shard_map/ppermute | solution.py:19
  48.1 1.7 collective-permute-done.3
  49.8 1.6 broadcast_in_dim.27
  51.4 4.2 %all-to-all-start.1 = ((bf16[4,8,64,512]{3,2,1,0:T(8,128)(2,1)}), bf16[4,8,64,512]{3,2,1,0:T(8,128)(2,1)S(1)}, u32[]{:S(2)}, u32[]{:S(2)}) async-start(bf16[4,8,64,512]{3,2,1,0:T(8,128)(2,1)} %broadcast_in_dim.27), calls=%async_computation.1 | async-start | bytes 4194304 | tf_op jit(solution)/shard_map/all_to_all | solution.py:37
  56.3 7.9 %collective-permute-start.7 = (bf16[312,512]{1,0:T(8,128)(2,1)}, bf16[312,512]{1,0:T(8,128)(2,1)}, u32[]{:S(2)}, u32[]{:S(2)}) collective-permute-start(bf16[312,512]{1,0:T(8,128)(2,1)} %slice.64), channel_id=1, source_target_pairs={{0,4},{4,0},{1,5},{5,1},{2,6},{6,2},{3,7},{7,3},{8,12},{12,8},{9,1... | collective-permute-start | bytes 958472 | tf_op jit(solution)/shard_map/ppermute | solution.py:14
  66.0 5.2 %collective-permute-start.4 = (bf16[304,512]{1,0:T(8,128)(2,1)}, bf16[304,512]{1,0:T(8,128)(2,1)S(1)}, u32[]{:S(2)}, u32[]{:S(2)}) collective-permute-start(bf16[304,512]{1,0:T(8,128)(2,1)} %copy-done.17), channel_id=1, source_target_pairs={{0,1},{1,2},{2,3},{3,0},{4,5},{5,6},{6,7},{7,4},{8,9},{9,10},{10,1... | collective-permute-start | bytes 933896 | tf_op jit(solution)/shard_map/ppermute | solution.py:19
  71.2 3.2 %collective-permute-start.5 = (bf16[304,512]{1,0:T(8,128)(2,1)}, bf16[304,512]{1,0:T(8,128)(2,1)S(1)}, u32[]{:S(2)}, u32[]{:S(2)}) collective-permute-start(bf16[304,512]{1,0:T(8,128)(2,1)} %copy-done.17), channel_id=1, source_target_pairs={{0,2},{1,3},{2,0},{3,1},{4,6},{5,7},{6,4},{7,5},{8,10},{9,11},{10,... | collective-permute-start | bytes 933896 | tf_op jit(solution)/shard_map/ppermute | solution.py:19
  74.4 3.0 %collective-permute-start.6 = (bf16[304,512]{1,0:T(8,128)(2,1)}, bf16[304,512]{1,0:T(8,128)(2,1)S(1)}, u32[]{:S(2)}, u32[]{:S(2)}) collective-permute-start(bf16[304,512]{1,0:T(8,128)(2,1)} %copy-done.17), channel_id=1, source_target_pairs={{0,3},{1,0},{2,1},{3,2},{4,7},{5,4},{6,5},{7,6},{8,11},{9,8},{10,9... | collective-permute-start | bytes 933896 | tf_op jit(solution)/shard_map/ppermute | solution.py:19
  80.6 2.0 collective-permute-done.6
  83.7 1.5 copy.30
  85.2 30.4 %collective-permute-start.8 = (bf16[4,8,64,512]{3,2,0,1:T(8,128)(2,1)}, bf16[4,8,64,512]{3,2,0,1:T(8,128)(2,1)}, u32[]{:S(2)}, u32[]{:S(2)}) collective-permute-start(bf16[4,8,64,512]{3,2,0,1:T(8,128)(2,1)} %copy.30), channel_id=1, source_target_pairs={{0,8},{8,0},{1,9},{9,1},{2,10},{10,2},{3,11},{11,3},{4,12},{12,4},... | collective-permute-start | bytes 6291464 | tf_op jit(solution)/shard_map/ppermute | solution.py:14
  116.8 4.0 %all-to-all-start.2 = ((f16[8,48,512]{2,1,0:T(8,128)(2,1)}), f16[8,48,512]{2,1,0:T(8,128)(2,1)S(1)}, u32[]{:S(2)}, u32[]{:S(2)}) async-start(f16[8,48,512]{2,1,0:T(8,128)(2,1)} %broadcast_in_dim.34), calls=%async_computation.2 | async-start | bytes 786432 | tf_op jit(solution)/shard_map/all_to_all | solution.py:37
  122.3 4.4 %collective-permute-start.9 = (bf16[312,512]{1,0:T(8,128)(2,1)}, bf16[312,512]{1,0:T(8,128)(2,1)S(1)}, u32[]{:S(2)}, u32[]{:S(2)}) collective-permute-start(bf16[312,512]{1,0:T(8,128)(2,1)} %collective-permute-done.7), channel_id=1, source_target_pairs={{0,1},{1,2},{2,3},{3,0},{4,5},{5,6},{6,7},{7,4},{8,9},{9,10},{10,1... | collective-permute-start | bytes 958472 | tf_op jit(solution)/shard_map/ppermute | solution.py:19
  126.7 3.4 %collective-permute-start.10 = (bf16[312,512]{1,0:T(8,128)(2,1)}, bf16[312,512]{1,0:T(8,128)(2,1)S(1)}, u32[]{:S(2)}, u32[]{:S(2)}) collective-permute-start(bf16[312,512]{1,0:T(8,128)(2,1)} %collective-permute-done.7), channel_id=1, source_target_pairs={{0,2},{1,3},{2,0},{3,1},{4,6},{5,7},{6,4},{7,5},{8,10},{9,11},{10,... | collective-permute-start | bytes 958472 | tf_op jit(solution)/shard_map/ppermute | solution.py:19
  130.1 3.0 %collective-permute-start.11 = (bf16[312,512]{1,0:T(8,128)(2,1)}, bf16[312,512]{1,0:T(8,128)(2,1)S(1)}, u32[]{:S(2)}, u32[]{:S(2)}) collective-permute-start(bf16[312,512]{1,0:T(8,128)(2,1)} %collective-permute-done.7), channel_id=1, source_target_pairs={{0,3},{1,0},{2,1},{3,2},{4,7},{5,4},{6,5},{7,6},{8,11},{9,8},{10,9... | collective-permute-start | bytes 958472 | tf_op jit(solution)/shard_map/ppermute | solution.py:19
  134.8 7.8 %collective-permute-done.10 = bf16[312,512]{1,0:T(8,128)(2,1)S(1)} collective-permute-done((bf16[312,512]{1,0:T(8,128)(2,1)}, bf16[312,512]{1,0:T(8,128)(2,1)S(1)}, u32[]{:S(2)}, u32[]{:S(2)}) %collective-permute-start.10) | collective-permute-done | bytes 319520 | tf_op jit(solution)/shard_map/ppermute | solution.py:19
  143.9 1.9 select_bitcast_fusion.1
  146.1 1.3 copy-done.2
  147.6 1.5 fusion.12
  152.6 10.8 %all-to-all-start.3 = ((f32[8,1,616]{2,1,0:T(1,128)}), f32[8,1,616]{2,1,0:T(1,128)S(1)}, u32[]{:S(2)}, u32[]{:S(2)}) async-start(f32[8,1,616]{2,1,0:T(1,128)} %broadcast_in_dim.35), calls=%async_computation.3 | async-start | bytes 40960 | tf_op jit(solution)/shard_map/all_to_all | solution.py:37
  163.4 15.4 %all-gather.5 = f16[64,24,512]{2,1,0:T(8,128)(2,1)S(1)} all-gather(f16[8,24,512]{2,1,0:T(8,128)(2,1)S(1)} %get-tuple-element.57), channel_id=2, replica_groups=mesh['zl'=8,'x'=4,'c'=2,'zh'=2,'y'=4] {'x','c'}, dimensions={0}, use_global_device_ids=true | all-gather | bytes 1769472 | tf_op jit(solution)/shard_map/all_gather | solution.py:103
  180.1 1.2 reshape.221
  181.6 2.5 concatenate.34
  184.2 14.8 %all-gather.4 = f16[64,24,512]{2,1,0:T(8,128)(2,1)S(1)} all-gather(f16[8,24,512]{2,1,0:T(8,128)(2,1)S(1)} %get-tuple-element.38), channel_id=3, replica_groups=mesh['zl'=8,'x'=4,'c'=2,'zh'=2,'y'=4] {'x','c'}, dimensions={0}, use_global_device_ids=true | all-gather | bytes 1769472 | tf_op jit(solution)/shard_map/all_gather | solution.py:109
  199.1 1.6 multiply_reduce_fusion
  200.7 1.8 fusion.60
  203.1 4.5 %all-to-all-start.4 = ((f32[4,8,1280]{2,1,0:T(8,128)}), f32[4,8,1280]{2,1,0:T(8,128)}, u32[]{:S(2)}, u32[]{:S(2)}) async-start(f32[4,8,1280]{2,1,0:T(8,128)} %broadcast_in_dim.36), calls=%async_computation.4 | async-start | bytes 327680 | tf_op jit(solution)/shard_map/all_to_all | solution.py:37
  207.7 1.3 fusion.79
  209.0 3.8 %all-to-all-done.4 = f32[4,8,1280]{2,1,0:T(8,128)} async-done(((f32[4,8,1280]{2,1,0:T(8,128)}), f32[4,8,1280]{2,1,0:T(8,128)}, u32[]{:S(2)}, u32[]{:S(2)}) %all-to-all-start.4) | async-done | bytes 163872 | tf_op jit(solution)/shard_map/all_to_all | solution.py:37
  213.7 11.9 %collective-permute-start.12 = (f32[8,1280]{1,0:T(8,128)S(1)}, f32[8,1280]{1,0:T(8,128)S(1)}, u32[]{:S(2)}, u32[]{:S(2)}) collective-permute-start(f32[8,1280]{1,0:T(8,128)S(1)} %reduce_sum.94), channel_id=1, source_target_pairs={{0,4},{4,0},{1,5},{5,1},{2,6},{6,2},{3,7},{7,3},{8,12},{12,8},{9,1... | collective-permute-start | bytes 122888 | tf_op jit(solution)/shard_map/ppermute | solution.py:14
  228.8 9.3 %all-to-all-start.5 = ((f16[8,8,1408]{2,1,0:T(8,128)(2,1)}), f16[8,8,1408]{2,1,0:T(8,128)(2,1)}, u32[]{:S(2)}, u32[]{:S(2)}) async-start(f16[8,8,1408]{2,1,0:T(8,128)(2,1)} %broadcast_in_dim.37), calls=%async_computation.5 | async-start | bytes 360448 | tf_op jit(solution)/shard_map/all_to_all | solution.py:37
  238.5 1.3 bitcast_convert_fusion.3
  239.8 9.2 %all-to-all-done.5 = f16[8,8,1408]{2,1,0:T(8,128)(2,1)} async-done(((f16[8,8,1408]{2,1,0:T(8,128)(2,1)}), f16[8,8,1408]{2,1,0:T(8,128)(2,1)}, u32[]{:S(2)}, u32[]{:S(2)}) %all-to-all-start.5) | async-done | bytes 180256 | tf_op jit(solution)/shard_map/all_to_all | solution.py:37
  249.1 3.8 %fusion.24 = f32[8,512]{1,0:T(8,128)S(1)} fusion(f32[8,1280]{1,0:T(8,128)S(1)} %get-tuple-element.37, s32[8]{0:T(128)S(1)} %iota_add_fusion.1, f32[]{:T(128)} %bitcast.63, f32[]{:T(128)} %bitcast.12, f32[512,256]{1,0:T(8,128)} %slice.93, f32[512,512]{1,0:T(8,128)S(1)} %bitcast_convert_fusion.2, f32[512,512]{1,0:T(8,128)} %bitcast_convert_fusion.3, ...), kind=kOutput, calls=%fused_computation.38 | convolution fusion | flops 64913408 | bytes 2680872 | tf_op jit(solution)/shard_map/dot_general | solution.py:139
  252.9 1.6 multiply_reduce_fusion.3
  254.5 1.9 broadcast_in_dim.38
  256.3 4.5 %all-to-all-start.6 = ((f16[4,8,8,1408]{3,2,1,0:T(8,128)(2,1)}), f16[4,8,8,1408]{3,2,1,0:T(8,128)(2,1)}, u32[]{:S(2)}, u32[]{:S(2)}) async-start(f16[4,8,8,1408]{3,2,1,0:T(8,128)(2,1)} %broadcast_in_dim.38), calls=%async_computation.6 | async-start | bytes 1441792 | tf_op jit(solution)/shard_map/all_to_all | solution.py:37
  261.9 7.1 %all-to-all-done.6 = f16[4,8,8,1408]{3,2,1,0:T(8,128)(2,1)} async-done(((f16[4,8,8,1408]{3,2,1,0:T(8,128)(2,1)}), f16[4,8,8,1408]{3,2,1,0:T(8,128)(2,1)}, u32[]{:S(2)}, u32[]{:S(2)}) %all-to-all-start.6) | async-done | bytes 720928 | tf_op jit(solution)/shard_map/all_to_all | solution.py:37
  270.2 7.4 %collective-permute-start.13 = (f16[4,8,8,1408]{3,2,1,0:T(8,128)(2,1)}, f16[4,8,8,1408]{3,2,1,0:T(8,128)(2,1)S(1)}, u32[]{:S(2)}, u32[]{:S(2)}) collective-permute-start(f16[4,8,8,1408]{3,2,1,0:T(8,128)(2,1)} %all-to-all-done.6), channel_id=1, source_target_pairs={{0,8},{8,0},{1,9},{9,1},{2,10},{10,2},{3,11},{11,3},{4,12},{12,4},... | collective-permute-start | bytes 2162696 | tf_op jit(solution)/shard_map/ppermute | solution.py:14
  279.8 2.4 fusion.43
  282.4 1.9 collective-permute-start.14
  (135 shorter events, 28.4 us)
Async XLA Ops:
  0.6 14.8 %copy-start = (bf16[616,512]{1,0:T(8,128)(2,1)S(1)}, bf16[616,512]{1,0:T(8,128)(2,1)}, u32[]{:S(2)}) copy-start(bf16[616,512]{1,0:T(8,128)(2,1)} %param.9) | copy-start | bytes 1892356
  2.4 47.4 %all-to-all-start = ((bf16[8,64,512]{2,1,0:T(8,128)(2,1)}), bf16[8,64,512]{2,1,0:T(8,128)(2,1)S(1)}, u32[]{:S(2)}, u32[]{:S(2)}) async-start(bf16[8,64,512]{2,1,0:T(8,128)(2,1)} %broadcast_in_dim.26), calls=%async_computation | async-start | bytes 1048576 | tf_op jit(solution)/shard_map/all_to_all | solution.py:37
  15.5 28.6 %collective-permute-start.1 = (bf16[616,512]{1,0:T(8,128)(2,1)S(1)}, bf16[616,512]{1,0:T(8,128)(2,1)S(1)}, u32[]{:S(2)}, u32[]{:S(2)}) collective-permute-start(bf16[616,512]{1,0:T(8,128)(2,1)S(1)} %copy-done), channel_id=1, source_target_pairs={{0,1},{1,2},{2,3},{3,0},{4,5},{5,6},{6,7},{7,4},{8,9},{9,10},{10,1... | collective-permute-start | bytes 1892360 | tf_op jit(solution)/shard_map/ppermute | solution.py:19
  18.7 29.4 %collective-permute-start.2 = (bf16[616,512]{1,0:T(8,128)(2,1)S(1)}, bf16[616,512]{1,0:T(8,128)(2,1)S(1)}, u32[]{:S(2)}, u32[]{:S(2)}) collective-permute-start(bf16[616,512]{1,0:T(8,128)(2,1)S(1)} %copy-done), channel_id=1, source_target_pairs={{0,2},{1,3},{2,0},{3,1},{4,6},{5,7},{6,4},{7,5},{8,10},{9,11},{10,... | collective-permute-start | bytes 1892360 | tf_op jit(solution)/shard_map/ppermute | solution.py:19
  23.2 26.5 %collective-permute-start.3 = (bf16[616,512]{1,0:T(8,128)(2,1)S(1)}, bf16[616,512]{1,0:T(8,128)(2,1)S(1)}, u32[]{:S(2)}, u32[]{:S(2)}) collective-permute-start(bf16[616,512]{1,0:T(8,128)(2,1)S(1)} %copy-done), channel_id=1, source_target_pairs={{0,3},{1,0},{2,1},{3,2},{4,7},{5,4},{6,5},{7,6},{8,11},{9,8},{10,9... | collective-permute-start | bytes 1892360 | tf_op jit(solution)/shard_map/ppermute | solution.py:19
  26.2 17.8 %collective-permute-start = (bf16[304,512]{1,0:T(8,128)(2,1)S(1)}, bf16[304,512]{1,0:T(8,128)(2,1)S(1)}, u32[]{:S(2)}, u32[]{:S(2)}) collective-permute-start(bf16[304,512]{1,0:T(8,128)(2,1)S(1)} %slice.63), channel_id=1, source_target_pairs={{0,4},{4,0},{1,5},{5,1},{2,6},{6,2},{3,7},{7,3},{8,12},{12,8},{9,1... | collective-permute-start | bytes 933896 | tf_op jit(solution)/shard_map/ppermute | solution.py:14
  44.1 4.0 %copy-start.17 = (bf16[304,512]{1,0:T(8,128)(2,1)}, bf16[304,512]{1,0:T(8,128)(2,1)S(1)}, u32[]{:S(2)}) copy-start(bf16[304,512]{1,0:T(8,128)(2,1)S(1)} %collective-permute-done) | copy-start | bytes 933892
  48.1 3.3 %copy-start.11 = (bf16[616,512]{1,0:T(8,128)(2,1)}, bf16[616,512]{1,0:T(8,128)(2,1)S(1)}, u32[]{:S(2)}) copy-start(bf16[616,512]{1,0:T(8,128)(2,1)S(1)} %collective-permute-done.2) | copy-start | bytes 1892356
  49.8 1.6 copy-start.13
  51.3 13.0 %copy-start.19 = (bf16[512,20]{0,1:T(8,128)(2,1)S(1)}, bf16[512,20]{0,1:T(8,128)(2,1)}, u32[]{:S(2)}) copy-start(bf16[512,20]{0,1:T(8,128)(2,1)} %param.14) | copy-start | bytes 61444
  51.3 14.3 %copy-start.4 = (f32[8,1280]{1,0:T(8,128)S(1)}, f32[8,1280]{1,0:T(8,128)}, u32[]{:S(2)}) copy-start(f32[8,1280]{1,0:T(8,128)} %param.15) | copy-start | bytes 122884
  51.4 32.3 %all-to-all-start.1 = ((bf16[4,8,64,512]{3,2,1,0:T(8,128)(2,1)}), bf16[4,8,64,512]{3,2,1,0:T(8,128)(2,1)S(1)}, u32[]{:S(2)}, u32[]{:S(2)}) async-start(bf16[4,8,64,512]{3,2,1,0:T(8,128)(2,1)} %broadcast_in_dim.27), calls=%async_computation.1 | async-start | bytes 4194304 | tf_op jit(solution)/shard_map/all_to_all | solution.py:37
  56.3 27.3 %collective-permute-start.7 = (bf16[312,512]{1,0:T(8,128)(2,1)}, bf16[312,512]{1,0:T(8,128)(2,1)}, u32[]{:S(2)}, u32[]{:S(2)}) collective-permute-start(bf16[312,512]{1,0:T(8,128)(2,1)} %slice.64), channel_id=1, source_target_pairs={{0,4},{4,0},{1,5},{5,1},{2,6},{6,2},{3,7},{7,3},{8,12},{12,8},{9,1... | collective-permute-start | bytes 958472 | tf_op jit(solution)/shard_map/ppermute | solution.py:14
  66.0 14.0 %collective-permute-start.4 = (bf16[304,512]{1,0:T(8,128)(2,1)}, bf16[304,512]{1,0:T(8,128)(2,1)S(1)}, u32[]{:S(2)}, u32[]{:S(2)}) collective-permute-start(bf16[304,512]{1,0:T(8,128)(2,1)} %copy-done.17), channel_id=1, source_target_pairs={{0,1},{1,2},{2,3},{3,0},{4,5},{5,6},{6,7},{7,4},{8,9},{9,10},{10,1... | collective-permute-start | bytes 933896 | tf_op jit(solution)/shard_map/ppermute | solution.py:19
  71.2 9.4 %collective-permute-start.5 = (bf16[304,512]{1,0:T(8,128)(2,1)}, bf16[304,512]{1,0:T(8,128)(2,1)S(1)}, u32[]{:S(2)}, u32[]{:S(2)}) collective-permute-start(bf16[304,512]{1,0:T(8,128)(2,1)} %copy-done.17), channel_id=1, source_target_pairs={{0,2},{1,3},{2,0},{3,1},{4,6},{5,7},{6,4},{7,5},{8,10},{9,11},{10,... | collective-permute-start | bytes 933896 | tf_op jit(solution)/shard_map/ppermute | solution.py:19
  74.4 8.1 %collective-permute-start.6 = (bf16[304,512]{1,0:T(8,128)(2,1)}, bf16[304,512]{1,0:T(8,128)(2,1)S(1)}, u32[]{:S(2)}, u32[]{:S(2)}) collective-permute-start(bf16[304,512]{1,0:T(8,128)(2,1)} %copy-done.17), channel_id=1, source_target_pairs={{0,3},{1,0},{2,1},{3,2},{4,7},{5,4},{6,5},{7,6},{8,11},{9,8},{10,9... | collective-permute-start | bytes 933896 | tf_op jit(solution)/shard_map/ppermute | solution.py:19
  77.7 1.1 copy-start.12
  77.8 1.2 copy-start.14
  79.0 1.0 copy-start.18
  79.1 1.5 copy-start.1
  82.6 1.0 copy-start.5
  85.2 35.6 %copy-start.21 = (s32[8]{0:T(128)S(1)}, s32[8]{0:T(128)}, u32[]{:S(2)}) copy-start(s32[8]{0:T(128)} %param.13) | copy-start | bytes 100
  85.2 58.6 %collective-permute-start.8 = (bf16[4,8,64,512]{3,2,0,1:T(8,128)(2,1)}, bf16[4,8,64,512]{3,2,0,1:T(8,128)(2,1)}, u32[]{:S(2)}, u32[]{:S(2)}) collective-permute-start(bf16[4,8,64,512]{3,2,0,1:T(8,128)(2,1)} %copy.30), channel_id=1, source_target_pairs={{0,8},{8,0},{1,9},{9,1},{2,10},{10,2},{3,11},{11,3},{4,12},{12,4},... | collective-permute-start | bytes 6291464 | tf_op jit(solution)/shard_map/ppermute | solution.py:14
  116.8 35.0 %all-to-all-start.2 = ((f16[8,48,512]{2,1,0:T(8,128)(2,1)}), f16[8,48,512]{2,1,0:T(8,128)(2,1)S(1)}, u32[]{:S(2)}, u32[]{:S(2)}) async-start(f16[8,48,512]{2,1,0:T(8,128)(2,1)} %broadcast_in_dim.34), calls=%async_computation.2 | async-start | bytes 786432 | tf_op jit(solution)/shard_map/all_to_all | solution.py:37
  122.3 12.4 %collective-permute-start.9 = (bf16[312,512]{1,0:T(8,128)(2,1)}, bf16[312,512]{1,0:T(8,128)(2,1)S(1)}, u32[]{:S(2)}, u32[]{:S(2)}) collective-permute-start(bf16[312,512]{1,0:T(8,128)(2,1)} %collective-permute-done.7), channel_id=1, source_target_pairs={{0,1},{1,2},{2,3},{3,0},{4,5},{5,6},{6,7},{7,4},{8,9},{9,10},{10,1... | collective-permute-start | bytes 958472 | tf_op jit(solution)/shard_map/ppermute | solution.py:19
  126.7 15.9 %collective-permute-start.10 = (bf16[312,512]{1,0:T(8,128)(2,1)}, bf16[312,512]{1,0:T(8,128)(2,1)S(1)}, u32[]{:S(2)}, u32[]{:S(2)}) collective-permute-start(bf16[312,512]{1,0:T(8,128)(2,1)} %collective-permute-done.7), channel_id=1, source_target_pairs={{0,2},{1,3},{2,0},{3,1},{4,6},{5,7},{6,4},{7,5},{8,10},{9,11},{10,... | collective-permute-start | bytes 958472 | tf_op jit(solution)/shard_map/ppermute | solution.py:19
  130.1 13.7 %collective-permute-start.11 = (bf16[312,512]{1,0:T(8,128)(2,1)}, bf16[312,512]{1,0:T(8,128)(2,1)S(1)}, u32[]{:S(2)}, u32[]{:S(2)}) collective-permute-start(bf16[312,512]{1,0:T(8,128)(2,1)} %collective-permute-done.7), channel_id=1, source_target_pairs={{0,3},{1,0},{2,1},{3,2},{4,7},{5,4},{6,5},{7,6},{8,11},{9,8},{10,9... | collective-permute-start | bytes 958472 | tf_op jit(solution)/shard_map/ppermute | solution.py:19
  145.7 1.7 copy-start.2
  145.7 1.8 copy-start.22
  147.6 1.5 copy-start.6
  152.6 31.6 %all-to-all-start.3 = ((f32[8,1,616]{2,1,0:T(1,128)}), f32[8,1,616]{2,1,0:T(1,128)S(1)}, u32[]{:S(2)}, u32[]{:S(2)}) async-start(f32[8,1,616]{2,1,0:T(1,128)} %broadcast_in_dim.35), calls=%async_computation.3 | async-start | bytes 40960 | tf_op jit(solution)/shard_map/all_to_all | solution.py:37
  184.2 14.9 %copy-start.20 = (f32[512]{0:T(512)S(1)}, f32[512]{0:T(512)}, u32[]{:S(2)}) copy-start(f32[512]{0:T(512)} %param.12) | copy-start | bytes 6148
  203.1 9.7 %all-to-all-start.4 = ((f32[4,8,1280]{2,1,0:T(8,128)}), f32[4,8,1280]{2,1,0:T(8,128)}, u32[]{:S(2)}, u32[]{:S(2)}) async-start(f32[4,8,1280]{2,1,0:T(8,128)} %broadcast_in_dim.36), calls=%async_computation.4 | async-start | bytes 327680 | tf_op jit(solution)/shard_map/all_to_all | solution.py:37
  213.7 13.9 %collective-permute-start.12 = (f32[8,1280]{1,0:T(8,128)S(1)}, f32[8,1280]{1,0:T(8,128)S(1)}, u32[]{:S(2)}, u32[]{:S(2)}) collective-permute-start(f32[8,1280]{1,0:T(8,128)S(1)} %reduce_sum.94), channel_id=1, source_target_pairs={{0,4},{4,0},{1,5},{5,1},{2,6},{6,2},{3,7},{7,3},{8,12},{12,8},{9,1... | collective-permute-start | bytes 122888 | tf_op jit(solution)/shard_map/ppermute | solution.py:14
  226.8 11.5 %copy-start.3 = (f16[8,8,8,512]{3,2,1,0:T(8,128)(2,1)S(1)}, f16[8,8,8,512]{3,2,1,0:T(8,128)(2,1)}, u32[]{:S(2)}) copy-start(f16[8,8,8,512]{3,2,1,0:T(8,128)(2,1)} %get-tuple-element.53) | copy-start | bytes 1572868
  228.8 20.2 %all-to-all-start.5 = ((f16[8,8,1408]{2,1,0:T(8,128)(2,1)}), f16[8,8,1408]{2,1,0:T(8,128)(2,1)}, u32[]{:S(2)}, u32[]{:S(2)}) async-start(f16[8,8,1408]{2,1,0:T(8,128)(2,1)} %broadcast_in_dim.37), calls=%async_computation.5 | async-start | bytes 360448 | tf_op jit(solution)/shard_map/all_to_all | solution.py:37
  238.5 14.4 %copy-start.7 = (f32[512,512]{1,0:T(8,128)}, f32[512,512]{1,0:T(8,128)S(1)}, u32[]{:S(2)}) copy-start(f32[512,512]{1,0:T(8,128)S(1)} %bitcast_convert_fusion.2) | copy-start | bytes 3145732
  249.1 3.8 %copy-start.9 = (f32[512,512]{1,0:T(8,128)S(1)}, f32[512,512]{1,0:T(8,128)}, u32[]{:S(2)}) copy-start(f32[512,512]{1,0:T(8,128)} %bitcast_convert_fusion.3) | copy-start | bytes 3145732
  249.1 3.8 %copy-start.15 = (f32[512,256]{1,0:T(8,128)S(1)}, f32[512,256]{1,0:T(8,128)}, u32[]{:S(2)}) copy-start(f32[512,256]{1,0:T(8,128)} %slice.93) | copy-start | bytes 1572868
  256.3 12.6 %all-to-all-start.6 = ((f16[4,8,8,1408]{3,2,1,0:T(8,128)(2,1)}), f16[4,8,8,1408]{3,2,1,0:T(8,128)(2,1)}, u32[]{:S(2)}, u32[]{:S(2)}) async-start(f16[4,8,8,1408]{3,2,1,0:T(8,128)(2,1)} %broadcast_in_dim.38), calls=%async_computation.6 | async-start | bytes 1441792 | tf_op jit(solution)/shard_map/all_to_all | solution.py:37
  270.1 9.6 %copy-start.8 = (f32[512,512]{1,0:T(8,128)S(1)}, f32[512,512]{1,0:T(8,128)}, u32[]{:S(2)}) copy-start(f32[512,512]{1,0:T(8,128)} %copy-done.7) | copy-start | bytes 3145732
  270.2 9.6 %copy-start.10 = (f32[512,512]{1,0:T(8,128)S(1)}, f32[512,512]{1,0:T(8,128)}, u32[]{:S(2)}) copy-start(f32[512,512]{1,0:T(8,128)} %bitcast_convert_fusion.3) | copy-start | bytes 3145732
  270.2 9.6 %copy-start.16 = (f32[512,256]{1,0:T(8,128)S(1)}, f32[512,256]{1,0:T(8,128)}, u32[]{:S(2)}) copy-start(f32[512,256]{1,0:T(8,128)} %slice.93) | copy-start | bytes 1572868
  270.2 12.0 %collective-permute-start.13 = (f16[4,8,8,1408]{3,2,1,0:T(8,128)(2,1)}, f16[4,8,8,1408]{3,2,1,0:T(8,128)(2,1)S(1)}, u32[]{:S(2)}, u32[]{:S(2)}) collective-permute-start(f16[4,8,8,1408]{3,2,1,0:T(8,128)(2,1)} %all-to-all-done.6), channel_id=1, source_target_pairs={{0,8},{8,0},{1,9},{9,1},{2,10},{10,2},{3,11},{11,3},{4,12},{12,4},... | collective-permute-start | bytes 2162696 | tf_op jit(solution)/shard_map/ppermute | solution.py:14
  282.4 4.8 %collective-permute-start.14 = (f32[]{:T(128)}, f32[]{:T(128)}, u32[]{:S(2)}, u32[]{:S(2)}) collective-permute-start(f32[]{:T(128)} %fusion.43), channel_id=1, source_target_pairs={{0,8},{8,0},{1,9},{9,1},{2,10},{10,2},{3,11},{11,3},{4,12},{12,4},... | collective-permute-start | bytes 20 | tf_op jit(solution)/shard_map/ppermute | solution.py:14
